TPU v7x, 32 devices: a whole 2x2x4 slice. The times are simulated.
32 devices in a mesh: clus: 8 (over z, x), col: 4 (over y, core).
Axes of the slice: x: 2, y: 2, z: 4, core: 2. Of those that a mesh axis runs over, the one named last changes fastest.
Arguments:
- features: bfloat16 [3, 12288, 2048], P(None, 'clus', 'col'), may hold values from -12 to 12
- neighbours: int32 [3, 12288, 16], P(None, 'clus'), may hold values from 0 to 1535
- node_counts: int32 [3, 8], P(None, 'clus'), may hold values from 768 to 1536, as said below
- row_counts: int32 [8], replicated, may hold values from 1 to 512, 2048 in all
- master_weight: float32 [4096, 2048], P('clus', 'col'), may hold values from -0.125 to 0.125
- weight_first: float32 [4096, 2048], P('clus', 'col'), may hold values from -40 to 40
- weight_second: float32 [4096, 2048], P('clus', 'col'), may hold values from 184.32 to 737.28
- master_bias: float32 [2048], P('col'), may hold values from -1.75 to 1.75
- bias_first: float32 [2048], P('col'), may hold values from -64 to 64
- bias_second: float32 [2048], P('col'), may hold values from 442.368 to 1843.2
- out_grad: bfloat16 [3, 12288, 2048], P(None, 'clus', 'col'), may hold values from -6 to 6
Outputs:
- layer_out: bfloat16 [3, 12288, 2048], P(None, 'clus', 'col')
- feature_grad: bfloat16 [3, 12288, 2048], P(None, 'clus', 'col')
- weight_new: float32 [4096, 2048], P('clus', 'col')
- weight_first_new: float32 [4096, 2048], P('clus', 'col')
- weight_second_new: float32 [4096, 2048], P('clus', 'col')
- bias_new: float32 [2048], P('col')
- bias_first_new: float32 [2048], P('col')
- bias_second_new: float32 [2048], P('col')
Inputs may be any that keep to these rules, and one draw needn't show every extreme that they name: `node_counts`: in every micro-batch some cluster has all 1536 slots live. `row_counts`: some owner holds exactly 512 rows.
All inputs are finite; a program needn't handle non-finite values.
Results may differ from a plain program's by a relative error of at most 0.0071.
Values may be sent and summed in bfloat16 or wider, within the bound.
A program may use at most 256 MiB of HBM per device.

v0:
```python
import math

import jax
import jax.numpy as jnp
from jax import lax
from jax.sharding import PartitionSpec as P

D = 2048
MB = 3
STEP = 10


BETA_ONE = 0.9
BETA_TWO = 0.95
EPSILON = 1e-08
DECAY = 0.1
RATE_WEIGHT = 0.06
RATE_BIAS = 0.6
LAMBDA_DIAG = 1.0


def build_counts(neighbour_rows, live_rows):
    nodes = neighbour_rows.shape[0]
    block_rows = math.gcd(nodes, 256)
    columns = jnp.arange(nodes, dtype=jnp.int32)
    grouped = neighbour_rows.reshape(nodes // block_rows, block_rows, neighbour_rows.shape[1])

    def count_block(row_block):
        return jnp.sum(
            (row_block[:, :, None] == columns[None, None, :]).astype(jnp.float32), axis=1
        )

    counted = lax.map(count_block, grouped).reshape(nodes, nodes)
    return counted * live_rows[:, None] * live_rows[None, :]


def owner_table(owners, groups):
    return (owners[:, None] == jnp.arange(groups, dtype=jnp.int32)[None, :]).astype(jnp.int32)


def row_owners(starts):
    row_ids = jnp.arange(D, dtype=jnp.int32)
    return jnp.sum((starts[None, :] <= row_ids[:, None]).astype(jnp.int32), axis=1) - 1


def place_rows(starts, groups, capacity):
    row_ids = jnp.arange(D, dtype=jnp.int32)
    owners = row_owners(starts)
    start_of = jnp.sum(owner_table(owners, groups) * starts[None, :], axis=1)
    return owners * capacity + row_ids - start_of


def slot_sources(starts, row_counts, groups, capacity):
    slot_ids = jnp.arange(groups * capacity, dtype=jnp.int32)
    owners = slot_ids // capacity
    offsets = slot_ids % capacity
    table = owner_table(owners, groups)
    start_of = jnp.sum(table * starts[None, :], axis=1)
    count_of = jnp.sum(table * row_counts[None, :], axis=1)
    row_ids = jnp.clip(start_of + offsets, 0, D - 1)
    return (row_ids, (offsets < count_of).astype(jnp.float32))


def fetch_weight(master_weight, row_place):
    gathered = lax.all_gather(master_weight.astype(jnp.bfloat16), "clus", axis=0, tiled=True)
    return jnp.take(gathered, row_place, axis=0)


def adamw_update(current, first_moment, second_moment, gradient, step_rate):
    first_new = BETA_ONE * first_moment + (1.0 - BETA_ONE) * gradient
    second_new = BETA_TWO * second_moment + (1.0 - BETA_TWO) * gradient * gradient
    fixed_first = first_new / (1.0 - BETA_ONE**STEP)
    fixed_second = second_new / (1.0 - BETA_TWO**STEP)
    updated = current - step_rate * (
        fixed_first / (jnp.sqrt(fixed_second) + EPSILON) + DECAY * current
    )
    return (updated, first_new, second_new)


def shards(
    features,
    neighbours,
    node_counts,
    row_counts,
    master_weight,
    weight_first,
    weight_second,
    master_bias,
    bias_first,
    bias_second,
    out_grad,
):
    groups = lax.axis_size("clus")
    capacity = master_weight.shape[0]
    width = master_weight.shape[1]
    own_index = lax.axis_index("clus")
    starts = jnp.cumsum(row_counts) - row_counts
    row_place = place_rows(starts, groups, capacity)
    nodes = features.shape[1]
    positions = jnp.arange(nodes, dtype=jnp.int32)
    grad_weight = jnp.zeros((D, width), jnp.float32)
    grad_bias = jnp.zeros((width,), jnp.float32)
    outputs = []
    input_grads = []
    for micro_batch in range(MB):
        live_rows = (positions < node_counts[micro_batch, 0]).astype(jnp.float32)
        counted = build_counts(neighbours[micro_batch], live_rows)
        degree = 1.0 + jnp.sum(counted, axis=1)
        self_term = 1.0 + LAMBDA_DIAG * (1.0 + jnp.diagonal(counted))
        row_scale = live_rows / degree
        adjacency = counted.astype(jnp.bfloat16)
        feature_shard = features[micro_batch]
        summed = jnp.dot(adjacency, feature_shard, preferred_element_type=jnp.float32)
        hidden_low = (
            (summed + self_term[:, None] * feature_shard.astype(jnp.float32)) * row_scale[:, None]
        ).astype(jnp.bfloat16)
        hidden_full = lax.all_gather(hidden_low, "col", axis=1, tiled=True)
        weight_fwd = fetch_weight(master_weight, row_place)
        preact = jnp.dot(hidden_full, weight_fwd, preferred_element_type=jnp.float32) + master_bias
        gate_value = jax.nn.sigmoid(preact)
        outputs.append((preact * gate_value * live_rows[:, None]).astype(jnp.bfloat16))
        slope_value = gate_value * (1.0 + preact * (1.0 - gate_value))
        grad_pre = (
            out_grad[micro_batch].astype(jnp.float32) * live_rows[:, None] * slope_value
        ).astype(jnp.bfloat16)
        weight_back = fetch_weight(master_weight, row_place)
        partial_hidden = lax.dot_general(
            grad_pre, weight_back, (((1,), (1,)), ((), ())), preferred_element_type=jnp.float32
        )
        grad_hidden = lax.psum_scatter(partial_hidden, "col", scatter_dimension=1, tiled=True)
        hidden_rounded = lax.optimization_barrier(grad_hidden.astype(jnp.bfloat16)).astype(
            jnp.float32
        )
        grad_mixed = hidden_rounded * row_scale[:, None]
        grad_shard = lax.dot_general(
            adjacency,
            grad_mixed.astype(jnp.bfloat16),
            (((0,), (0,)), ((), ())),
            preferred_element_type=jnp.float32,
        )
        grad_shard = grad_shard + self_term[:, None] * grad_mixed
        input_grads.append(grad_shard.astype(jnp.bfloat16))
        grad_weight = grad_weight + lax.dot_general(
            hidden_full, grad_pre, (((0,), (0,)), ((), ())), preferred_element_type=jnp.float32
        )
        grad_bias = grad_bias + jnp.sum(grad_pre.astype(jnp.float32), axis=0)
    own_count = jnp.sum(jnp.where(jnp.arange(groups, dtype=jnp.int32) == own_index, row_counts, 0))
    slot_offsets = jnp.arange(capacity, dtype=jnp.int32)
    slot_mask = (slot_offsets < own_count).astype(jnp.float32)[:, None]
    row_ids, live_sources = slot_sources(starts, row_counts, groups, capacity)
    outgoing = (jnp.take(grad_weight, row_ids, axis=0) * live_sources[:, None]).reshape(
        groups, capacity, width
    )
    bias_out = jnp.broadcast_to(grad_bias[None, None, :], (groups, 1, width))
    incoming, bias_in = (
        lax.all_to_all(outgoing, "clus", split_axis=0, concat_axis=0, tiled=True),
        lax.all_to_all(bias_out, "clus", split_axis=0, concat_axis=0, tiled=True),
    )
    grad_slots = jnp.sum(incoming, axis=0)
    grad_bias_all = jnp.sum(bias_in, axis=(0, 1))
    weight_new, first_new, second_new = adamw_update(
        master_weight, weight_first, weight_second, grad_slots, RATE_WEIGHT
    )
    bias_new, bias_first_new, bias_second_new = adamw_update(
        master_bias, bias_first, bias_second, grad_bias_all, RATE_BIAS
    )
    return (
        jnp.stack(outputs),
        jnp.stack(input_grads),
        weight_new * slot_mask,
        first_new * slot_mask,
        second_new * slot_mask,
        bias_new,
        bias_first_new,
        bias_second_new,
    )


def solution(mesh):
    in_specs = (
        P(None, "clus", "col"),
        P(None, "clus", None),
        P(None, "clus"),
        P(),
        P("clus", "col"),
        P("clus", "col"),
        P("clus", "col"),
        P("col"),
        P("col"),
        P("col"),
        P(None, "clus", "col"),
    )
    out_specs = (
        P(None, "clus", "col"),
        P(None, "clus", "col"),
        P("clus", "col"),
        P("clus", "col"),
        P("clus", "col"),
        P("col"),
        P("col"),
        P("col"),
    )
    return jax.shard_map(shards, mesh=mesh, in_specs=in_specs, out_specs=out_specs, check_vma=False)
```

profile of v0, /device:TPU:0, one launch (start us, length us, event | category | flops | bytes accessed | tf_op | source)
XLA Modules:
  0.0 716.7 jit_solution(14715837656211305280)
XLA Ops:
  13.1 4.8 broadcast.313.clone.1
  17.9 47.0 %while.34 = (s32[]{:T(128)}, f32[6,256,1536]{2,1,0:T(8,128)}, s32[6,256,16]{1,0,2:T(8,128)S(1)}, s32[]{:T(128)}) while((s32[]{:T(128)}, f32[6,256,1536]{2,1,0:T(8,128)}, s32[6,256,16]{1,0,2:T(8,128)S(1)}, s32[]{:T(128)}) %tuple.94), condition=%wide.region_9.11_spmd.clone, body=%wide.region_7.10_spmd.clone.sunk | while | flops 18481152 | bytes 4801081 | solution.py:33
  18.0 6.4 convert_reduce_fusion.11
  25.9 6.4 convert_reduce_fusion.11
  33.7 6.4 convert_reduce_fusion.11
  41.5 6.4 convert_reduce_fusion.11
  49.4 6.4 convert_reduce_fusion.11
  57.2 6.4 convert_reduce_fusion.11
  65.0 7.1 fusion.11
  72.3 8.3 %fusion.7 = f32[1536,1536]{1,0:T(8,128)} fusion(f32[6,256,1536]{2,1,0:T(8,128)} %get-tuple-element.76, f32[1536]{0:T(1024)S(1)} %fusion.95), kind=kLoop, calls=%fused_computation.23 | loop fusion | flops 4718592 | bytes 18880512 | tf_op jit(solution)/shard_map/mul | solution.py:34
  80.6 25.7 %gather_fusion.1 = f32[1536]{0:T(1024)S(1)} fusion(f32[1536,1536]{1,0:T(8,128)} %fusion.7, s32[1536]{0:T(1024)S(1)} %or_reduce_fusion), kind=kCustom, calls=%fused_computation.2 | custom fusion | bytes 24576 | tf_op jit(solution)/shard_map/jit(diagonal)/cond/branch_0_fun/gather | solution.py:109
  107.0 7.2 %fusion.43 = bf16[1536,512]{1,0:T(8,128)(2,1)} fusion(bf16[1536,1536]{1,0:T(8,128)(2,1)} %bitcast.108, f32[1536]{0:T(1024)S(1)} %fusion.98, f32[1536]{0:T(1024)S(1)} %broadcast_add_fusion.5, bf16[3,1536,512]{2,1,0:T(8,128)(2,1)} %param.19), kind=kOutput, calls=%fused_computation.82 | convolution fusion | flops 2419851264 | bytes 9449472 | tf_op jit(solution)/shard_map/dot_general | solution.py:113
  115.6 4.8 broadcast.313.clone
  120.5 47.1 %while.35 = (s32[]{:T(128)}, f32[6,256,1536]{2,1,0:T(8,128)}, s32[6,256,16]{1,0,2:T(8,128)S(1)}, s32[]{:T(128)}) while((s32[]{:T(128)}, f32[6,256,1536]{2,1,0:T(8,128)}, s32[6,256,16]{1,0,2:T(8,128)S(1)}, s32[]{:T(128)}) %tuple.91), condition=%wide.region_13.15_spmd.clone, body=%wide.region_11.14_spmd.clone.sunk | while | flops 18481152 | bytes 4801081 | solution.py:33
  120.6 6.4 convert_reduce_fusion.12
  128.4 6.4 convert_reduce_fusion.12
  136.2 6.4 convert_reduce_fusion.12
  144.1 6.4 convert_reduce_fusion.12
  151.9 6.4 convert_reduce_fusion.12
  159.7 6.4 convert_reduce_fusion.12
  167.5 7.1 fusion.13
  174.6 8.1 %fusion.6 = f32[1536,1536]{1,0:T(8,128)} fusion(f32[6,256,1536]{2,1,0:T(8,128)} %get-tuple-element.77, f32[1536]{0:T(1024)S(1)} %fusion.96), kind=kLoop, calls=%fused_computation.21 | loop fusion | flops 4718592 | bytes 18880512 | tf_op jit(solution)/shard_map/mul | solution.py:34
  182.7 25.0 %gather_fusion.2 = f32[1536]{0:T(1024)S(1)} fusion(f32[1536,1536]{1,0:T(8,128)} %fusion.6, s32[1536]{0:T(1024)S(1)} %or_reduce_fusion), kind=kCustom, calls=%fused_computation.3 | custom fusion | bytes 24576 | tf_op jit(solution)/shard_map/jit(diagonal)/cond/branch_0_fun/gather | solution.py:109
  208.4 7.2 %fusion.44 = bf16[1536,512]{1,0:T(8,128)(2,1)} fusion(bf16[1536,1536]{1,0:T(8,128)(2,1)} %bitcast.110, f32[1536]{0:T(1024)S(1)} %fusion.97, f32[1536]{0:T(1024)S(1)} %broadcast_add_fusion.4, bf16[3,1536,512]{2,1,0:T(8,128)(2,1)} %param.19), kind=kOutput, calls=%fused_computation.83 | convolution fusion | flops 2419851264 | bytes 9449472 | tf_op jit(solution)/shard_map/dot_general | solution.py:113
  215.6 9.0 %all-gather.5.cloned.1.call-start = ((), (), s32[]{:S(2)}) async-start(), calls=%async_computation.5 | async-start | bytes 7864320 | tf_op jit(solution)/shard_map/all_gather | solution.py:117
  226.0 5.3 broadcast.313.clone.2
  231.2 47.1 %while.33 = (s32[]{:T(128)}, f32[6,256,1536]{2,1,0:T(8,128)}, s32[6,256,16]{1,0,2:T(8,128)S(1)}, s32[]{:T(128)}) while((s32[]{:T(128)}, f32[6,256,1536]{2,1,0:T(8,128)}, s32[6,256,16]{1,0,2:T(8,128)S(1)}, s32[]{:T(128)}) %tuple.97), condition=%wide.region_2.3_spmd.clone, body=%wide.region_0.2_spmd.clone.sunk | while | flops 18481152 | bytes 4801081 | solution.py:33
  231.4 6.4 convert_reduce_fusion.10
  239.2 6.4 convert_reduce_fusion.10
  247.0 6.4 convert_reduce_fusion.10
  254.9 6.4 convert_reduce_fusion.10
  262.7 6.4 convert_reduce_fusion.10
  270.5 6.4 convert_reduce_fusion.10
  278.3 7.0 fusion.9
  285.4 8.1 %fusion.8 = f32[1536,1536]{1,0:T(8,128)} fusion(f32[6,256,1536]{2,1,0:T(8,128)} %get-tuple-element.75, f32[1536]{0:T(1024)S(1)} %fusion.94), kind=kLoop, calls=%fused_computation.25 | loop fusion | flops 4718592 | bytes 18880512 | tf_op jit(solution)/shard_map/mul | solution.py:34
  293.4 25.3 %gather_fusion = f32[1536]{0:T(1024)S(1)} fusion(f32[1536,1536]{1,0:T(8,128)} %fusion.8, s32[1536]{0:T(1024)S(1)} %or_reduce_fusion), kind=kCustom, calls=%fused_computation.1 | custom fusion | bytes 24576 | tf_op jit(solution)/shard_map/jit(diagonal)/cond/branch_0_fun/gather | solution.py:109
  319.5 7.2 %fusion.42 = bf16[1536,512]{1,0:T(8,128)(2,1)} fusion(bf16[1536,1536]{1,0:T(8,128)(2,1)} %bitcast.109, f32[1536]{0:T(1024)S(1)} %fusion.99, f32[1536]{0:T(1024)S(1)} %broadcast_add_fusion.6, bf16[3,1536,512]{2,1,0:T(8,128)(2,1)} %param.19), kind=kOutput, calls=%fused_computation.81 | convolution fusion | flops 2419851264 | bytes 9449472 | tf_op jit(solution)/shard_map/dot_general | solution.py:113
  328.1 10.3 %gather_fusion.4 = bf16[2048,512]{1,0:T(8,128)(2,1)S(1)} fusion(bf16[4096,512]{1,0:T(8,128)(2,1)} %all-gather.7.cloned.1.call-done, s32[2048]{0:T(1024)S(1)} %broadcast_clamp_fusion.1), kind=kCustom, calls=%fused_computation.clone | custom fusion | bytes 4202496 | tf_op jit(solution)/shard_map/jit(_take)/gather | solution.py:66
  338.4 8.5 %convolution_add_fusion.2 = f32[1536,512]{1,0:T(8,128)} fusion(bf16[1536,2048]{1,0:T(8,128)(2,1)} %all-gather.9.cloned.1.call-done, f32[512]{0:T(512)S(1)} %copy-done.15, bf16[2048,512]{1,0:T(8,128)(2,1)S(1)} %gather_fusion.4, pred[2048]{0:T(1024)(128)(4,1)S(1)} %compare_and_fusion.1), kind=kOutput, calls=%fused_computation.51 | convolution fusion | flops 3223060480 | bytes 11538432 | tf_op jit(solution)/shard_map/dot_general | solution.py:119
  346.9 8.0 %convolution_add_fusion = f32[1536,512]{1,0:T(8,128)} fusion(bf16[1536,2048]{1,0:T(8,128)(2,1)} %all-gather.11.cloned.1.call-done, f32[512]{0:T(512)S(1)} %copy-done.15, bf16[2048,512]{1,0:T(8,128)(2,1)S(1)} %gather_fusion.4, pred[2048]{0:T(1024)(128)(4,1)S(1)} %compare_and_fusion.1), kind=kOutput, calls=%fused_computation.48 | convolution fusion | flops 3223060480 | bytes 11538432 | tf_op jit(solution)/shard_map/dot_general | solution.py:119
  354.8 20.4 %all-gather.5.cloned.1.call-done = bf16[1536,2048]{1,0:T(8,128)(2,1)} async-done(((bf16[1536,512]{1,0:T(8,128)(2,1)}), bf16[1536,2048]{1,0:T(8,128)(2,1)}) %all-gather.5.cloned.1.call-update) | async-done | bytes 6291472 | tf_op jit(solution)/shard_map/all_gather | solution.py:117
  375.3 12.8 %convert_reduce_fusion.5 = (f32[512]{0:T(512)S(1)}, bf16[1536,512]{1,0:T(8,128)(2,1)S(1)}, f32[512]{0:T(512)S(1)}, bf16[1536,512]{1,0:T(8,128)(2,1)}, f32[512]{0...) fusion(f32[1536]{0:T(1024)S(1)} %fusion.94, ...), kind=kOutput, calls=%fused_computation.68 | convolution fusion | flops 3260807680 | bytes 28864512 | tf_op jit(solution)/shard_map/dot_general | solution.py:119
  389.2 6.7 fusion.105
  395.9 10.1 %fusion.104 = f32[1536,2048]{1,0:T(8,128)} fusion(bf16[1536,512]{1,0:T(8,128)(2,1)} %get-tuple-element.167, bf16[2048,512]{1,0:T(8,128)(2,1)S(1)} %gather_fusion.4, pred[2048]{0:T(1024)(128)(4,1)S(1)} %compare_and_fusion.1), kind=kOutput, calls=%fused_computation.174 | convolution fusion | flops 3222274048 | bytes 16254976 | tf_op jit(solution)/shard_map/dot_general | solution.py:127
  406.1 9.7 %fusion.103 = f32[1536,2048]{1,0:T(8,128)} fusion(bf16[1536,512]{1,0:T(8,128)(2,1)} %get-tuple-element.165, bf16[2048,512]{1,0:T(8,128)(2,1)S(1)} %gather_fusion.4, pred[2048]{0:T(1024)(128)(4,1)S(1)} %compare_and_fusion.1), kind=kOutput, calls=%fused_computation.173 | convolution fusion | flops 3222274048 | bytes 16254976 | tf_op jit(solution)/shard_map/dot_general | solution.py:127
  416.8 5.6 all-to-all-start.1
  422.4 6.3 fusion.113
  428.7 5.8 fusion.112
  434.5 5.0 add_add_fusion
  439.5 20.3 %gather_fusion.3 = f32[4096,512]{1,0:T(8,128)} fusion(f32[2048,512]{1,0:T(8,128)} %add_add_fusion, s32[4096]{0:T(1024)S(1)} %broadcast_clamp_fusion), kind=kCustom, calls=%fused_computation.4 | custom fusion | bytes 16793600 | tf_op jit(solution)/shard_map/jit(_take)/gather | solution.py:151
  459.8 8.1 %select_multiply_fusion = f32[8,512,512]{2,1,0:T(8,128)} fusion(f32[8,512,512]{2,1,0:T(8,128)} %bitcast.104, f32[8,512]{1,0:T(8,128)S(1)} %get-tuple-element.182, pred[8,512]{1,0:T(8,128)(4,1)S(1)} %get-tuple-element.183), kind=kLoop, calls=%fused_computation.29 | loop fusion | flops 4194304 | bytes 16797696 | tf_op jit(solution)/shard_map/mul | solution.py:151
  467.9 6.5 all-to-all-start
  475.1 3.7 pad_maximum_fusion
  479.5 177.2 %all-to-all-done = f32[8,512,512]{2,1,0:T(8,128)} async-done(((f32[8,512,512]{2,1,0:T(8,128)}), f32[8,512,512]{2,1,0:T(8,128)}, u32[]{:S(2)}, u32[]{:S(2)}) %all-to-all-start) | async-done | bytes 8388640 | tf_op jit(solution)/shard_map/all_to_all | solution.py:156
  656.7 4.5 reduce_sum.160
  661.3 4.1 broadcast_multiply_fusion
  665.4 3.4 convert_element_type.237
  668.7 2.2 convert_element_type.245
  671.1 7.0 fusion.54
  678.1 4.1 fusion.57
  682.3 16.0 %reduce-scatter.8.cloned.1.call-done = f32[1536,512]{1,0:T(8,128)} async-done(((f32[1536,2048]{1,0:T(8,128)}), f32[1536,512]{1,0:T(8,128)}) %reduce-scatter.8.cloned.1.call-update) | async-done | bytes 3145744 | tf_op jit(solution)/shard_map/reduce_scatter | solution.py:130
  698.3 2.1 convert_element_type.253
  700.4 6.8 fusion.60
  707.2 2.5 pad_maximum_fusion.1
  (173 shorter events, 41.1 us)
Async XLA Ops:
  7.2 320.9 %all-gather.7.cloned.1.call-start = ((), (), s32[]{:S(2)}) async-start(), calls=%async_computation.6 | async-start | bytes 4718592 | tf_op jit(solution)/shard_map/all_gather | solution.py:65
  9.3 329.1 %all-gather.9.cloned.1.call-start = ((), (), s32[]{:S(2)}) async-start(), calls=%async_computation.7 | async-start | bytes 7864320 | tf_op jit(solution)/shard_map/all_gather | solution.py:117
  107.0 7.2 %copy-start.6 = (f32[1536]{0:T(1024)}, f32[1536]{0:T(1024)S(1)}, u32[]{:S(2)}) copy-start(f32[1536]{0:T(1024)S(1)} %fusion.98) | copy-start | bytes 18436
  107.0 7.2 %copy-start.8 = (f32[1536]{0:T(1024)}, f32[1536]{0:T(1024)S(1)}, u32[]{:S(2)}) copy-start(f32[1536]{0:T(1024)S(1)} %broadcast_add_fusion.5) | copy-start | bytes 18436
  114.2 232.7 %all-gather.11.cloned.1.call-start = ((), (), s32[]{:S(2)}) async-start(), calls=%async_computation.8 | async-start | bytes 7864320 | tf_op jit(solution)/shard_map/all_gather | solution.py:117
  208.3 7.2 %copy-start.10 = (f32[1536]{0:T(1024)}, f32[1536]{0:T(1024)S(1)}, u32[]{:S(2)}) copy-start(f32[1536]{0:T(1024)S(1)} %fusion.97) | copy-start | bytes 18436
  208.4 7.2 %copy-start.12 = (f32[1536]{0:T(1024)}, f32[1536]{0:T(1024)S(1)}, u32[]{:S(2)}) copy-start(f32[1536]{0:T(1024)S(1)} %broadcast_add_fusion.4) | copy-start | bytes 18436
  215.6 159.7 %all-gather.5.cloned.1.call-start = ((), (), s32[]{:S(2)}) async-start(), calls=%async_computation.5 | async-start | bytes 7864320 | tf_op jit(solution)/shard_map/all_gather | solution.py:117
  319.5 7.5 %copy-start.14 = (s32[8]{0:T(128)S(1)}, s32[8]{0:T(128)}, u32[]{:S(2)}) copy-start(s32[8]{0:T(128)} %param.22) | copy-start | bytes 100
  326.7 338.7 %reduce-scatter.4.cloned.1.call-start = ((), (), s32[]{:S(2)}) async-start(), calls=%async_computation.9 | async-start | bytes 15728640 | tf_op jit(solution)/shard_map/reduce_scatter | solution.py:130
  328.0 10.4 %copy-start.15 = (f32[512]{0:T(512)S(1)}, f32[512]{0:T(512)}, u32[]{:S(2)}) copy-start(f32[512]{0:T(512)} %param.26) | copy-start | bytes 6148
  388.1 1.1 copy-start.19
  395.9 272.8 %reduce-scatter.6.cloned.1.call-start = ((), (), s32[]{:S(2)}) async-start(), calls=%async_computation.10 | async-start | bytes 15728640 | tf_op jit(solution)/shard_map/reduce_scatter | solution.py:130
  406.0 292.2 %reduce-scatter.8.cloned.1.call-start = ((), (), s32[]{:S(2)}) async-start(), calls=%async_computation.11 | async-start | bytes 15728640 | tf_op jit(solution)/shard_map/reduce_scatter | solution.py:130
  415.8 6.5 copy-start.21
  416.8 51.1 %all-to-all-start.1 = ((f32[8,1,512]{2,1,0:T(1,128)}), f32[8,1,512]{2,1,0:T(1,128)S(1)}, u32[]{:S(2)}, u32[]{:S(2)}) async-start(f32[8,1,512]{2,1,0:T(1,128)} %broadcast_in_dim.48), calls=%async_computation.4 | async-start | bytes 32768 | tf_op jit(solution)/shard_map/all_to_all | solution.py:157
  422.3 6.3 copy-start.20
  422.4 12.1 %slice-start.3 = ((s8[6291456]{0:T(1024)(128)(4,1)}), s8[4194304]{0:T(1024)(128)(4,1)S(1)}, s32[]{:S(2)}) async-start(s8[6291456]{0:T(1024)(128)(4,1)} %bitcast.114), calls=%async_computation.15 | async-start | bytes 8388608
  428.6 5.8 slice-start.4
  428.6 5.8 copy-start.18
  467.9 7.2 %copy-start.1 = (bf16[1,1536,512]{2,1,0:T(8,128)(2,1)S(1)}, bf16[1,1536,512]{2,1,0:T(8,128)(2,1)}, u32[]{:S(2)}) copy-start(bf16[1,1536,512]{2,1,0:T(8,128)(2,1)} %get-tuple-element.168) | copy-start | bytes 4718596
  467.9 7.2 %copy-start.2 = (bf16[1,1536,512]{2,1,0:T(8,128)(2,1)S(1)}, bf16[1,1536,512]{2,1,0:T(8,128)(2,1)}, u32[]{:S(2)}) copy-start(bf16[1,1536,512]{2,1,0:T(8,128)(2,1)} %get-tuple-element.169) | copy-start | bytes 4718596
  467.9 188.8 %all-to-all-start = ((f32[8,512,512]{2,1,0:T(8,128)}), f32[8,512,512]{2,1,0:T(8,128)}, u32[]{:S(2)}, u32[]{:S(2)}) async-start(f32[8,512,512]{2,1,0:T(8,128)} %select_multiply_fusion), calls=%async_computation.3 | async-start | bytes 16777216 | tf_op jit(solution)/shard_map/all_to_all | solution.py:156
  475.1 3.8 copy-start.16
  475.1 3.8 copy-start.17
  479.5 181.7 %copy-start = (f32[512,512]{1,0:T(8,128)S(1)}, f32[512,512]{1,0:T(8,128)}, u32[]{:S(2)}) copy-start(f32[512,512]{1,0:T(8,128)} %param.23) | copy-start | bytes 3145732
  479.5 181.7 %copy-start.5 = (f32[512,512]{1,0:T(8,128)S(1)}, f32[512,512]{1,0:T(8,128)}, u32[]{:S(2)}) copy-start(f32[512,512]{1,0:T(8,128)} %param.25) | copy-start | bytes 3145732
  665.4 12.7 %slice-start = ((s8[9437184]{0:T(1024)(128)(4,1)}), s8[1048576]{0:T(1024)(128)(4,1)S(1)}, s32[]{:S(2)}) async-start(s8[9437184]{0:T(1024)(128)(4,1)} %bitcast.102), calls=%async_computation.12 | async-start | bytes 2097152
  668.7 2.4 copy-start.4
  671.1 7.0 slice-start.1
  671.1 7.0 slice-start.2
  671.1 7.0 copy-start.7
  671.1 7.0 copy-start.9
  682.3 18.1 %copy-start.11 = (f32[1536]{0:T(1024)S(1)}, f32[1536]{0:T(1024)}, u32[]{:S(2)}) copy-start(f32[1536]{0:T(1024)} %copy-done.10) | copy-start | bytes 18436
  682.3 18.1 %copy-start.13 = (f32[1536]{0:T(1024)S(1)}, f32[1536]{0:T(1024)}, u32[]{:S(2)}) copy-start(f32[1536]{0:T(1024)} %copy-done.12) | copy-start | bytes 18436
  700.4 6.8 copy-start.3
Sparse Core Ops, SparseCore 0:
  10.7 76.0 all-gather.6
  114.3 48.8 all-gather.8
  215.7 48.8 all-gather.10
  326.8 48.4 all-gather.4
  396.0 99.0 reduce-scatter.3
  497.5 99.0 reduce-scatter.5
  599.2 99.0 reduce-scatter.7
where the time goes:
time: 728 us; the launch traced here: 717 us
  waiting for transfers between devices  214 us (29%)
  other arithmetic  203 us (28%)
  local copies, waits for them, and re-layouts  151 us (21%)
  matrix products  112 us (15%)
  starting transfers between devices  21.5 us (3%)
  between operations  14.9 us (2%)
    all_to_all x1, waiting for transfers between devices, shards(): lax.all_to_all(outgoing, 'clus', split_axis=0, concat_axis=0, tiled=True)  177 us
    reduce_sum x18, other arithmetic, count_block(): jnp.sum((row_block[:, :, None] == columns[None, None, :]).astype(jnp.floa...  116 us
    gather x3, local copies, waits for them, and re-layouts, shards(): self_term = 1.0 + LAMBDA_DIAG * (1.0 + jnp.diagonal(counted))  76.1 us
    dot_general x3, matrix products, shards(): jnp.dot(hidden_full, weight_fwd, preferred_element_type=jnp.float32)  29.2 us
    dot_general x3, matrix products, shards(): lax.dot_general(grad_pre, weight_back, (((1,), (1,)), ((), ())), preferre...  26.5 us
    mul x3, other arithmetic, build_counts(): return counted * live_rows[:, None] * live_rows[None, :]  24.4 us
    dynamic_update_slice x18, local copies, waits for them, and re-layouts, build_counts(): counted = lax.map(count_block, grouped).reshape(nodes, nodes)  23 us
    dot_general x3, matrix products, shards(): jnp.dot(adjacency, feature_shard, preferred_element_type=jnp.float32)  21.6 us
  transfers between devices with their start and end apart: 9, of which 3 were waited for; matrix products, arithmetic and copies ran while one was open for 60% of the time, Pallas kernels for 0%

commit v1 on v0

v1 whole, which is shorter than its diff:
```python
import functools

import jax
import jax.numpy as jnp
from jax import lax
from jax.experimental import pallas as pl
from jax.experimental.pallas import tpu as pltpu
from jax.sharding import PartitionSpec as P

D = 2048
MB = 3
STEP = 10

BETA_ONE = 0.9
BETA_TWO = 0.95
EPSILON = 1e-08
DECAY = 0.1
RATE_WEIGHT = 0.06
RATE_BIAS = 0.6

LANES = 128
DIGIT_BITS = 5
DIGITS = 6
STRIP = 32
SUBLANES = 8
TILE = 256
VMEM_BYTES = 48 * 1024 * 1024

GROUP, COLUMN, LIMITS = 0, 1, 2
STARTS = LIMITS + MB

F32, BF16 = jnp.float32, jnp.bfloat16


def launch(name, body, table, ins, outs, grid=(1,), after=(), alias=None, scratch=()):
    arrays = [array for array, _, _ in ins]
    in_specs = [
        pl.BlockSpec(memory_space=pl.ANY) if block is None else pl.BlockSpec(block, lambda *a, f=index: f(*a[:-1]))
        for _, block, index in ins
    ]
    unread = ([alias[0]] if alias else []) + list(after)
    out_specs = [pl.BlockSpec(block, lambda *a, f=index: f(*a[:-1])) for _, _, block, index in outs]

    def kernel(table_ref, *refs):
        kept = refs[: len(ins)] + refs[len(ins) + len(unread) :]
        body(table_ref, *kept)

    return pl.pallas_call(
        kernel,
        grid_spec=pltpu.PrefetchScalarGridSpec(
            num_scalar_prefetch=1,
            grid=grid,
            in_specs=in_specs + [pl.BlockSpec(memory_space=pl.ANY)] * len(unread),
            out_specs=out_specs,
            scratch_shapes=list(scratch),
        ),
        out_shape=[jax.ShapeDtypeStruct(shape, kind) for shape, kind, _, _ in outs],
        input_output_aliases={1 + len(ins): alias[1]} if alias else {},
        compiler_params=pltpu.CompilerParams(vmem_limit_bytes=VMEM_BYTES),
        cost_estimate=pl.CostEstimate(flops=1, bytes_accessed=1, transcendentals=0),
        name=name,
    )(table, *arrays, *unread)


def flip(values, axis, bit):
    size = lax.axis_size(axis)
    return lax.ppermute(values, axis, [(i, i ^ bit) for i in range(size)])


def product(left, right):
    return jnp.dot(left, right, preferred_element_type=F32)


def product_back(left, right):
    return lax.dot_general(left, right, (((1,), (1,)), ((), ())), preferred_element_type=F32)


def product_rows(left, right):
    return lax.dot_general(left, right, (((0,), (0,)), ((), ())), preferred_element_type=F32)


def put_rows(ref, first, rows):
    base = pl.multiple_of((first // SUBLANES) * SUBLANES, SUBLANES)
    offset = first - base
    spare = jnp.zeros((SUBLANES, rows.shape[1]), rows.dtype)
    moved = pltpu.roll(jnp.concatenate([rows, spare], axis=0), offset, 0)
    head = ref[pl.ds(base, SUBLANES), :]
    row_ids = lax.broadcasted_iota(jnp.int32, head.shape, 0)
    ref[pl.ds(base, SUBLANES), :] = jnp.where(row_ids < offset, head, moved[:SUBLANES])
    ref[pl.ds(pl.multiple_of(base + SUBLANES, SUBLANES), rows.shape[0]), :] = moved[SUBLANES:]


def take_rows(ref, first, count):
    base = pl.multiple_of((first // SUBLANES) * SUBLANES, SUBLANES)
    length = count + SUBLANES
    moved = pltpu.roll(ref[pl.ds(base, length), :], lax.rem(length - (first - base), length), 0)
    return moved[:count]


def pick_kernel(table_ref, source_ref, out_ref):
    out_ref[...] = source_ref[0]


def pick(table, stacked, m, after=()):
    _, rows, width = stacked.shape
    return launch(
        f"pick{m}", pick_kernel, table,
        [(stacked, (1, rows // 4, width), lambda i: (m, i, 0))],
        [((rows, width), stacked.dtype, (rows // 4, width), lambda i: (i, 0))],
        grid=(4,), after=after,
    )[0]


def gather_kernel(m, table_ref, neighbour_ref, feature_ref, matrix_ref, scale_ref, mixed_ref):
    limit = table_ref[LIMITS + m]
    tile, nodes = matrix_ref.shape
    words = -(-(nodes // LANES) // DIGITS)
    lane = lax.broadcasted_iota(jnp.int32, (STRIP, LANES), 1)
    for strip in range(tile // STRIP):
        rows = pl.ds(strip * STRIP, STRIP)
        first_row = pl.program_id(0) * tile + strip * STRIP
        entries = neighbour_ref[0, rows, :]
        row_ids = first_row + lax.broadcasted_iota(jnp.int32, entries.shape, 0)
        valid = (entries < limit) & (row_ids < limit)
        low = entries & (LANES - 1)
        high = entries >> 7
        digits = []
        for word in range(words):
            inside = valid & (high >= word * DIGITS) & (high < (word + 1) * DIGITS)
            shift = jnp.where(inside, (high - word * DIGITS) * DIGIT_BITS, 0)
            digits.append(jnp.where(inside, jnp.left_shift(1, shift), 0))
        sums = [jnp.zeros((STRIP, LANES), jnp.int32) for _ in range(words)]
        for entry in range(entries.shape[1]):
            hit = lane == low[:, entry : entry + 1]
            for word in range(words):
                sums[word] = sums[word] + jnp.where(hit, digits[word][:, entry : entry + 1], 0)
        own_row = first_row + lax.broadcasted_iota(jnp.int32, (STRIP, LANES), 0)
        for block in range(nodes // LANES):
            word, digit = block // DIGITS, block % DIGITS
            count = jnp.right_shift(sums[word], digit * DIGIT_BITS) & ((1 << DIGIT_BITS) - 1)
            count = jnp.where(lane + block * LANES == own_row, 2 * count + 2, count)
            matrix_ref[rows, block * LANES : (block + 1) * LANES] = count.astype(F32).astype(BF16)
        degree = 1.0 + jnp.sum(valid.astype(F32), axis=1, keepdims=True)
        scale_ref[rows, :] = (row_ids[:, :1] < limit).astype(F32) / degree
    mixed_ref[...] = (product(matrix_ref[...], feature_ref[0]) * scale_ref[...]).astype(BF16)


def gather(table, m, neighbours, features, after=()):
    _, nodes, entries = neighbours.shape
    width = features.shape[2]
    return launch(
        f"gather{m}", functools.partial(gather_kernel, m), table,
        [
            (neighbours, (1, TILE, entries), lambda i: (m, i, 0)),
            (features, (1, nodes, width), lambda i: (m, 0, 0)),
        ],
        [
            ((nodes, nodes), BF16, (TILE, nodes), lambda i: (i, 0)),
            ((nodes, 1), F32, (TILE, 1), lambda i: (i, 0)),
            ((nodes, width), BF16, (TILE, width), lambda i: (i, 0)),
        ],
        grid=(nodes // TILE,), after=after,
    )


def mix_kernel(table_ref, matrix_ref, scale_ref, feature_ref, mixed_ref):
    mixed_ref[...] = (product(matrix_ref[...], feature_ref[...]) * scale_ref[...]).astype(BF16)


def mix(table, m, matrix, scale, far, after=()):
    nodes, width = far.shape
    return launch(
        f"mix{m}", mix_kernel, table,
        [
            (matrix, (TILE, nodes), lambda i: (i, 0)),
            (scale, (TILE, 1), lambda i: (i, 0)),
            (far, (nodes, width), lambda i: (0, 0)),
        ],
        [((nodes, width), BF16, (TILE, width), lambda i: (i, 0))],
        grid=(nodes // TILE,), after=after,
    )[0]


def place_kernel(groups, table_ref, slots_ref, weight_ref, mate_ref, rows_ref):
    owner = pl.program_id(0)

    @pl.when(owner == 0)
    def _():
        rows_ref[...] = jnp.zeros_like(rows_ref)

    put_rows(rows_ref, table_ref[STARTS + owner], slots_ref[...].astype(F32))

    @pl.when(owner == groups - 1)
    def _():
        width = weight_ref.shape[2]
        for block in range(weight_ref.shape[0]):
            source = pl.multiple_of((table_ref[COLUMN] ^ block) * width, width)
            rows = rows_ref[pl.ds(source, width), :].astype(BF16)
            weight_ref[block] = rows
            if block % 2:
                mate_ref[block // 2] = rows


def place(table, slots, groups, after=()):
    capacity, width = slots.shape[0] // groups, slots.shape[1]
    blocks = D // width
    return launch(
        "place", functools.partial(place_kernel, groups), table,
        [(slots, (capacity, width), lambda i: (i, 0))],
        [
            ((blocks, width, width), BF16, (blocks, width, width), lambda i: (0, 0, 0)),
            ((blocks // 2, width, width), BF16, (blocks // 2, width, width), lambda i: (0, 0, 0)),
        ],
        grid=(groups,), after=after, scratch=[pltpu.VMEM((D + capacity + SUBLANES, width), F32)],
    )


def layer_kernel(m, table_ref, *refs):
    mixed_refs, (weight_ref, bias_ref, grad_ref, out_ref, pre_ref, sum_ref) = refs[:4], refs[4:]
    tile = out_ref.shape[1]
    preact = bias_ref[...]
    for block in range(4):
        preact = preact + product(mixed_refs[block][...], weight_ref[block])
    first_row = pl.program_id(0) * tile
    row_ids = first_row + lax.broadcasted_iota(jnp.int32, preact.shape, 0)
    live = row_ids < table_ref[LIMITS + m]
    gate = jax.nn.sigmoid(preact)
    out_ref[0] = jnp.where(live, preact * gate, 0.0).astype(BF16)
    slope = gate * (1.0 + preact * (1.0 - gate))
    grad_pre = jnp.where(live, grad_ref[0].astype(F32) * slope, 0.0).astype(BF16)
    pre_ref[...] = grad_pre

    @pl.when(pl.program_id(0) == 0)
    def _():
        sum_ref[...] = jnp.zeros_like(sum_ref)

    sum_ref[...] += jnp.sum(grad_pre.astype(F32), axis=0, keepdims=True)


def layer(table, m, mixed, weight, bias, out_grad, outputs, after=()):
    nodes, width = mixed[0].shape
    return launch(
        f"layer{m}", functools.partial(layer_kernel, m), table,
        [(part, (TILE, width), lambda i: (i, 0)) for part in mixed]
        + [
            (weight, weight.shape, lambda i: (0, 0, 0)),
            (bias, (1, width), lambda i: (0, 0)),
            (out_grad, (1, TILE, width), lambda i: (m, i, 0)),
        ],
        [
            ((MB, nodes, width), BF16, (1, TILE, width), lambda i: (m, i, 0)),
            ((nodes, width), BF16, (TILE, width), lambda i: (i, 0)),
            ((1, width), F32, (1, width), lambda i: (0, 0)),
        ],
        grid=(nodes // TILE,), after=after, alias=None if outputs is None else (outputs, 0),
    )


def back_kernel(chunks, table_ref, here_ref, mate_ref, weight_ref, weight_mate_ref, *out_refs):
    own_ref, away_refs = out_refs[0], out_refs[1:]
    here, mate = here_ref[...], mate_ref[...]
    away = (product_back(here, weight_ref[2]) + product_back(mate, weight_mate_ref[1])).astype(BF16)
    step = away.shape[1] // chunks
    for chunk in range(chunks):
        away_refs[chunk][...] = away[:, chunk * step : (chunk + 1) * step]
    own_ref[...] = product_back(here, weight_ref[0]) + product_back(mate, weight_mate_ref[0])


def back(table, m, here, mate, weight, weight_mate, chunks, after=()):
    nodes, width = here.shape
    step = width // chunks
    return launch(
        f"back{m}", functools.partial(back_kernel, chunks), table,
        [
            (here, (TILE, width), lambda i: (i, 0)),
            (mate, (TILE, width), lambda i: (i, 0)),
            (weight, weight.shape, lambda i: (0, 0, 0)),
            (weight_mate, weight_mate.shape, lambda i: (0, 0, 0)),
        ],
        [((nodes, width), F32, (TILE, width), lambda i: (i, 0))]
        + [((nodes, step), BF16, (TILE, step), lambda i: (i, 0)) for _ in range(chunks)],
        grid=(nodes // TILE,), after=after,
    )


def scatter_kernel(table_ref, own_ref, got_ref, scale_ref, matrix_ref, out_ref, sum_ref):
    @pl.when(pl.program_id(0) == 0)
    def _():
        grad_mixed = (own_ref[...] + got_ref[...].astype(F32)).astype(BF16)
        sum_ref[...] = (grad_mixed.astype(F32) * scale_ref[...]).astype(BF16)

    out_ref[0] = product_rows(matrix_ref[...], sum_ref[...]).astype(BF16)


def scatter(table, m, chunk, own, got, scale, matrix, grads, after=()):
    nodes, width = own.shape
    step = got.shape[1]
    return launch(
        f"scatter{m}_{chunk}", scatter_kernel, table,
        [
            (own, (nodes, step), lambda i: (0, chunk)),
            (got, (nodes, step), lambda i: (0, 0)),
            (scale, (nodes, 1), lambda i: (0, 0)),
            (matrix, (nodes, TILE), lambda i: (0, i)),
        ],
        [((MB, nodes, width), BF16, (1, TILE, step), lambda i: (m, i, chunk))],
        grid=(nodes // TILE,), after=after, alias=None if grads is None else (grads, 0),
        scratch=[pltpu.VMEM((nodes, step), BF16)],
    )[0]


def weight_kernel(parts, table_ref, *refs):
    blocks = len(refs[: MB * 4]) // MB
    mixed_refs, pre_refs = refs[: MB * blocks], refs[MB * blocks : MB * blocks + MB]
    bias_refs = refs[MB * blocks + MB : MB * blocks + 2 * MB]
    keep_refs, sent_refs = refs[MB * blocks + 2 * MB :][:2], refs[MB * blocks + 2 * MB + 2 : -2]
    bias_out_ref, total_ref = refs[-2:]
    step = pl.program_id(0)

    for m in range(MB):

        @pl.when(step // parts == m)
        def _(m=m):
            for block in range(blocks):
                term = product_rows(mixed_refs[m * blocks + block][...], pre_refs[m][...])
                if m == 0:
                    term = jnp.where(step == 0, term, total_ref[block] + term)
                else:
                    term = total_ref[block] + term
                total_ref[block] = term

    @pl.when(step == parts * MB - 1)
    def _():
        bias_out_ref[...] = sum(ref[...] for ref in bias_refs)
        width = total_ref.shape[1]
        quarter = width // 4
        upper = (table_ref[GROUP] & 1) == 1
        for block in range(blocks):
            rows = pl.ds(pl.multiple_of((table_ref[COLUMN] ^ block) * width, width), width)
            for chunk in range(2):
                low = total_ref[block, :, chunk * quarter : (chunk + 1) * quarter]
                high = total_ref[block, :, (2 + chunk) * quarter : (3 + chunk) * quarter]
                keep_refs[chunk][rows, :] = jnp.where(upper, high, low)
                sent_refs[chunk][rows, :] = jnp.where(upper, low, high).astype(BF16)


def weight_gradient(table, mixed, pres, biases, after=()):
    nodes, width = pres[0].shape
    parts = 2
    rows, quarter = nodes // parts, width // 4
    blocks = len(mixed[0])

    def turn(m):
        return lambda i: (jnp.clip(i - m * parts, 0, parts - 1), 0)

    whole = lambda i: (0, 0)
    return launch(
        "weight", functools.partial(weight_kernel, parts), table,
        [(mixed[m][b], (rows, width), turn(m)) for m in range(MB) for b in range(blocks)]
        + [(pres[m], (rows, width), turn(m)) for m in range(MB)]
        + [(bias, (1, width), whole) for bias in biases],
        [((D, quarter), F32, (D, quarter), whole)] * 2
        + [((D, quarter), BF16, (D, quarter), whole)] * 2
        + [((1, width), F32, (1, width), whole)],
        grid=(parts * MB,), after=after, scratch=[pltpu.VMEM((blocks, width, width), F32)],
    )


def pairs_kernel(capacity, table_ref, keep_ref, got_ref, bias_ref, bias_got_ref, held_ref, sent_ref, bias_out_ref, total_ref):
    rows = keep_ref.shape[0]
    total_ref[:rows, :] = keep_ref[...] + got_ref[...].astype(F32)
    total_ref[rows:, :] = jnp.zeros((2 * capacity + SUBLANES, keep_ref.shape[1]), F32)
    bit = (table_ref[GROUP] >> 1) & 1
    for j in range(held_ref.shape[0]):
        kept, gone = 2 * j + bit, 2 * j + 1 - bit
        held_ref[j] = take_rows(total_ref, table_ref[STARTS + 2 * kept], 2 * capacity)
        sent_ref[j] = take_rows(total_ref, table_ref[STARTS + 2 * gone], 2 * capacity).astype(BF16)
    bias_out_ref[...] = bias_ref[...] + bias_got_ref[...]


def pairs(table, name, keep, got, bias, bias_got, groups, capacity, after=()):
    rows, width = keep.shape
    count = groups // 4
    shape = (count, 2 * capacity, width)
    flat, deep = (lambda i: (0, 0)), (lambda i: (0, 0, 0))
    return launch(
        name, functools.partial(pairs_kernel, capacity), table,
        [(array, array.shape, flat) for array in (keep, got, bias, bias_got)],
        [(shape, F32, shape, deep), (shape, BF16, shape, deep), (bias.shape, F32, bias.shape, flat)],
        after=after, scratch=[pltpu.VMEM((rows + 2 * capacity + SUBLANES, width), F32)],
    )


def halve_kernel(level, table_ref, held_ref, got_ref, bias_ref, bias_got_ref, out_ref, sent_ref, bias_out_ref):
    bit = (table_ref[GROUP] >> level) & 1
    for j in range(out_ref.shape[0]):
        kept, gone = 2 * j + bit, 2 * j + 1 - bit
        out_ref[j] = held_ref[kept] + got_ref[kept].astype(F32)
        sent_ref[j] = (held_ref[gone] + got_ref[gone].astype(F32)).astype(BF16)
    bias_out_ref[...] = bias_ref[...] + bias_got_ref[...]


def halve(table, name, level, held, got, bias, bias_got, after=()):
    shape = (held.shape[0] // 2,) + held.shape[1:]
    flat, deep = (lambda i: (0, 0)), (lambda i: (0, 0, 0))
    return launch(
        name, functools.partial(halve_kernel, level), table,
        [(held, held.shape, deep), (got, got.shape, deep), (bias, bias.shape, flat), (bias_got, bias.shape, flat)],
        [(shape, F32, shape, deep), (shape, BF16, shape, deep), (bias.shape, F32, bias.shape, flat)],
        after=after,
    )


def part_kernel(capacity, table_ref, held_ref, got_ref, bias_ref, bias_got_ref, own_ref, sent_ref, bias_out_ref, total_ref):
    rows = held_ref.shape[1]
    total_ref[:rows, :] = held_ref[0] + got_ref[0].astype(F32)
    total_ref[rows:, :] = jnp.zeros((SUBLANES, held_ref.shape[2]), F32)
    own = table_ref[GROUP]
    first = table_ref[STARTS + (own & ~1)]
    own_ref[...] = take_rows(total_ref, table_ref[STARTS + own] - first, capacity)
    sent_ref[...] = take_rows(total_ref, table_ref[STARTS + (own ^ 1)] - first, capacity).astype(BF16)
    bias_out_ref[...] = bias_ref[...] + bias_got_ref[...]


def part(table, name, held, got, bias, bias_got, capacity, after=()):
    shape = (capacity, held.shape[2])
    flat, deep = (lambda i: (0, 0)), (lambda i: (0, 0, 0))
    return launch(
        name, functools.partial(part_kernel, capacity), table,
        [(held, held.shape, deep), (got, got.shape, deep), (bias, bias.shape, flat), (bias_got, bias.shape, flat)],
        [(shape, F32, shape, flat), (shape, BF16, shape, flat), (bias.shape, F32, bias.shape, flat)],
        after=after, scratch=[pltpu.VMEM((held.shape[1] + SUBLANES, held.shape[2]), F32)],
    )


def adamw_update(current, first_moment, second_moment, gradient, step_rate):
    first_new = BETA_ONE * first_moment + (1.0 - BETA_ONE) * gradient
    second_new = BETA_TWO * second_moment + (1.0 - BETA_TWO) * gradient * gradient
    fixed_first = first_new / (1.0 - BETA_ONE**STEP)
    fixed_second = second_new / (1.0 - BETA_TWO**STEP)
    updated = current - step_rate * (
        fixed_first / (jnp.sqrt(fixed_second) + EPSILON) + DECAY * current
    )
    return (updated, first_new, second_new)


def adamw_kernel(groups, table_ref, *refs):
    own_refs, got_refs, (bias_grad_ref, *states), outs = refs[:2], refs[2:4], refs[4:11], refs[11:]
    weights, biases = states[:3], states[3:]
    rows, width = weights[0].shape
    quarter = width // 4
    own = table_ref[GROUP]
    row_ids = pl.program_id(0) * rows + lax.broadcasted_iota(jnp.int32, (rows, quarter), 0)
    used = row_ids < table_ref[STARTS + groups + own]
    for block in range(4):
        mine = (own & 1) == block // 2
        gradient = jnp.where(mine, own_refs[block % 2][...], got_refs[block % 2][...].astype(F32))
        columns = slice(block * quarter, (block + 1) * quarter)
        results = adamw_update(*(ref[:, columns] for ref in weights), gradient, RATE_WEIGHT)
        for out_ref, result in zip(outs[:3], results):
            out_ref[:, columns] = jnp.where(used, result, 0.0)
    results = adamw_update(*(ref[...] for ref in biases), bias_grad_ref[...], RATE_BIAS)
    for out_ref, result in zip(outs[3:], results):
        out_ref[...] = result


def adamw(table, groups, own, got, bias_grad, weights, biases, after=()):
    capacity, width = weights[0].shape
    steps = 4 if capacity % 64 == 0 and capacity >= 256 else 1
    rows, quarter = capacity // steps, width // 4
    down, fixed = (lambda i: (i, 0)), (lambda i: (0, 0))
    return launch(
        "adamw", functools.partial(adamw_kernel, groups), table,
        [(array, (rows, quarter), down) for array in (*own, *got)]
        + [(bias_grad, (1, width), fixed)]
        + [(array, (rows, width), down) for array in weights]
        + [(array, (1, width), fixed) for array in biases],
        [((capacity, width), F32, (rows, width), down)] * 3 + [((1, width), F32, (1, width), fixed)] * 3,
        grid=(steps,), after=after,
    )


def shards(
    features,
    neighbours,
    node_counts,
    row_counts,
    master_weight,
    weight_first,
    weight_second,
    master_bias,
    bias_first,
    bias_second,
    out_grad,
):
    groups = lax.axis_size("clus")
    capacity, width = master_weight.shape
    owner_ids = jnp.arange(groups, dtype=jnp.int32)
    starts = jnp.sum(jnp.where(owner_ids[None, :] < owner_ids[:, None], row_counts[None, :], 0), axis=1)
    table = jnp.concatenate(
        [
            jnp.stack([lax.axis_index("clus"), lax.axis_index("col")]).astype(jnp.int32),
            node_counts[:, 0],
            starts.astype(jnp.int32),
            row_counts,
        ]
    )
    bias_row, bias_first_row, bias_second_row = (
        array.reshape(1, width) for array in (master_bias, bias_first, bias_second)
    )

    picked = []
    for m in range(MB):
        picked.append(pick(table, features, m, picked[-1:]))
    far = [flip(part_, "col", 2) for part_ in picked]
    slots = lax.all_gather(master_weight.astype(BF16), "clus", axis=0, tiled=True)

    matrix, scale, mixed = [], [], []
    last = picked[-1]
    for m in range(MB):
        matrix_m, scale_m, here = gather(table, m, neighbours, features, [last])
        matrix.append(matrix_m)
        scale.append(scale_m)
        mixed.append([here, flip(here, "col", 1)])
        last = here

    def aggregate(m):
        nonlocal last
        last = there = mix(table, m, matrix[m], scale[m], far[m], [last])
        mixed[m] += [there, flip(there, "col", 1)]

    outputs, input_grads = None, None
    pres, mates, biases, own, away = [], [], [], [], []

    def forward(m):
        nonlocal last, outputs
        outputs, grad_pre, bias_sum = layer(table, m, mixed[m], weight, bias_row, out_grad, outputs, [last])
        pres.append(grad_pre)
        mates.append(flip(grad_pre, "col", 1))
        biases.append(bias_sum)
        last = grad_pre

    def backward(m, chunks):
        nonlocal last
        own_m, *away_m = back(table, m, pres[m], mates[m], weight, weight_mate, chunks, [last])
        own.append(own_m)
        away.append([flip(chunk, "col", 2) for chunk in away_m])
        last = own_m

    def finish(m):
        nonlocal last, input_grads
        for chunk, got in enumerate(away[m]):
            last = input_grads = scatter(table, m, chunk, own[m], got, scale[m], matrix[m], input_grads, [last])

    aggregate(0)
    aggregate(1)
    weight, for_mate = place(table, slots, groups, [last])
    weight_mate = flip(for_mate, "col", 1)
    last = for_mate
    forward(0)
    forward(1)
    backward(0, 1)
    backward(1, 1)
    aggregate(2)
    forward(2)
    backward(2, 2)
    *held, bias_sum = weight_gradient(table, mixed, pres, biases, [last])
    keep, sent = held[:2], held[2:]
    last = bias_sum
    got = [flip(chunk, "clus", 1) for chunk in sent]
    bias_got = flip(bias_sum, "clus", 1)
    finish(0)

    held = [None, None]
    zero = jnp.zeros_like(bias_sum)
    level, bit = 1, 2
    while bit < groups:
        for chunk in range(2):
            here, there = (bias_sum, bias_got) if chunk == 0 else (zero, zero)
            if level == 1:
                held[chunk], out, total = pairs(
                    table, f"pairs{chunk}", keep[chunk], got[chunk], here, there, groups, capacity, [last]
                )
            else:
                held[chunk], out, total = halve(
                    table, f"halve{level}_{chunk}", level, held[chunk], got[chunk], here, there, [last]
                )
            last = out
            got[chunk] = flip(out, "clus", bit)
            if chunk == 0:
                new_sum, new_got = total, flip(total, "clus", bit)
        bias_sum, bias_got = new_sum, new_got
        level, bit = level + 1, 2 * bit
    finish(1)
    mine, other = [], []
    for chunk in range(2):
        here, there = (bias_sum, bias_got) if chunk == 0 else (zero, zero)
        own_rows, out, total = part(
            table, f"part{chunk}", held[chunk], got[chunk], here, there, capacity, [last]
        )
        last = out
        mine.append(own_rows)
        other.append(flip(out, "clus", 1))
        if chunk == 0:
            bias_total = total
    updated = adamw(
        table, groups, mine, other, bias_total,
        (master_weight, weight_first, weight_second), (bias_row, bias_first_row, bias_second_row), [last],
    )
    last = updated[0]
    finish(2)
    return (outputs, input_grads, *updated[:3], *(row.reshape(width) for row in updated[3:]))


def solution(mesh):
    in_specs = (
        P(None, "clus", "col"),
        P(None, "clus", None),
        P(None, "clus"),
        P(),
        P("clus", "col"),
        P("clus", "col"),
        P("clus", "col"),
        P("col"),
        P("col"),
        P("col"),
        P(None, "clus", "col"),
    )
    out_specs = (
        P(None, "clus", "col"),
        P(None, "clus", "col"),
        P("clus", "col"),
        P("clus", "col"),
        P("clus", "col"),
        P("col"),
        P("col"),
        P("col"),
    )
    return jax.shard_map(shards, mesh=mesh, in_specs=in_specs, out_specs=out_specs, check_vma=False)
```

time: 728 us -> 344 us (0.47); the launches traced: 717 us -> 342 us
  Pallas kernels: 0 us -> 210 us
  other arithmetic: 203 us -> 2.2 us
  waiting for transfers between devices: 214 us -> 63.5 us
  local copies, waits for them, and re-layouts: 151 us -> 23.6 us
  matrix products: 112 us -> 0 us
    pallas_call x0 -> x28, Pallas kernels: none -> 210 us  [launch(): pl.pallas_call(kernel, grid_spec=pltpu.PrefetchScalarGridSpec(num_scalar_...]
    all_to_all x2 -> x0, waiting for transfers between devices: 177 us -> none  [the longest x1 177 us: shards(): lax.all_to_all(outgoing, 'clus', split_axis=0, concat_axis=0, tiled=True)]
    reduce_sum x27 -> x1, other arithmetic: 142 us -> 0.12 us  [shards(): jnp.sum(jnp.where(owner_ids[None, :] < owner_ids[:, None], row_counts[Non...]
    dot_general x15 -> x0, matrix products: 112 us -> none  [the longest x3 29.2 us: shards(): jnp.dot(hidden_full, weight_fwd, preferred_element_type=jnp.float32)]
    gather x5 -> x0, local copies, waits for them, and re-layouts: 107 us -> none  [the longest x3 76.1 us: shards(): self_term = 1.0 + LAMBDA_DIAG * (1.0 + jnp.diagonal(counted))]
    ppermute x0 -> x28, waiting for transfers between devices: none -> 63.5 us  [flip(): return lax.ppermute(values, axis, [(i, i ^ bit) for i in range(size)])]
    mul x5 -> x0, other arithmetic: 36.6 us -> none  [the longest x3 24.4 us: build_counts(): return counted * live_rows[:, None] * live_rows[None, :]]
    ppermute x0 -> x28, starting transfers between devices: none -> 27.8 us  [flip(): return lax.ppermute(values, axis, [(i, i ^ bit) for i in range(size)])]
  transfers between devices with their start and end apart: 9 -> 29, of which waited for: 3 -> 10; matrix products, arithmetic and copies ran while one was open for 60% -> 2% of each run, Pallas kernels for 0% -> 57%
where the time goes in v1:
time: 344 us; the launch traced here: 342 us
  Pallas kernels  210 us (61%)
  waiting for transfers between devices  63.5 us (18%)
  starting transfers between devices  27.8 us (8%)
  local copies, waits for them, and re-layouts  23.6 us (7%)
  between operations  14.4 us (4%)
    pallas_call x28, Pallas kernels, launch(): pl.pallas_call(kernel, grid_spec=pltpu.PrefetchScalarGridSpec(num_scalar_...  210 us
    ppermute x28, waiting for transfers between devices, flip(): return lax.ppermute(values, axis, [(i, i ^ bit) for i in range(size)])  63.5 us
    ppermute x28, starting transfers between devices, flip(): return lax.ppermute(values, axis, [(i, i ^ bit) for i in range(size)])  27.8 us
    unnamed x88, local copies, waits for them, and re-layouts  23.5 us
  transfers between devices with their start and end apart: 29, of which 10 were waited for; matrix products, arithmetic and copies ran while one was open for 2% of the time, Pallas kernels for 57%

profile of v1, /device:TPU:0, one launch (start us, length us, event | category | flops | bytes accessed | tf_op | source)
XLA Modules:
  0.0 341.7 jit_solution(3811197281714287951)
XLA Ops:
  7.2 2.1 convert_element_type.3
  9.6 2.8 pick0.1.refs_1_
  12.3 3.0 collective-permute-start.4
  15.4 4.1 %pick1.1.refs_1_ = bf16[1536,512]{1,0:T(8,128)(2,1)} custom-call(s32[21]{0:T(128)S(1)} %concatenate.3.table_ref, bf16[3,1536,512]{2,1,0:T(8,128)(2,1)} %refs_1_.5, bf16[1536,512]{1,0:T(8,128)(2,1)S(1)} %pick0.1.refs_1_), custom_call_target="tpu_custom_call" | custom-call | flops 1 | bytes 1 | tf_op jit(solution)/shard_map/pick1/pallas_call | solution.py:48
  19.5 2.8 pick2.1.refs_2_
  22.4 2.1 copy.29.refs_0_
  24.4 19.5 %gather0.1 = (bf16[1536,1536]{1,0:T(8,128)(2,1)}, f32[1536,1]{1,0:T(8,128)S(1)}, bf16[1536,512]{1,0:T(8,128)(2,1)}) custom-call(s32[21]{0:T(128)S(1)} %concatenate.3.table_ref, s32[3,1536,16]{2,1,0:T(8,128)} %copy.29.refs_0_, bf16[3,1536,512]{2,1,0:T(8,128)(2,1)} %refs_1_.5, bf16[1536,512]{1,0:T(8,128)(2,1)S(1)} %pick2.1.refs_2_), custom_call_target="tpu_custom_call" | custom-call | flops 1 | bytes 1 | tf_op jit(solution)/shard_map/gather0/pallas_call | solution.py:48
  44.1 19.5 %gather1.1 = (bf16[1536,1536]{1,0:T(8,128)(2,1)}, f32[1536,1]{1,0:T(8,128)S(1)}, bf16[1536,512]{1,0:T(8,128)(2,1)}) custom-call(s32[21]{0:T(128)S(1)} %concatenate.3.table_ref, s32[3,1536,16]{2,1,0:T(8,128)} %copy.29.refs_0_, bf16[3,1536,512]{2,1,0:T(8,128)(2,1)} %refs_1_.5, bf16[1536,512]{1,0:T(8,128)(2,1)} %get-tuple-element.61.refs_2_.refs_0_), custom_call_target="tpu_custom_call" | custom-call | flops 1 | bytes 1 | tf_op jit(solution)/shard_map/gather1/pallas_call | solution.py:48
  63.5 19.4 %gather2.1 = (bf16[1536,1536]{1,0:T(8,128)(2,1)}, f32[1536,1]{1,0:T(8,128)S(1)}, bf16[1536,512]{1,0:T(8,128)(2,1)S(1)}) custom-call(s32[21]{0:T(128)S(1)} %concatenate.3.table_ref, s32[3,1536,16]{2,1,0:T(8,128)} %copy.29.refs_0_, bf16[3,1536,512]{2,1,0:T(8,128)(2,1)} %refs_1_.5, bf16[1536,512]{1,0:T(8,128)(2,1)} %get-tuple-element.62.refs_2_.refs_0_.refs_4_), custom_call_target="tpu_custom_call" | custom-call | flops 1 | bytes 1 | tf_op jit(solution)/shard_map/gather2/pallas_call | solution.py:48
  82.9 0.9 copy-done.15
  83.8 6.9 %mix0.1.refs_3_.refs_2_ = bf16[1536,512]{1,0:T(8,128)(2,1)S(1)} custom-call(s32[21]{0:T(128)S(1)} %concatenate.3.table_ref, bf16[1536,1536]{1,0:T(8,128)(2,1)} %get-tuple-element.68.refs_0_.refs_3_, f32[1536,1]{1,0:T(8,128)S(1)} %get-tuple-element.69.refs_1_.refs_2_, bf16[1536,512]{1,0:T(8,128)(2,1)} %collective-permute-done.4.refs_2_, ...), custom_call_target="tpu_custom_call" | custom-call | flops 1 | bytes 1 | tf_op jit(solution)/shard_map/mix0/pallas_call | solution.py:48
  91.4 6.9 %mix1.1.refs_1_.refs_2_.refs_6_ = bf16[1536,512]{1,0:T(8,128)(2,1)S(1)} custom-call(s32[21]{0:T(128)S(1)} %concatenate.3.table_ref, bf16[1536,1536]{1,0:T(8,128)(2,1)} %get-tuple-element.66.refs_0_.refs_3_, f32[1536,1]{1,0:T(8,128)S(1)} %get-tuple-element.67.refs_1_.refs_2_, bf16[1536,512]{1,0:T(8,128)(2,1)} %collective-permute-done.3.refs_2_, ...), custom_call_target="tpu_custom_call" | custom-call | flops 1 | bytes 1 | tf_op jit(solution)/shard_map/mix1/pallas_call | solution.py:48
  98.8 9.3 %place.1 = (bf16[4,512,512]{2,1,0:T(8,128)(2,1)S(1)}, bf16[2,512,512]{2,1,0:T(8,128)(2,1)}) custom-call(s32[21]{0:T(128)S(1)} %concatenate.3.table_ref, bf16[4096,512]{1,0:T(8,128)(2,1)} %all-gather.2.cloned.1.call-done.refs_0_, bf16[1536,512]{1,0:T(8,128)(2,1)S(1)} %mix1.1.refs_1_.refs_2_.refs_6_), custom_call_target="tpu_custom_call" | custom-call | flops 1 | bytes 1 | tf_op jit(solution)/shard_map/place/pallas_call | solution.py:48
  108.1 1.4 copy-done.1
  109.5 10.0 %layer0.1 = (bf16[3,1536,512]{2,1,0:T(8,128)(2,1)}, bf16[1536,512]{1,0:T(8,128)(2,1)S(1)}, f32[1,512]{1,0:T(1,128)S(1)}) custom-call(s32[21]{0:T(128)S(1)} %concatenate.3.table_ref, bf16[1536,512]{1,0:T(8,128)(2,1)} %get-tuple-element.61.refs_2_.refs_0_, bf16[1536,512]{1,0:T(8,128)(2,1)} %collective-permute-done.6.refs_1_, bf16[1536,512]{1,0:T(8,128)(2,1)} %copy-done.3, ...), custom_call_target="tpu_custom_call" | custom-call | flops 1 | bytes 1 | tf_op jit(solution)/shard_map/layer0/pallas_call | solution.py:48
  119.6 1.1 copy-done.8
  120.6 10.3 %layer1.1 = (bf16[3,1536,512]{2,1,0:T(8,128)(2,1)}, bf16[1536,512]{1,0:T(8,128)(2,1)S(1)}, f32[1,512]{1,0:T(1,128)S(1)}) custom-call(s32[21]{0:T(128)S(1)} %concatenate.3.table_ref, bf16[1536,512]{1,0:T(8,128)(2,1)} %get-tuple-element.62.refs_2_.refs_0_.refs_4_, ...), custom_call_target="tpu_custom_call", output_to_operand_aliasing={{0}: (8, {})} | custom-call | flops 1 | bytes 1 | tf_op jit(solution)/shard_map/layer1/pallas_call | solution.py:48
  131.0 2.0 collective-permute-start.1
  133.5 2.5 collective-permute-done.9.refs_3_
  136.0 1.2 copy-done.25
  137.2 1.4 copy-done.9
  138.6 1.4 copy-done.26
  140.0 7.5 %back0.1 = (f32[1536,512]{1,0:T(8,128)}, bf16[1536,512]{1,0:T(8,128)(2,1)}) custom-call(s32[21]{0:T(128)S(1)} %concatenate.3.table_ref, bf16[1536,512]{1,0:T(8,128)(2,1)S(1)} %copy-done.9, bf16[1536,512]{1,0:T(8,128)(2,1)S(1)} %copy-done.26, bf16[4,512,512]{2,1,0:T(8,128)(2,1)} %copy-done.1, bf16[2,512,512]{2,1,0:T(8,128)(2,1)S(1)} %collective-permute-done.9.refs_3_, ...), custom_call_target="tpu_custom_call" | custom-call | flops 1 | bytes 1 | tf_op jit(solution)/shard_map/back0/pallas_call | solution.py:48
  147.5 1.4 copy-done.11
  149.0 7.6 %back1.1 = (f32[1536,512]{1,0:T(8,128)}, bf16[1536,512]{1,0:T(8,128)(2,1)}) custom-call(s32[21]{0:T(128)S(1)} %concatenate.3.table_ref, bf16[1536,512]{1,0:T(8,128)(2,1)S(1)} %copy-done.11, bf16[1536,512]{1,0:T(8,128)(2,1)S(1)} %collective-permute-done.8.refs_1_, bf16[4,512,512]{2,1,0:T(8,128)(2,1)} %copy-done.1, ...), custom_call_target="tpu_custom_call" | custom-call | flops 1 | bytes 1 | tf_op jit(solution)/shard_map/back1/pallas_call | solution.py:48
  156.5 11.5 %collective-permute-done.1.refs_2_ = bf16[1536,512]{1,0:T(8,128)(2,1)} collective-permute-done((bf16[1536,512]{1,0:T(8,128)(2,1)S(1)}, bf16[1536,512]{1,0:T(8,128)(2,1)}, u32[]{:S(2)}, u32[]{:S(2)}) %collective-permute-start.1) | collective-permute-done | bytes 1572896 | tf_op jit(solution)/shard_map/ppermute | solution.py:67
  168.1 6.9 %mix2.1.refs_2_.refs_8_.refs_10_ = bf16[1536,512]{1,0:T(8,128)(2,1)S(1)} custom-call(s32[21]{0:T(128)S(1)} %concatenate.3.table_ref, bf16[1536,1536]{1,0:T(8,128)(2,1)} %get-tuple-element.64.refs_0_.refs_3_, f32[1536,1]{1,0:T(8,128)S(1)} %copy-done.16, bf16[1536,512]{1,0:T(8,128)(2,1)} %collective-permute-done.1.refs_2_, ...), custom_call_target="tpu_custom_call" | custom-call | flops 1 | bytes 1 | tf_op jit(solution)/shard_map/mix2/pallas_call | solution.py:48
  175.1 3.4 collective-permute-done.11.refs_3_.refs_11_
  178.5 1.1 copy-done.39
  179.6 9.4 %layer2.1 = (bf16[3,1536,512]{2,1,0:T(8,128)(2,1)}, bf16[1536,512]{1,0:T(8,128)(2,1)S(1)}, f32[1,512]{1,0:T(1,128)S(1)}) custom-call(s32[21]{0:T(128)S(1)} %concatenate.3.table_ref, bf16[1536,512]{1,0:T(8,128)(2,1)S(1)} %copy-done.7, bf16[1536,512]{1,0:T(8,128)(2,1)S(1)} %collective-permute-done.refs_1_.refs_9_, ...), custom_call_target="tpu_custom_call", output_to_operand_aliasing={{0}: (8, {})} | custom-call | flops 1 | bytes 1 | tf_op jit(solution)/shard_map/layer2/pallas_call | solution.py:48
  189.2 1.8 collective-permute-start.16
  191.3 1.2 collective-permute-done.12.refs_1_
  192.5 7.5 %back2.1 = (f32[1536,512]{1,0:T(8,128)}, bf16[1536,256]{1,0:T(8,128)(2,1)}, bf16[1536,256]{1,0:T(8,128)(2,1)}) custom-call(s32[21]{0:T(128)S(1)} %concatenate.3.table_ref, bf16[1536,512]{1,0:T(8,128)(2,1)S(1)} %get-tuple-element.79.refs_0_.refs_4_.refs_14_, bf16[1536,512]{1,0:T(8,128)(2,1)S(1)} %collective-permute-done.12.refs_1_, ...), custom_call_target="tpu_custom_call" | custom-call | flops 1 | bytes 1 | tf_op jit(solution)/shard_map/back2/pallas_call | solution.py:48
  200.1 17.2 %weight.1 = (f32[2048,128]{1,0:T(8,128)S(1)}, f32[2048,128]{1,0:T(8,128)S(1)}, bf16[2048,128]{1,0:T(8,128)(2,1)S(1)}, bf16[2048,128]{1,0:T(8,128)(2,1)S(1)}, f32[1,512]{1,0:T(1,128)S(1)}) custom-call(s32[21]{0:T(128)S(1)} %concatenate.3.table_ref, bf16[1536,512]{1,0:T(8,128)(2,1)} %get-tuple-element.61.refs_2_.refs_0_, ...), custom_call_target="tpu_custom_call" | custom-call | flops 1 | bytes 1 | tf_op jit(solution)/shard_map/weight/pallas_call | solution.py:48
  217.3 1.8 collective-permute-start.18
  219.4 1.7 collective-permute-start.19
  221.2 5.5 %collective-permute-done.16.refs_1_ = bf16[1536,512]{1,0:T(8,128)(2,1)S(1)} collective-permute-done((bf16[1536,512]{1,0:T(8,128)(2,1)}, bf16[1536,512]{1,0:T(8,128)(2,1)S(1)}, u32[]{:S(2)}, u32[]{:S(2)}) %collective-permute-start.16) | collective-permute-done | bytes 1572896 | tf_op jit(solution)/shard_map/ppermute | solution.py:67
  226.7 8.0 %scatter0_0.1.refs_4_ = bf16[3,1536,512]{2,1,0:T(8,128)(2,1)} custom-call(s32[21]{0:T(128)S(1)} %concatenate.3.table_ref, f32[1536,512]{1,0:T(8,128)S(1)} %copy-done.13, bf16[1536,512]{1,0:T(8,128)(2,1)S(1)} %collective-permute-done.16.refs_1_, f32[1536,1]{1,0:T(8,128)S(1)} %copy-done.24, bf16[1536,1536]{1,0:T(8,128)(2,1)} %get-tuple-element.68.refs_0_.refs_3_, ...), custom_call_target="tpu_custom_call" | custom-call | flops 1 | bytes 1 | tf_op jit(solution)/shard_map/scatter0_0/pallas_call | solution.py:48
  234.6 8.0 %collective-permute-done.19.refs_3_ = f32[1,512]{1,0:T(1,128)S(1)} collective-permute-done((f32[1,512]{1,0:T(1,128)S(1)}, f32[1,512]{1,0:T(1,128)S(1)}, u32[]{:S(2)}, u32[]{:S(2)}) %collective-permute-start.19) | collective-permute-done | bytes 2080 | tf_op jit(solution)/shard_map/ppermute | solution.py:67
  242.6 1.2 copy-done.31
  243.9 2.0 pairs0.1
  245.9 1.9 collective-permute-start.21
  247.7 2.6 pairs1.1
  250.5 1.8 collective-permute-start.22
  252.3 1.5 collective-permute-start.14
  253.9 16.6 %collective-permute-done.22.refs_3_ = f32[1,512]{1,0:T(1,128)S(1)} collective-permute-done((f32[1,512]{1,0:T(1,128)S(1)}, f32[1,512]{1,0:T(1,128)S(1)}, u32[]{:S(2)}, u32[]{:S(2)}) %collective-permute-start.22) | collective-permute-done | bytes 2080 | tf_op jit(solution)/shard_map/ppermute | solution.py:67
  270.4 1.7 collective-permute-start.13
  272.8 2.7 collective-permute-start.23
  275.4 1.1 halve2_1.1
  276.9 2.6 collective-permute-start.24
  279.5 8.0 %scatter1_0.1.refs_4_ = bf16[3,1536,512]{2,1,0:T(8,128)(2,1)} custom-call(s32[21]{0:T(128)S(1)} %concatenate.3.table_ref, f32[1536,512]{1,0:T(8,128)S(1)} %copy-done.14, bf16[1536,512]{1,0:T(8,128)(2,1)S(1)} %collective-permute-done.15.refs_1_, f32[1536,1]{1,0:T(8,128)S(1)} %copy-done.22, ...), custom_call_target="tpu_custom_call", output_to_operand_aliasing={{}: (5, {})} | custom-call | flops 1 | bytes 1 | tf_op jit(solution)/shard_map/scatter1_0/pallas_call | solution.py:48
  287.5 9.6 %collective-permute-done.24.refs_3_ = f32[1,512]{1,0:T(1,128)S(1)} collective-permute-done((f32[1,512]{1,0:T(1,128)S(1)}, f32[1,512]{1,0:T(1,128)S(1)}, u32[]{:S(2)}, u32[]{:S(2)}) %collective-permute-start.24) | collective-permute-done | bytes 2080 | tf_op jit(solution)/shard_map/ppermute | solution.py:67
  297.8 2.3 copy-done
  300.1 0.9 copy-done.35
  301.1 0.8 part0.1
  302.1 2.3 part1.1
  304.4 1.4 collective-permute-start.27
  306.5 3.7 %collective-permute-done.27.refs_3_ = bf16[512,128]{1,0:T(8,128)(2,1)S(1)} collective-permute-done((bf16[512,128]{1,0:T(8,128)(2,1)S(1)}, bf16[512,128]{1,0:T(8,128)(2,1)S(1)}, u32[]{:S(2)}, u32[]{:S(2)}) %collective-permute-start.27) | collective-permute-done | bytes 131104 | tf_op jit(solution)/shard_map/ppermute | solution.py:67
  310.2 1.4 collective-permute-done.26.refs_2_
  311.6 3.2 adamw.1
  314.8 1.2 copy-done.27
  316.0 7.0 %scatter2_0.1.refs_5_ = bf16[3,1536,512]{2,1,0:T(8,128)(2,1)} custom-call(s32[21]{0:T(128)S(1)} %concatenate.3.table_ref, f32[1536,512]{1,0:T(8,128)S(1)} %copy-done.2, bf16[1536,256]{1,0:T(8,128)(2,1)S(1)} %collective-permute-done.14.refs_1_, f32[1536,1]{1,0:T(8,128)S(1)} %copy-done.16, ...), custom_call_target="tpu_custom_call", output_to_operand_aliasing={{}: (5, {})} | custom-call | flops 1 | bytes 1 | tf_op jit(solution)/shard_map/scatter2_0/pallas_call | solution.py:48
  323.1 4.8 %copy.34.refs_4_ = bf16[3,1536,512]{2,1,0:T(8,128)(2,1)} copy(bf16[3,1536,512]{2,1,0:T(8,128)(2,1)} %scatter2_0.1.refs_5_) | data formatting | bytes 9437184
  327.9 7.0 %scatter2_1.1 = bf16[3,1536,512]{2,1,0:T(8,128)(2,1)} custom-call(s32[21]{0:T(128)S(1)} %concatenate.3.table_ref, f32[1536,512]{1,0:T(8,128)S(1)} %copy-done.2, bf16[1536,256]{1,0:T(8,128)(2,1)S(1)} %collective-permute-done.13.refs_1_, f32[1536,1]{1,0:T(8,128)S(1)} %copy-done.16, ...), custom_call_target="tpu_custom_call", output_to_operand_aliasing={{}: (5, {})} | custom-call | flops 1 | bytes 1 | tf_op jit(solution)/shard_map/scatter2_1/pallas_call | solution.py:48
  (115 shorter events, 5.8 us)
Async XLA Ops:
  7.2 2.2 copy-start.42
  7.2 2.3 copy-start.41
  7.2 91.6 %all-gather.2.cloned.1.call-start = ((), (), s32[]{:S(2)}) async-start(), calls=%async_computation | async-start | bytes 4718592 | tf_op jit(solution)/shard_map/all_gather | solution.py:516
  12.3 71.4 %collective-permute-start.4 = (bf16[1536,512]{1,0:T(8,128)(2,1)S(1)}, bf16[1536,512]{1,0:T(8,128)(2,1)}, u32[]{:S(2)}, u32[]{:S(2)}) collective-permute-start(bf16[1536,512]{1,0:T(8,128)(2,1)S(1)} %pick0.1.refs_1_), channel_id=1, source_target_pairs={{0,2},{1,3},{2,0},{3,1},{4,6},{5,7},{6,4},{7,5},{8,10},{9,11},{10,... | collective-permute-start | bytes 4718600 | tf_op jit(solution)/shard_map/ppermute | solution.py:67
  19.5 2.9 copy-start.40
  19.5 71.9 %collective-permute-start.3 = (bf16[1536,512]{1,0:T(8,128)(2,1)}, bf16[1536,512]{1,0:T(8,128)(2,1)}, u32[]{:S(2)}, u32[]{:S(2)}) collective-permute-start(bf16[1536,512]{1,0:T(8,128)(2,1)} %pick1.1.refs_1_), channel_id=1, source_target_pairs={{0,2},{1,3},{2,0},{3,1},{4,6},{5,7},{6,4},{7,5},{8,10},{9,11},{10,... | collective-permute-start | bytes 4718600 | tf_op jit(solution)/shard_map/ppermute | solution.py:67
  22.4 21.6 %copy-start.17 = (bf16[1536,512]{1,0:T(8,128)(2,1)}, bf16[1536,512]{1,0:T(8,128)(2,1)S(1)}, u32[]{:S(2)}) copy-start(bf16[1536,512]{1,0:T(8,128)(2,1)S(1)} %pick2.1.refs_2_) | copy-start | bytes 4718596
  44.0 39.8 %copy-start.23 = (f32[1536,1]{1,0:T(8,128)}, f32[1536,1]{1,0:T(8,128)S(1)}, u32[]{:S(2)}) copy-start(f32[1536,1]{1,0:T(8,128)S(1)} %get-tuple-element.69.refs_1_.refs_2_) | copy-start | bytes 18436
  44.0 65.5 %collective-permute-start.6 = (bf16[1536,512]{1,0:T(8,128)(2,1)}, bf16[1536,512]{1,0:T(8,128)(2,1)}, u32[]{:S(2)}, u32[]{:S(2)}) collective-permute-start(bf16[1536,512]{1,0:T(8,128)(2,1)} %get-tuple-element.61.refs_2_.refs_0_), channel_id=1, source_target_pairs={{0,1},{1,0},{2,3},{3,2},{4,5},{5,4},{6,7},{7,6},{8,9},{9,8},{10,11... | collective-permute-start | bytes 4718600 | tf_op jit(solution)/shard_map/ppermute | solution.py:67
  63.5 27.9 %copy-start.21 = (f32[1536,1]{1,0:T(8,128)}, f32[1536,1]{1,0:T(8,128)S(1)}, u32[]{:S(2)}) copy-start(f32[1536,1]{1,0:T(8,128)S(1)} %get-tuple-element.67.refs_1_.refs_2_) | copy-start | bytes 18436
  83.8 6.9 %copy-start.6 = (bf16[1536,512]{1,0:T(8,128)(2,1)}, bf16[1536,512]{1,0:T(8,128)(2,1)S(1)}, u32[]{:S(2)}) copy-start(bf16[1536,512]{1,0:T(8,128)(2,1)S(1)} %get-tuple-element.63.refs_3_.refs_0_.refs_8_) | copy-start | bytes 4718596
  90.7 7.6 %copy-start.3 = (bf16[1536,512]{1,0:T(8,128)(2,1)}, bf16[1536,512]{1,0:T(8,128)(2,1)S(1)}, u32[]{:S(2)}) copy-start(bf16[1536,512]{1,0:T(8,128)(2,1)S(1)} %mix0.1.refs_3_.refs_2_) | copy-start | bytes 4718596
  90.7 18.7 %collective-permute-start.7 = (bf16[1536,512]{1,0:T(8,128)(2,1)S(1)}, bf16[1536,512]{1,0:T(8,128)(2,1)}, u32[]{:S(2)}, u32[]{:S(2)}) collective-permute-start(bf16[1536,512]{1,0:T(8,128)(2,1)S(1)} %mix0.1.refs_3_.refs_2_), channel_id=1, source_target_pairs={{0,1},{1,0},{2,3},{3,2},{4,5},{5,4},{6,7},{7,6},{8,9},{9,8},{10,11... | collective-permute-start | bytes 4718600 | tf_op jit(solution)/shard_map/ppermute | solution.py:67
  91.3 28.3 %collective-permute-start.2 = (bf16[1536,512]{1,0:T(8,128)(2,1)}, bf16[1536,512]{1,0:T(8,128)(2,1)}, u32[]{:S(2)}, u32[]{:S(2)}) collective-permute-start(bf16[1536,512]{1,0:T(8,128)(2,1)} %get-tuple-element.62.refs_2_.refs_0_.refs_4_), channel_id=1, source_target_pairs={{0,1},{1,0},{2,3},{3,2},{4,5},{5,4},{6,7},{7,6},{8,9},{9,8},{10,11... | collective-permute-start | bytes 4718600 | tf_op jit(solution)/shard_map/ppermute | solution.py:67
  98.3 9.8 %copy-start.4 = (bf16[1536,512]{1,0:T(8,128)(2,1)}, bf16[1536,512]{1,0:T(8,128)(2,1)S(1)}, u32[]{:S(2)}) copy-start(bf16[1536,512]{1,0:T(8,128)(2,1)S(1)} %mix1.1.refs_1_.refs_2_.refs_6_) | copy-start | bytes 4718596
  98.3 11.1 %copy-start.36 = (f32[512]{0:T(512)S(1)}, f32[512]{0:T(512)}, u32[]{:S(2)}) copy-start(f32[512]{0:T(512)} %param.18) | copy-start | bytes 6148
  98.3 21.2 %collective-permute-start.5 = (bf16[1536,512]{1,0:T(8,128)(2,1)S(1)}, bf16[1536,512]{1,0:T(8,128)(2,1)}, u32[]{:S(2)}, u32[]{:S(2)}) collective-permute-start(bf16[1536,512]{1,0:T(8,128)(2,1)S(1)} %mix1.1.refs_1_.refs_2_.refs_6_), channel_id=1, source_target_pairs={{0,1},{1,0},{2,3},{3,2},{4,5},{5,4},{6,7},{7,6},{8,9},{9,8},{10,11... | collective-permute-start | bytes 4718600 | tf_op jit(solution)/shard_map/ppermute | solution.py:67
  108.1 1.4 copy-start.1
  119.5 16.5 %collective-permute-start.10 = (bf16[1536,512]{1,0:T(8,128)(2,1)S(1)}, bf16[1536,512]{1,0:T(8,128)(2,1)S(1)}, u32[]{:S(2)}, u32[]{:S(2)}) collective-permute-start(bf16[1536,512]{1,0:T(8,128)(2,1)S(1)} %get-tuple-element.73.refs_8_.refs_0_.refs_12_), channel_id=1, source_target_pairs={{0,1},{1,0},{2,3},{3,2},{4,5},{5,4},{6,7},{7,6},{8,9},{9,8},{10,11... | collective-permute-start | bytes 4718600 | tf_op jit(solution)/shard_map/ppermute | solution.py:67
  120.6 10.3 %copy-start.18 = (bf16[1536,512]{1,0:T(8,128)(2,1)S(1)}, bf16[1536,512]{1,0:T(8,128)(2,1)}, u32[]{:S(2)}) copy-start(bf16[1536,512]{1,0:T(8,128)(2,1)} %copy-done.17) | copy-start | bytes 4718596
  120.6 12.5 %copy-start.7 = (bf16[1536,512]{1,0:T(8,128)(2,1)S(1)}, bf16[1536,512]{1,0:T(8,128)(2,1)}, u32[]{:S(2)}) copy-start(bf16[1536,512]{1,0:T(8,128)(2,1)} %copy-done.6) | copy-start | bytes 4718596
  130.9 5.1 %copy-start.10 = (bf16[1536,512]{1,0:T(8,128)(2,1)}, bf16[1536,512]{1,0:T(8,128)(2,1)S(1)}, u32[]{:S(2)}) copy-start(bf16[1536,512]{1,0:T(8,128)(2,1)S(1)} %get-tuple-element.74.refs_4_.refs_0_.refs_13_) | copy-start | bytes 4718596
  130.9 16.7 %collective-permute-start.8 = (bf16[1536,512]{1,0:T(8,128)(2,1)S(1)}, bf16[1536,512]{1,0:T(8,128)(2,1)S(1)}, u32[]{:S(2)}, u32[]{:S(2)}) collective-permute-start(bf16[1536,512]{1,0:T(8,128)(2,1)S(1)} %get-tuple-element.74.refs_4_.refs_0_.refs_13_), channel_id=1, source_target_pairs={{0,1},{1,0},{2,3},{3,2},{4,5},{5,4},{6,7},{7,6},{8,9},{9,8},{10,11... | collective-permute-start | bytes 4718600 | tf_op jit(solution)/shard_map/ppermute | solution.py:67
  131.0 37.1 %collective-permute-start.1 = (bf16[1536,512]{1,0:T(8,128)(2,1)S(1)}, bf16[1536,512]{1,0:T(8,128)(2,1)}, u32[]{:S(2)}, u32[]{:S(2)}) collective-permute-start(bf16[1536,512]{1,0:T(8,128)(2,1)S(1)} %copy-done.18), channel_id=1, source_target_pairs={{0,2},{1,3},{2,0},{3,1},{4,6},{5,7},{6,4},{7,5},{8,10},{9,11},{10,... | collective-permute-start | bytes 4718600 | tf_op jit(solution)/shard_map/ppermute | solution.py:67
  133.0 3.0 collective-permute-start.9
  133.1 42.0 %collective-permute-start = (bf16[1536,512]{1,0:T(8,128)(2,1)S(1)}, bf16[1536,512]{1,0:T(8,128)(2,1)S(1)}, u32[]{:S(2)}, u32[]{:S(2)}) collective-permute-start(bf16[1536,512]{1,0:T(8,128)(2,1)S(1)} %copy-done.7), channel_id=1, source_target_pairs={{0,1},{1,0},{2,3},{3,2},{4,5},{5,4},{6,7},{7,6},{8,9},{9,8},{10,11... | collective-permute-start | bytes 4718600 | tf_op jit(solution)/shard_map/ppermute | solution.py:67
  137.2 1.4 copy-start.9
  138.6 1.4 copy-start.26
  147.5 1.4 copy-start.11
  148.9 19.1 %copy-start.16 = (f32[1536,1]{1,0:T(8,128)S(1)}, f32[1536,1]{1,0:T(8,128)}, u32[]{:S(2)}) copy-start(f32[1536,1]{1,0:T(8,128)} %copy-done.15) | copy-start | bytes 18436
  175.0 3.5 %copy-start.5 = (bf16[1536,512]{1,0:T(8,128)(2,1)}, bf16[1536,512]{1,0:T(8,128)(2,1)S(1)}, u32[]{:S(2)}) copy-start(bf16[1536,512]{1,0:T(8,128)(2,1)S(1)} %mix2.1.refs_2_.refs_8_.refs_10_) | copy-start | bytes 4718596
  175.0 3.5 %collective-permute-start.11 = (bf16[1536,512]{1,0:T(8,128)(2,1)S(1)}, bf16[1536,512]{1,0:T(8,128)(2,1)S(1)}, u32[]{:S(2)}, u32[]{:S(2)}) collective-permute-start(bf16[1536,512]{1,0:T(8,128)(2,1)S(1)} %mix2.1.refs_2_.refs_8_.refs_10_), channel_id=1, source_target_pairs={{0,1},{1,0},{2,3},{3,2},{4,5},{5,4},{6,7},{7,6},{8,9},{9,8},{10,11... | collective-permute-start | bytes 4718600 | tf_op jit(solution)/shard_map/ppermute | solution.py:67
  175.1 13.9 %copy-start.19 = (bf16[1536,512]{1,0:T(8,128)(2,1)}, bf16[1536,512]{1,0:T(8,128)(2,1)S(1)}, u32[]{:S(2)}) copy-start(bf16[1536,512]{1,0:T(8,128)(2,1)S(1)} %collective-permute-done.refs_1_.refs_9_) | copy-start | bytes 4718596
  189.0 11.0 %copy-start.12 = (bf16[1536,512]{1,0:T(8,128)(2,1)}, bf16[1536,512]{1,0:T(8,128)(2,1)S(1)}, u32[]{:S(2)}) copy-start(bf16[1536,512]{1,0:T(8,128)(2,1)S(1)} %get-tuple-element.79.refs_0_.refs_4_.refs_14_) | copy-start | bytes 4718596
  189.0 3.5 %collective-permute-start.12 = (bf16[1536,512]{1,0:T(8,128)(2,1)S(1)}, bf16[1536,512]{1,0:T(8,128)(2,1)S(1)}, u32[]{:S(2)}, u32[]{:S(2)}) collective-permute-start(bf16[1536,512]{1,0:T(8,128)(2,1)S(1)} %get-tuple-element.79.refs_0_.refs_4_.refs_14_), channel_id=1, source_target_pairs={{0,1},{1,0},{2,3},{3,2},{4,5},{5,4},{6,7},{7,6},{8,9},{9,8},{10,11... | collective-permute-start | bytes 4718600 | tf_op jit(solution)/shard_map/ppermute | solution.py:67
  189.2 37.4 %collective-permute-start.16 = (bf16[1536,512]{1,0:T(8,128)(2,1)}, bf16[1536,512]{1,0:T(8,128)(2,1)S(1)}, u32[]{:S(2)}, u32[]{:S(2)}) collective-permute-start(bf16[1536,512]{1,0:T(8,128)(2,1)} %get-tuple-element.84), channel_id=1, source_target_pairs={{0,2},{1,3},{2,0},{3,1},{4,6},{5,7},{6,4},{7,5},{8,10},{9,11},{10,... | collective-permute-start | bytes 4718600 | tf_op jit(solution)/shard_map/ppermute | solution.py:67
  191.0 85.9 %collective-permute-start.15 = (bf16[1536,512]{1,0:T(8,128)(2,1)}, bf16[1536,512]{1,0:T(8,128)(2,1)S(1)}, u32[]{:S(2)}, u32[]{:S(2)}) collective-permute-start(bf16[1536,512]{1,0:T(8,128)(2,1)} %get-tuple-element.83), channel_id=1, source_target_pairs={{0,2},{1,3},{2,0},{3,1},{4,6},{5,7},{6,4},{7,5},{8,10},{9,11},{10,... | collective-permute-start | bytes 4718600 | tf_op jit(solution)/shard_map/ppermute | solution.py:67
  200.0 26.6 %copy-start.13 = (f32[1536,512]{1,0:T(8,128)S(1)}, f32[1536,512]{1,0:T(8,128)}, u32[]{:S(2)}) copy-start(f32[1536,512]{1,0:T(8,128)} %get-tuple-element.75.refs_4_.refs_0_) | copy-start | bytes 9437188
  200.1 26.6 %copy-start.24 = (f32[1536,1]{1,0:T(8,128)S(1)}, f32[1536,1]{1,0:T(8,128)}, u32[]{:S(2)}) copy-start(f32[1536,1]{1,0:T(8,128)} %copy-done.23) | copy-start | bytes 18436
  217.3 17.3 %copy-start.30 = (f32[2048,128]{1,0:T(8,128)}, f32[2048,128]{1,0:T(8,128)S(1)}, u32[]{:S(2)}) copy-start(f32[2048,128]{1,0:T(8,128)S(1)} %get-tuple-element.91.refs_0_) | copy-start | bytes 3145732
  217.3 25.3 %collective-permute-start.18 = (bf16[2048,128]{1,0:T(8,128)(2,1)S(1)}, bf16[2048,128]{1,0:T(8,128)(2,1)S(1)}, u32[]{:S(2)}, u32[]{:S(2)}) collective-permute-start(bf16[2048,128]{1,0:T(8,128)(2,1)S(1)} %get-tuple-element.92), channel_id=1, source_target_pairs={{0,4},{4,0},{8,12},{12,8},{16,20},{20,16},{24,28},{28,24},{1,5},{5... | collective-permute-start | bytes 1572872 | tf_op jit(solution)/shard_map/ppermute | solution.py:67
  219.1 28.6 %collective-permute-start.17 = (bf16[2048,128]{1,0:T(8,128)(2,1)S(1)}, bf16[2048,128]{1,0:T(8,128)(2,1)S(1)}, u32[]{:S(2)}, u32[]{:S(2)}) collective-permute-start(bf16[2048,128]{1,0:T(8,128)(2,1)S(1)} %get-tuple-element.90), channel_id=1, source_target_pairs={{0,4},{4,0},{8,12},{12,8},{16,20},{20,16},{24,28},{28,24},{1,5},{5... | collective-permute-start | bytes 1572872 | tf_op jit(solution)/shard_map/ppermute | solution.py:67
  219.4 23.2 %collective-permute-start.19 = (f32[1,512]{1,0:T(1,128)S(1)}, f32[1,512]{1,0:T(1,128)S(1)}, u32[]{:S(2)}, u32[]{:S(2)}) collective-permute-start(f32[1,512]{1,0:T(1,128)S(1)} %get-tuple-element.88.refs_4_.refs_2_), channel_id=1, source_target_pairs={{0,4},{4,0},{8,12},{12,8},{16,20},{20,16},{24,28},{28,24},{1,5},{5... | collective-permute-start | bytes 6152 | tf_op jit(solution)/shard_map/ppermute | solution.py:67
  245.9 26.2 %collective-permute-start.21 = (bf16[2,1024,128]{2,1,0:T(8,128)(2,1)S(1)}, bf16[2,1024,128]{2,1,0:T(8,128)(2,1)S(1)}, u32[]{:S(2)}, u32[]{:S(2)}) collective-permute-start(bf16[2,1024,128]{2,1,0:T(8,128)(2,1)S(1)} %get-tuple-element.93.refs_4_), channel_id=1, source_target_pairs={{0,8},{4,12},{8,0},{12,4},{16,24},{20,28},{24,16},{28,20},{1,9},{5... | collective-permute-start | bytes 1572872 | tf_op jit(solution)/shard_map/ppermute | solution.py:67
  250.3 25.1 %collective-permute-start.20 = (bf16[2,1024,128]{2,1,0:T(8,128)(2,1)S(1)}, bf16[2,1024,128]{2,1,0:T(8,128)(2,1)S(1)}, u32[]{:S(2)}, u32[]{:S(2)}) collective-permute-start(bf16[2,1024,128]{2,1,0:T(8,128)(2,1)S(1)} %get-tuple-element.95.refs_4_), channel_id=1, source_target_pairs={{0,8},{4,12},{8,0},{12,4},{16,24},{20,28},{24,16},{28,20},{1,9},{5... | collective-permute-start | bytes 1572872 | tf_op jit(solution)/shard_map/ppermute | solution.py:67
  250.5 19.9 %collective-permute-start.22 = (f32[1,512]{1,0:T(1,128)S(1)}, f32[1,512]{1,0:T(1,128)S(1)}, u32[]{:S(2)}, u32[]{:S(2)}) collective-permute-start(f32[1,512]{1,0:T(1,128)S(1)} %get-tuple-element.97.refs_2_), channel_id=1, source_target_pairs={{0,8},{4,12},{8,0},{12,4},{16,24},{20,28},{24,16},{28,20},{1,9},{5... | collective-permute-start | bytes 6152 | tf_op jit(solution)/shard_map/ppermute | solution.py:67
  252.3 62.5 %collective-permute-start.14 = (bf16[1536,256]{1,0:T(8,128)(2,1)}, bf16[1536,256]{1,0:T(8,128)(2,1)S(1)}, u32[]{:S(2)}, u32[]{:S(2)}) collective-permute-start(bf16[1536,256]{1,0:T(8,128)(2,1)} %get-tuple-element.82), channel_id=1, source_target_pairs={{0,2},{1,3},{2,0},{3,1},{4,6},{5,7},{6,4},{7,5},{8,10},{9,11},{10,... | collective-permute-start | bytes 2359304 | tf_op jit(solution)/shard_map/ppermute | solution.py:67
  270.4 57.5 %collective-permute-start.13 = (bf16[1536,256]{1,0:T(8,128)(2,1)}, bf16[1536,256]{1,0:T(8,128)(2,1)S(1)}, u32[]{:S(2)}, u32[]{:S(2)}) collective-permute-start(bf16[1536,256]{1,0:T(8,128)(2,1)} %get-tuple-element.81), channel_id=1, source_target_pairs={{0,2},{1,3},{2,0},{3,1},{4,6},{5,7},{6,4},{7,5},{8,10},{9,11},{10,... | collective-permute-start | bytes 2359304 | tf_op jit(solution)/shard_map/ppermute | solution.py:67
  272.1 7.4 %copy-start.14 = (f32[1536,512]{1,0:T(8,128)S(1)}, f32[1536,512]{1,0:T(8,128)}, u32[]{:S(2)}) copy-start(f32[1536,512]{1,0:T(8,128)} %get-tuple-element.76.refs_3_.refs_0_) | copy-start | bytes 9437188
  272.1 7.4 %copy-start.22 = (f32[1536,1]{1,0:T(8,128)S(1)}, f32[1536,1]{1,0:T(8,128)}, u32[]{:S(2)}) copy-start(f32[1536,1]{1,0:T(8,128)} %copy-done.21) | copy-start | bytes 18436
  272.8 24.3 %collective-permute-start.23 = (bf16[1,1024,128]{2,1,0:T(8,128)(2,1)S(1)}, bf16[1,1024,128]{2,1,0:T(8,128)(2,1)S(1)}, u32[]{:S(2)}, u32[]{:S(2)}) collective-permute-start(bf16[1,1024,128]{2,1,0:T(8,128)(2,1)S(1)} %get-tuple-element.98.refs_4_), channel_id=1, source_target_pairs={{0,16},{4,20},{8,24},{12,28},{16,0},{20,4},{24,8},{28,12},{1,17},{... | collective-permute-start | bytes 786440 | tf_op jit(solution)/shard_map/ppermute | solution.py:67
  276.6 10.9 %copy-start.32 = (f32[1,1024,128]{2,1,0:T(8,128)}, f32[1,1024,128]{2,1,0:T(8,128)S(1)}, u32[]{:S(2)}) copy-start(f32[1,1024,128]{2,1,0:T(8,128)S(1)} %get-tuple-element.103.refs_0_) | copy-start | bytes 1572868
  276.6 25.4 %collective-permute-start.25 = (bf16[1,1024,128]{2,1,0:T(8,128)(2,1)S(1)}, bf16[1,1024,128]{2,1,0:T(8,128)(2,1)}, u32[]{:S(2)}, u32[]{:S(2)}) collective-permute-start(bf16[1,1024,128]{2,1,0:T(8,128)(2,1)S(1)} %get-tuple-element.99.refs_5_), channel_id=1, source_target_pairs={{0,16},{4,20},{8,24},{12,28},{16,0},{20,4},{24,8},{28,12},{1,17},{... | collective-permute-start | bytes 786440 | tf_op jit(solution)/shard_map/ppermute | solution.py:67
  276.9 20.2 %collective-permute-start.24 = (f32[1,512]{1,0:T(1,128)S(1)}, f32[1,512]{1,0:T(1,128)S(1)}, u32[]{:S(2)}, u32[]{:S(2)}) collective-permute-start(f32[1,512]{1,0:T(1,128)S(1)} %get-tuple-element.101.refs_2_), channel_id=1, source_target_pairs={{0,16},{4,20},{8,24},{12,28},{16,0},{20,4},{24,8},{28,12},{1,17},{... | collective-permute-start | bytes 6152 | tf_op jit(solution)/shard_map/ppermute | solution.py:67
  297.8 2.3 copy-start
  301.1 10.5 %copy-start.20 = (f32[512,512]{1,0:T(8,128)S(1)}, f32[512,512]{1,0:T(8,128)}, u32[]{:S(2)}) copy-start(f32[512,512]{1,0:T(8,128)} %refs_5_.1) | copy-start | bytes 3145732
  301.1 10.5 %copy-start.28 = (f32[512,512]{1,0:T(8,128)S(1)}, f32[512,512]{1,0:T(8,128)}, u32[]{:S(2)}) copy-start(f32[512,512]{1,0:T(8,128)} %refs_6_.7) | copy-start | bytes 3145732
  301.1 10.5 %copy-start.29 = (f32[512,512]{1,0:T(8,128)S(1)}, f32[512,512]{1,0:T(8,128)}, u32[]{:S(2)}) copy-start(f32[512,512]{1,0:T(8,128)} %refs_7_.1) | copy-start | bytes 3145732
  301.1 10.5 %copy-start.37 = (f32[512]{0:T(512)S(1)}, f32[512]{0:T(512)}, u32[]{:S(2)}) copy-start(f32[512]{0:T(512)} %param.19) | copy-start | bytes 6148
  301.1 10.5 %copy-start.38 = (f32[512]{0:T(512)S(1)}, f32[512]{0:T(512)}, u32[]{:S(2)}) copy-start(f32[512]{0:T(512)} %param.20) | copy-start | bytes 6148
  304.4 5.8 %collective-permute-start.27 = (bf16[512,128]{1,0:T(8,128)(2,1)S(1)}, bf16[512,128]{1,0:T(8,128)(2,1)S(1)}, u32[]{:S(2)}, u32[]{:S(2)}) collective-permute-start(bf16[512,128]{1,0:T(8,128)(2,1)S(1)} %get-tuple-element.106.refs_11_), channel_id=1, source_target_pairs={{0,4},{4,0},{8,12},{12,8},{16,20},{20,16},{24,28},{28,24},{1,5},{5... | collective-permute-start | bytes 393224 | tf_op jit(solution)/shard_map/ppermute | solution.py:67
  305.9 5.7 %collective-permute-start.26 = (bf16[512,128]{1,0:T(8,128)(2,1)S(1)}, bf16[512,128]{1,0:T(8,128)(2,1)S(1)}, u32[]{:S(2)}, u32[]{:S(2)}) collective-permute-start(bf16[512,128]{1,0:T(8,128)(2,1)S(1)} %get-tuple-element.104.refs_4_), channel_id=1, source_target_pairs={{0,4},{4,0},{8,12},{12,8},{16,20},{20,16},{24,28},{28,24},{1,5},{5... | collective-permute-start | bytes 393224 | tf_op jit(solution)/shard_map/ppermute | solution.py:67
  311.6 3.2 copy-start.2
  314.8 1.2 copy-start.27
  (8 other events, 8.3 us)
Sparse Core Ops, SparseCore 0:
  10.7 76.0 all-gather.1

commit v2 on v1

v2 whole, which is shorter than its diff:
```python
import functools

import jax
import jax.numpy as jnp
from jax import lax
from jax.experimental import pallas as pl
from jax.experimental.pallas import tpu as pltpu
from jax.sharding import PartitionSpec as P

D = 2048
MB = 3
STEP = 10

BETA_ONE = 0.9
BETA_TWO = 0.95
EPSILON = 1e-08
DECAY = 0.1
RATE_WEIGHT = 0.06
RATE_BIAS = 0.6

LANES = 128
DIGIT_BITS = 5
DIGITS = 6
STRIP = 32
SUBLANES = 8
TILE = 256
WIDE = 512
VMEM_BYTES = 48 * 1024 * 1024

GROUP, COLUMN, LIMITS = 0, 1, 2
STARTS = LIMITS + MB

FRONT_ID, MIX_ID, BACK_ID, SUM_ID = 1, 2, 2 + MB, 2 + 2 * MB

F32, BF16 = jnp.float32, jnp.bfloat16


def launch(name, body, table, ins, outs, grid=(1,), after=(), alias=None, scratch=(), barrier=None):
    def spec(block, index):
        if block is None:
            return pl.BlockSpec(memory_space=pl.ANY)
        return pl.BlockSpec(block, lambda *a: index(*a[:-1]))

    unread = ([alias[0]] if alias else []) + [array for array in after if alias is None or array is not alias[0]]

    def kernel(table_ref, *refs):
        body(table_ref, *refs[: len(ins)], *refs[len(ins) + len(unread) :])

    call = functools.partial(
        pl.pallas_call,
        kernel,
        grid_spec=pltpu.PrefetchScalarGridSpec(
            num_scalar_prefetch=1,
            grid=grid,
            in_specs=[spec(block, index) for _, block, index in ins]
            + [pl.BlockSpec(memory_space=pl.ANY)] * len(unread),
            out_specs=[spec(block, index) for _, _, block, index in outs],
            scratch_shapes=list(scratch),
        ),
        out_shape=[jax.ShapeDtypeStruct(shape, kind) for shape, kind, _, _ in outs],
        input_output_aliases={1 + len(ins): alias[1]} if alias else {},
        compiler_params=pltpu.CompilerParams(
            vmem_limit_bytes=VMEM_BYTES, collective_id=barrier, has_side_effects=barrier is not None
        ),
        cost_estimate=pl.CostEstimate(flops=1, bytes_accessed=1, transcendentals=0),
        name=name,
    )
    operands = (table, *(array for array, _, _ in ins), *unread)
    if barrier == FRONT_ID:
        return call()(*operands)
    if barrier == SUM_ID:
        return call()(*operands)
    if barrier is not None and barrier >= BACK_ID:
        return call()(*operands)
    if barrier is not None:
        return call()(*operands)
    return call()(*operands)


def flip(values, axis, bit):
    size = lax.axis_size(axis)
    return lax.ppermute(values, axis, [(i, i ^ bit) for i in range(size)])


def partner(index, bit):
    return index + bit * (1 - 2 * ((index // bit) % 2))


def product(left, right):
    return jnp.dot(left, right, preferred_element_type=F32)


def product_back(left, right):
    return lax.dot_general(left, right, (((1,), (1,)), ((), ())), preferred_element_type=F32)


def product_rows(left, right):
    return lax.dot_general(left, right, (((0,), (0,)), ((), ())), preferred_element_type=F32)


def scaled(values, scale):
    return values * jnp.concatenate([scale] * (values.shape[1] // LANES), axis=1)


def put_rows(ref, first, rows):
    base = pl.multiple_of((first // SUBLANES) * SUBLANES, SUBLANES)
    offset = first - base
    spare = jnp.zeros((SUBLANES, rows.shape[1]), rows.dtype)
    moved = pltpu.roll(jnp.concatenate([rows, spare], axis=0), offset, 0)
    head = ref[pl.ds(base, SUBLANES), :]
    row_ids = lax.broadcasted_iota(jnp.int32, head.shape, 0)
    ref[pl.ds(base, SUBLANES), :] = jnp.where(row_ids < offset, head, moved[:SUBLANES])
    ref[pl.ds(pl.multiple_of(base + SUBLANES, SUBLANES), rows.shape[0]), :] = moved[SUBLANES:]


def take_rows(ref, first, count, largest):
    bit = 1 << (largest.bit_length() - 1)
    rows = ref[: count + 2 * bit, :]
    while bit:
        length = count + max(bit, SUBLANES)
        moved = rows[bit : bit + length] if bit >= SUBLANES else pltpu.roll(rows, length - bit, 0)
        chosen = (jnp.broadcast_to(first, (length, rows.shape[1])) & bit) != 0
        rows = jnp.where(chosen, moved, rows[:length])
        bit //= 2
    return rows[:count]


def pick_kernel(m, table_ref, source_ref, out_ref, semaphore):
    copy = pltpu.make_async_copy(source_ref.at[m], out_ref, semaphore)
    copy.start()
    copy.wait()


def pick(table, stacked, m, after=()):
    return launch(
        f"pick{m}", functools.partial(pick_kernel, m), table,
        [(stacked, None, None)], [(stacked.shape[1:], stacked.dtype, None, None)],
        after=after, scratch=[pltpu.SemaphoreType.DMA],
    )[0]


def count_tile(limit, first, neighbour_ref, matrix_ref, scale_ref, lanes):
    nodes = matrix_ref.shape[1]
    words = -(-(nodes // LANES) // DIGITS)
    entries = neighbour_ref[0, :, lanes]
    node_ids = first + lax.broadcasted_iota(jnp.int32, entries.shape, 1)
    valid = (entries < limit) & (node_ids < limit)
    low = entries & (LANES - 1)
    high = entries >> 7
    digits = []
    for word in range(words):
        inside = valid & (high >= word * DIGITS) & (high < (word + 1) * DIGITS)
        shift = jnp.where(inside, (high - word * DIGITS) * DIGIT_BITS, 0)
        digits.append(jnp.where(inside, jnp.left_shift(1, shift), 0))
    for strip in range(LANES // STRIP):
        row_ids = strip * STRIP + lax.broadcasted_iota(jnp.int32, (STRIP, LANES), 0)
        sums = [jnp.zeros((STRIP, LANES), jnp.int32) for _ in range(words)]
        for entry in range(entries.shape[0]):
            hit = row_ids == low[entry : entry + 1, :]
            for word in range(words):
                sums[word] = sums[word] + jnp.where(hit, digits[word][entry : entry + 1, :], 0)
        for block in range(nodes // LANES):
            word, digit = block // DIGITS, block % DIGITS
            count = jnp.right_shift(sums[word], digit * DIGIT_BITS) & ((1 << DIGIT_BITS) - 1)
            rows = slice(block * LANES + strip * STRIP, block * LANES + (strip + 1) * STRIP)
            matrix_ref[0, rows, lanes] = count.astype(F32).astype(BF16)
    rows = pl.ds(pl.multiple_of(first, LANES), LANES)
    square = matrix_ref[0, rows, lanes].astype(F32)
    on_diagonal = lax.broadcasted_iota(jnp.int32, square.shape, 0) == lax.broadcasted_iota(jnp.int32, square.shape, 1)
    matrix_ref[0, rows, lanes] = jnp.where(on_diagonal, 2.0 * square + 2.0, square).astype(BF16)
    degree = 1.0 + jnp.sum(valid.astype(F32), axis=0, keepdims=True)
    factor = (node_ids[:1] < limit).astype(F32) / degree
    scale_ref[0, lanes, :] = jnp.transpose(jnp.broadcast_to(factor, (LANES, LANES)))


def front_kernel(
    groups, total, table_ref, master_ref, neighbour_ref, feature_ref, matrix_ref, scale_ref, mixed_ref, slots_ref,
    block_ref, local_semaphore, line_send, line_receive, pair_send, pair_receive,
):
    batch, tile_id = pl.program_id(0), pl.program_id(1)
    tiles = pl.num_programs(1)
    step = batch * tiles + tile_id
    own = lax.axis_index("clus")
    place, side = own // 2, own % 2
    pairs = groups // 2
    other = partner(own, 1)

    def line_copy(direction, hop):
        origin = place - hop if direction == 0 else place + hop
        target = place + 1 if direction == 0 else place - 1
        slot = origin * 2 + side
        return pltpu.make_async_remote_copy(
            src_ref=block_ref if hop == 0 else slots_ref.at[slot],
            dst_ref=slots_ref.at[slot],
            send_sem=line_send.at[direction, hop],
            recv_sem=line_receive.at[direction, hop],
            device_id={"clus": target * 2 + side},
            device_id_type=pl.DeviceIdType.MESH,
        )

    def sends(direction, hop):
        if direction == 0:
            return (place - hop >= 0) & (place + 1 < pairs)
        return (place + hop < pairs) & (place - 1 >= 0)

    def arrives(direction, hop):
        return place - 1 - hop >= 0 if direction == 0 else place + 1 + hop < pairs

    def arrival(direction, hop):
        origin = place - 1 - hop if direction == 0 else place + 1 + hop
        slot = slots_ref.at[origin * 2 + side]
        return pltpu.make_async_remote_copy(
            src_ref=slot,
            dst_ref=slot,
            send_sem=line_send.at[direction, hop],
            recv_sem=line_receive.at[direction, hop],
            device_id={"clus": other},
            device_id_type=pl.DeviceIdType.MESH,
        )

    def pair_copy(direction, hop):
        origin = place - 1 - hop if direction == 0 else place + 1 + hop
        number = 0 if hop < 0 else 1 + 2 * hop + direction
        slot = own if hop < 0 else origin * 2 + side
        return pltpu.make_async_remote_copy(
            src_ref=block_ref if hop < 0 else slots_ref.at[slot],
            dst_ref=slots_ref.at[slot],
            send_sem=pair_send.at[number],
            recv_sem=pair_receive.at[number],
            device_id={"clus": other},
            device_id_type=pl.DeviceIdType.MESH,
        )

    def pair_arrival(direction, hop):
        origin = place - 1 - hop if direction == 0 else place + 1 + hop
        number = 0 if hop < 0 else 1 + 2 * hop + direction
        slot = slots_ref.at[other if hop < 0 else origin * 2 + 1 - side]
        return pltpu.make_async_remote_copy(
            src_ref=slot,
            dst_ref=slot,
            send_sem=pair_send.at[number],
            recv_sem=pair_receive.at[number],
            device_id={"clus": other},
            device_id_type=pl.DeviceIdType.MESH,
        )

    local_copy = pltpu.make_async_copy(block_ref, slots_ref.at[own], local_semaphore)
    hops = pairs - 1

    @pl.when(step == 0)
    def _():
        barrier = pltpu.get_barrier_semaphore()

        def greet(index):
            pl.semaphore_signal(barrier, inc=1, device_id={"clus": index}, device_id_type=pl.DeviceIdType.MESH)

        greet(other)

        @pl.when(place + 1 < pairs)
        def _():
            greet(own + 2)

        @pl.when(place - 1 >= 0)
        def _():
            greet(own - 2)

        pl.semaphore_wait(barrier, 1 + jnp.where(place + 1 < pairs, 1, 0) + jnp.where(place - 1 >= 0, 1, 0))
        block_ref[...] = master_ref[...].astype(BF16)
        local_copy.start()
        for direction in range(2):
            pl.when(sends(direction, 0))(line_copy(direction, 0).start)
        pair_copy(0, -1).start()

    limit = table_ref[LIMITS + batch]
    tile = mixed_ref.shape[1]
    for part in range(tile // LANES):
        first = tile_id * tile + part * LANES
        count_tile(limit, first, neighbour_ref, matrix_ref, scale_ref, slice(part * LANES, (part + 1) * LANES))
    mixed_ref[0] = scaled(product_rows(matrix_ref[0], feature_ref[0]), scale_ref[0]).astype(BF16)

    for hop in range(hops):
        when = min(total - 1, ((hop + 1) * total) // hops)

        @pl.when(step == when)
        def _(hop=hop):
            for direction in range(2):

                @pl.when(arrives(direction, hop))
                def _(direction=direction):
                    arrival(direction, hop).wait_recv()
                    pair_copy(direction, hop).start()

                if hop + 1 < hops:
                    pl.when(sends(direction, hop + 1))(line_copy(direction, hop + 1).start)

    @pl.when(step == total - 1)
    def _():
        local_copy.wait()
        pair_copy(0, -1).wait_send()
        pair_arrival(0, -1).wait_recv()
        for hop in range(hops):
            for direction in range(2):
                pl.when(sends(direction, hop))(line_copy(direction, hop).wait_send)

                @pl.when(arrives(direction, hop))
                def _(direction=direction, hop=hop):
                    pair_copy(direction, hop).wait_send()
                    pair_arrival(direction, hop).wait_recv()


def front(table, groups, master, neighbours, features, after=()):
    _, entries, nodes = neighbours.shape
    capacity, width = master.shape
    hops = groups // 2 - 1
    steps = MB * (nodes // TILE)
    return launch(
        "front", functools.partial(front_kernel, groups, steps), table,
        [
            (master, (capacity, width), lambda b, i: (0, 0)),
            (neighbours, (1, entries, TILE), lambda b, i: (b, 0, i)),
            (features, (1, nodes, width), lambda b, i: (b, 0, 0)),
        ],
        [
            ((MB, nodes, nodes), BF16, (1, nodes, TILE), lambda b, i: (b, 0, i)),
            ((MB, nodes, LANES), F32, (1, TILE, LANES), lambda b, i: (b, i, 0)),
            ((MB, nodes, width), BF16, (1, TILE, width), lambda b, i: (b, i, 0)),
            ((groups, capacity, width), BF16, None, None),
        ],
        grid=(MB, nodes // TILE), after=after, barrier=FRONT_ID,
        scratch=[
            pltpu.VMEM((capacity, width), BF16),
            pltpu.SemaphoreType.DMA,
            pltpu.SemaphoreType.DMA((2, hops)),
            pltpu.SemaphoreType.DMA((2, hops)),
            pltpu.SemaphoreType.DMA((1 + 2 * hops,)),
            pltpu.SemaphoreType.DMA((1 + 2 * hops,)),
        ],
    )


def greet_mate(mate):
    barrier = pltpu.get_barrier_semaphore()
    pl.semaphore_signal(barrier, inc=1, device_id={"col": mate}, device_id_type=pl.DeviceIdType.MESH)
    pl.semaphore_wait(barrier, 1)


def mix_kernel(
    m, steps, table_ref, matrix_ref, scale_ref, far_ref, here_ref, there_ref, here_mate_ref, there_mate_ref,
    buffer_ref, send, receive,
):
    step = pl.program_id(0)
    tile = there_ref.shape[0]
    mate = partner(lax.axis_index("col"), 1)

    def copy(number):
        rows = pl.ds((number - 1) * tile, tile)
        return pltpu.make_async_remote_copy(
            src_ref=here_ref.at[m] if number == 0 else buffer_ref.at[rows],
            dst_ref=here_mate_ref if number == 0 else there_mate_ref.at[rows],
            send_sem=send.at[number],
            recv_sem=receive.at[number],
            device_id={"col": mate},
            device_id_type=pl.DeviceIdType.MESH,
        )

    @pl.when(step == 0)
    def _():
        greet_mate(mate)
        copy(0).start()

    result = scaled(product_rows(matrix_ref[0], far_ref[...]), scale_ref[0]).astype(BF16)
    there_ref[...] = result
    for number in range(1, steps + 1):

        @pl.when(step == number - 1)
        def _(number=number):
            buffer_ref[(number - 1) * tile : number * tile, :] = result
            copy(number).start()

    @pl.when(step == steps - 1)
    def _():
        for number in range(steps + 1):
            copy(number).wait()


def mix(table, m, matrix, scale, far, here, after=()):
    nodes, width = far.shape
    steps = nodes // WIDE
    shape = (nodes, width)
    return launch(
        f"mix{m}", functools.partial(mix_kernel, m, steps), table,
        [
            (matrix, (1, nodes, WIDE), lambda i: (m, 0, i)),
            (scale, (1, WIDE, LANES), lambda i: (m, i, 0)),
            (far, shape, lambda i: (0, 0)),
            (here, None, None),
        ],
        [
            (shape, BF16, (WIDE, width), lambda i: (i, 0)),
            (shape, BF16, None, None),
            (shape, BF16, None, None),
        ],
        grid=(steps,), after=after, barrier=MIX_ID + m,
        scratch=[
            pltpu.VMEM(shape, BF16),
            pltpu.SemaphoreType.DMA((steps + 1,)),
            pltpu.SemaphoreType.DMA((steps + 1,)),
        ],
    )


def place_kernel(groups, table_ref, slots_ref, weight_ref, mate_ref, rows_ref):
    owner = pl.program_id(0)

    @pl.when(owner == 0)
    def _():
        rows_ref[...] = jnp.zeros_like(rows_ref)

    put_rows(rows_ref, table_ref[STARTS + owner], slots_ref[0].astype(F32))

    @pl.when(owner == groups - 1)
    def _():
        width = weight_ref.shape[2]
        for block in range(weight_ref.shape[0]):
            source = pl.multiple_of((table_ref[COLUMN] ^ block) * width, width)
            rows = rows_ref[pl.ds(source, width), :].astype(BF16)
            weight_ref[block] = rows
            if block % 2:
                mate_ref[block // 2] = rows


def place(table, slots, after=()):
    groups, capacity, width = slots.shape
    blocks = D // width
    return launch(
        "place", functools.partial(place_kernel, groups), table,
        [(slots, (1, capacity, width), lambda i: (i, 0, 0))],
        [
            ((blocks, width, width), BF16, (blocks, width, width), lambda i: (0, 0, 0)),
            ((blocks // 2, width, width), BF16, (blocks // 2, width, width), lambda i: (0, 0, 0)),
        ],
        grid=(groups,), after=after, scratch=[pltpu.VMEM((D + capacity + SUBLANES, width), F32)],
    )


def layer_kernel(m, table_ref, *refs):
    mixed_refs, (weight_ref, bias_ref, grad_ref, out_ref, pre_ref, sum_ref) = refs[:4], refs[4:]
    tile = out_ref.shape[1]
    preact = bias_ref[...]
    for block in range(4):
        mixed = mixed_refs[block][0] if block == 0 else mixed_refs[block][...]
        preact = preact + product(mixed, weight_ref[block])
    first_row = pl.program_id(0) * tile
    row_ids = first_row + lax.broadcasted_iota(jnp.int32, preact.shape, 0)
    live = row_ids < table_ref[LIMITS + m]
    gate = jax.nn.sigmoid(preact)
    out_ref[0] = jnp.where(live, preact * gate, 0.0).astype(BF16)
    slope = gate * (1.0 + preact * (1.0 - gate))
    grad_pre = jnp.where(live, grad_ref[0].astype(F32) * slope, 0.0).astype(BF16)
    pre_ref[...] = grad_pre

    @pl.when(pl.program_id(0) == 0)
    def _():
        sum_ref[...] = jnp.zeros_like(sum_ref)

    sum_ref[...] += jnp.sum(grad_pre.astype(F32), axis=0, keepdims=True)


def layer(table, m, here, mixed, weight, bias, out_grad, outputs, after=()):
    _, nodes, width = here.shape
    return launch(
        f"layer{m}", functools.partial(layer_kernel, m), table,
        [(here, (1, TILE, width), lambda i: (m, i, 0))]
        + [(part, (TILE, width), lambda i: (i, 0)) for part in mixed]
        + [
            (weight, weight.shape, lambda i: (0, 0, 0)),
            (bias, (1, width), lambda i: (0, 0)),
            (out_grad, (1, TILE, width), lambda i: (m, i, 0)),
        ],
        [
            ((MB, nodes, width), BF16, (1, TILE, width), lambda i: (m, i, 0)),
            ((nodes, width), BF16, (TILE, width), lambda i: (i, 0)),
            ((1, width), F32, (1, width), lambda i: (0, 0)),
        ],
        grid=(nodes // TILE,), after=after, alias=None if outputs is None else (outputs, 0),
    )


def back_kernel(chunks, table_ref, here_hbm, for_mate_hbm, here_ref, weight_ref, *refs):
    own_ref, away_refs = refs[0], refs[1 : 1 + chunks]
    mate_ref, mate_weight_ref, own_total, away_total, send, receive = refs[1 + chunks :]
    half, step = pl.program_id(0), pl.program_id(1)
    tile = here_ref.shape[0]
    mate = partner(lax.axis_index("col"), 1)
    rows = pl.ds(pl.multiple_of(step * tile, tile), tile)

    def copy(number):
        return pltpu.make_async_remote_copy(
            src_ref=(here_hbm, for_mate_hbm)[number],
            dst_ref=(mate_ref, mate_weight_ref)[number],
            send_sem=send.at[number],
            recv_sem=receive.at[number],
            device_id={"col": mate},
            device_id_type=pl.DeviceIdType.MESH,
        )

    @pl.when((half == 0) & (step == 0))
    def _():
        greet_mate(mate)
        copy(1).start()
        copy(0).start()

    @pl.when(half == 0)
    def _():
        here = here_ref[...]
        away_total[rows, :] = product_back(here, weight_ref[2])
        own_total[rows, :] = product_back(here, weight_ref[0])

    @pl.when((half == 1) & (step == 0))
    def _():
        copy(1).wait()
        copy(0).wait()

    @pl.when(half == 1)
    def _():
        mate_rows = mate_ref[rows, :]
        away = (away_total[rows, :] + product_back(mate_rows, mate_weight_ref[1])).astype(BF16)
        width = away.shape[1] // chunks
        for chunk in range(chunks):
            away_refs[chunk][...] = away[:, chunk * width : (chunk + 1) * width]
        own_ref[...] = own_total[rows, :] + product_back(mate_rows, mate_weight_ref[0])


def back(table, m, here, weight, for_mate, chunks, after=()):
    nodes, width = here.shape
    step = width // chunks
    down = lambda h, i: (i * h, 0)
    return launch(
        f"back{m}", functools.partial(back_kernel, chunks), table,
        [
            (here, None, None),
            (for_mate, None, None),
            (here, (WIDE, width), lambda h, i: (i * (1 - h) + h * (nodes // WIDE - 1), 0)),
            (weight, weight.shape, lambda h, i: (0, 0, 0)),
        ],
        [((nodes, width), F32, (WIDE, width), down)]
        + [((nodes, step), BF16, (WIDE, step), down) for _ in range(chunks)],
        grid=(2, nodes // WIDE), after=after, barrier=BACK_ID + m,
        scratch=[
            pltpu.VMEM((nodes, width), BF16),
            pltpu.VMEM(for_mate.shape, BF16),
            pltpu.VMEM((nodes, width), F32),
            pltpu.VMEM((nodes, width), F32),
            pltpu.SemaphoreType.DMA((2,)),
            pltpu.SemaphoreType.DMA((2,)),
        ],
    )


def scatter_kernel(table_ref, own_ref, got_ref, scale_ref, matrix_ref, out_ref, sum_ref):
    @pl.when(pl.program_id(0) == 0)
    def _():
        grad_mixed = (own_ref[...] + got_ref[...].astype(F32)).astype(BF16)
        sum_ref[...] = scaled(grad_mixed.astype(F32), scale_ref[0]).astype(BF16)

    out_ref[0] = product(matrix_ref[0], sum_ref[...]).astype(BF16)


def scatter(table, m, chunk, own, got, scale, matrix, grads, after=()):
    nodes, width = own.shape
    step = got.shape[1]
    return launch(
        f"scatter{m}_{chunk}", scatter_kernel, table,
        [
            (own, (nodes, step), lambda i: (0, chunk)),
            (got, (nodes, step), lambda i: (0, 0)),
            (scale, (1, nodes, LANES), lambda i: (m, 0, 0)),
            (matrix, (1, WIDE, nodes), lambda i: (m, i, 0)),
        ],
        [((MB, nodes, width), BF16, (1, WIDE, step), lambda i: (m, i, chunk))],
        grid=(nodes // WIDE,), after=after, alias=None if grads is None else (grads, 0),
        scratch=[pltpu.VMEM((nodes, step), BF16)],
    )[0]


def weight_kernel(parts, table_ref, *refs):
    blocks = 4
    mixed_refs, pre_refs = refs[: MB * blocks], refs[MB * blocks : MB * blocks + MB]
    bias_refs = refs[MB * blocks + MB : MB * blocks + 2 * MB]
    keep_refs, sent_refs = refs[MB * blocks + 2 * MB :][:2], refs[MB * blocks + 2 * MB + 2 : -2]
    bias_out_ref, total_ref = refs[-2:]
    step = pl.program_id(0)

    for m in range(MB):

        @pl.when(step // parts == m)
        def _(m=m):
            for block in range(blocks):
                source = mixed_refs[m * blocks + block]
                term = product_rows(source[0] if block == 0 else source[...], pre_refs[m][...])
                if m == 0:
                    term = jnp.where(step == 0, term, total_ref[block] + term)
                else:
                    term = total_ref[block] + term
                total_ref[block] = term

    @pl.when(step == parts * MB - 1)
    def _():
        bias_out_ref[...] = sum(ref[...] for ref in bias_refs)
        width = total_ref.shape[1]
        quarter = width // 4
        upper = (table_ref[GROUP] & 1) == 1
        for block in range(blocks):
            rows = pl.ds(pl.multiple_of((table_ref[COLUMN] ^ block) * width, width), width)
            for chunk in range(2):
                low = total_ref[block, :, chunk * quarter : (chunk + 1) * quarter]
                high = total_ref[block, :, (2 + chunk) * quarter : (3 + chunk) * quarter]
                keep_refs[chunk][rows, :] = jnp.where(upper, high, low)
                sent_refs[chunk][rows, :] = jnp.where(upper, low, high).astype(BF16)


def weight_gradient(table, here, mixed, pres, biases, after=()):
    nodes, width = pres[0].shape
    parts = 2
    rows, quarter = nodes // parts, width // 4

    def turn(m):
        return lambda i: (jnp.clip(i - m * parts, 0, parts - 1), 0)

    whole = lambda i: (0, 0)
    ins = []
    for m in range(MB):
        ins.append((here, (1, rows, width), lambda i, m=m: (m, *turn(m)(i))))
        ins += [(part, (rows, width), turn(m)) for part in mixed[m]]
    return launch(
        "weight", functools.partial(weight_kernel, parts), table,
        ins
        + [(pres[m], (rows, width), turn(m)) for m in range(MB)]
        + [(bias, (1, width), whole) for bias in biases],
        [((D, quarter), F32, (D, quarter), whole)] * 2
        + [((D, quarter), BF16, (D, quarter), whole)] * 2
        + [((1, width), F32, (1, width), whole)],
        grid=(parts * MB,), after=after, scratch=[pltpu.VMEM((4, width, width), F32)],
    )


def sum_kernel(groups, capacity, table_ref, *refs):
    keep_refs, sent_refs, bias_ref = refs[0:2], refs[2:4], refs[4]
    own_refs, got_refs, bias_out_ref = refs[5:7], refs[7:9], refs[9]
    *total_refs, land_ref, bias_land_ref = refs[10:14]
    levels = refs[14:]
    depth = groups.bit_length() - 2
    held_refs, out_refs, in_refs = levels[:depth], levels[depth : 2 * depth], levels[2 * depth : 3 * depth]
    end_out_ref, end_in_ref, send, receive, bias_send, bias_receive = levels[3 * depth :]
    own = lax.axis_index("clus")
    rows = keep_refs[0].shape[0]

    def copy(source, target, level, chunk, bit):
        return pltpu.make_async_remote_copy(
            src_ref=source,
            dst_ref=target,
            send_sem=send.at[level, chunk],
            recv_sem=receive.at[level, chunk],
            device_id={"clus": partner(own, bit)},
            device_id_type=pl.DeviceIdType.MESH,
        )

    def bias_copy(level):
        return pltpu.make_async_remote_copy(
            src_ref=bias_land_ref.at[level, 0],
            dst_ref=bias_land_ref.at[level, 1],
            send_sem=bias_send.at[level],
            recv_sem=bias_receive.at[level],
            device_id={"clus": partner(own, 2**level)},
            device_id_type=pl.DeviceIdType.MESH,
        )

    def bias_step(level):
        bias_copy(level).wait()
        total = bias_land_ref[level, 0] + bias_land_ref[level, 1]
        if level <= depth - 1:
            bias_land_ref[level + 1, 0] = total
            bias_copy(level + 1).start()
        else:
            bias_out_ref[...] = total

    copies = []
    barrier = pltpu.get_barrier_semaphore()
    for level in range(depth + 1):
        pl.semaphore_signal(
            barrier, inc=1, device_id={"clus": partner(own, 2**level)}, device_id_type=pl.DeviceIdType.MESH
        )
    pl.semaphore_wait(barrier, depth + 1)
    bias_land_ref[0, 0] = bias_ref[...]
    bias_copy(0).start()
    first = [copy(sent_refs[chunk], land_ref.at[chunk], 0, chunk, 1) for chunk in range(2)]
    for item in first:
        item.start()
    copies += first

    inner = [
        [
            copy(out_refs[level - 1].at[chunk], in_refs[level - 1].at[chunk], level, chunk, 2**level)
            for chunk in range(2)
        ]
        for level in range(1, depth + 1)
    ]
    bit = (own // 2) % 2
    for chunk in range(2):
        first[chunk].wait_recv()
        total_refs[chunk][:rows, :] = keep_refs[chunk][...] + land_ref[chunk].astype(F32)
        total_refs[chunk][rows:, :] = jnp.zeros((2 * capacity + SUBLANES, LANES), F32)
        for j in range(groups // 4):
            gone = 2 * j + 1 - bit
            window = take_rows(total_refs[chunk], table_ref[STARTS + 2 * gone], 2 * capacity, rows - 1)
            out_refs[0][chunk, j] = window.astype(BF16)
        inner[0][chunk].start()
        for j in range(groups // 4):
            kept = 2 * j + bit
            held_refs[0][chunk, j] = take_rows(total_refs[chunk], table_ref[STARTS + 2 * kept], 2 * capacity, rows - 1)
    bias_step(0)
    copies += inner[0]
    for level in range(2, depth + 1):
        bit = (own // 2**level) % 2
        held_ref, in_ref = held_refs[level - 2], in_refs[level - 2]
        for chunk in range(2):
            inner[level - 2][chunk].wait_recv()
            for j in range(held_refs[level - 1].shape[1]):
                gone = 2 * j + 1 - bit
                out_refs[level - 1][chunk, j] = (held_ref[chunk, gone] + in_ref[chunk, gone].astype(F32)).astype(BF16)
            inner[level - 1][chunk].start()
            for j in range(held_refs[level - 1].shape[1]):
                kept = 2 * j + bit
                held_refs[level - 1][chunk, j] = held_ref[chunk, kept] + in_ref[chunk, kept].astype(F32)
        bias_step(level - 1)
        copies += inner[level - 1]
    lead = table_ref[STARTS + (own // 2) * 2]
    ends = [copy(end_out_ref.at[chunk], end_in_ref.at[chunk], depth + 1, chunk, 1) for chunk in range(2)]
    for chunk in range(2):
        inner[depth - 1][chunk].wait_recv()
        total_refs[chunk][: 2 * capacity, :] = held_refs[depth - 1][chunk, 0] + in_refs[depth - 1][chunk, 0].astype(F32)
        other = table_ref[STARTS + partner(own, 1)] - lead
        end_out_ref[chunk] = take_rows(total_refs[chunk], other, capacity, capacity).astype(BF16)
        ends[chunk].start()
        own_refs[chunk][...] = take_rows(total_refs[chunk], table_ref[STARTS + own] - lead, capacity, capacity)
    bias_step(depth)
    for chunk in range(2):
        ends[chunk].wait_recv()
        got_refs[chunk][...] = end_in_ref[chunk]
    for item in copies + ends:
        item.wait_send()


def sum_over_owners(table, groups, capacity, keep, sent, bias, after=()):
    rows, quarter = keep[0].shape
    width = bias.shape[1]
    depth = groups.bit_length() - 2
    flat = lambda i: (0, 0)
    sizes = [(2, groups // 2 ** (level + 1), 2 * capacity, quarter) for level in range(1, depth + 1)]
    shape = (capacity, quarter)
    return launch(
        "sum", functools.partial(sum_kernel, groups, capacity), table,
        [(array, array.shape, flat) for array in (*keep, *sent, bias)],
        [(shape, F32, shape, flat)] * 2 + [(shape, BF16, shape, flat)] * 2 + [(bias.shape, F32, bias.shape, flat)],
        after=after, barrier=SUM_ID,
        scratch=[
            pltpu.VMEM((rows + 2 * capacity + SUBLANES, quarter), F32),
            pltpu.VMEM((rows + 2 * capacity + SUBLANES, quarter), F32),
            pltpu.VMEM((2, rows, quarter), BF16),
            pltpu.VMEM((depth + 1, 2, 1, width), F32),
        ]
        + [pltpu.VMEM(size, F32) for size in sizes]
        + [pltpu.VMEM(size, BF16) for size in sizes]
        + [pltpu.VMEM(size, BF16) for size in sizes]
        + [
            pltpu.VMEM((2, *shape), BF16),
            pltpu.VMEM((2, *shape), BF16),
            pltpu.SemaphoreType.DMA((depth + 2, 2)),
            pltpu.SemaphoreType.DMA((depth + 2, 2)),
            pltpu.SemaphoreType.DMA((depth + 1,)),
            pltpu.SemaphoreType.DMA((depth + 1,)),
        ],
    )


def adamw_update(current, first_moment, second_moment, gradient, step_rate):
    first_new = BETA_ONE * first_moment + (1.0 - BETA_ONE) * gradient
    second_new = BETA_TWO * second_moment + (1.0 - BETA_TWO) * gradient * gradient
    fixed_first = first_new / (1.0 - BETA_ONE**STEP)
    fixed_second = second_new / (1.0 - BETA_TWO**STEP)
    updated = current - step_rate * (
        fixed_first / (jnp.sqrt(fixed_second) + EPSILON) + DECAY * current
    )
    return (updated, first_new, second_new)


def adamw_kernel(groups, table_ref, *refs):
    own_refs, got_refs, (bias_grad_ref, *states), outs = refs[:2], refs[2:4], refs[4:11], refs[11:]
    weights, biases = states[:3], states[3:]
    rows, width = weights[0].shape
    quarter = width // 4
    own = table_ref[GROUP]
    row_ids = pl.program_id(0) * rows + lax.broadcasted_iota(jnp.int32, (rows, quarter), 0)
    used = row_ids < table_ref[STARTS + groups + own]
    for block in range(4):
        mine = (own & 1) == block // 2
        gradient = jnp.where(mine, own_refs[block % 2][...], got_refs[block % 2][...].astype(F32))
        columns = slice(block * quarter, (block + 1) * quarter)
        results = adamw_update(*(ref[:, columns] for ref in weights), gradient, RATE_WEIGHT)
        for out_ref, result in zip(outs[:3], results):
            out_ref[:, columns] = jnp.where(used, result, 0.0)
    results = adamw_update(*(ref[...] for ref in biases), bias_grad_ref[...], RATE_BIAS)
    for out_ref, result in zip(outs[3:], results):
        out_ref[...] = result


def adamw(table, groups, own, got, bias_grad, weights, biases, after=()):
    capacity, width = weights[0].shape
    steps = 4 if capacity % 64 == 0 and capacity >= 256 else 1
    rows, quarter = capacity // steps, width // 4
    down, fixed = (lambda i: (i, 0)), (lambda i: (0, 0))
    return launch(
        "adamw", functools.partial(adamw_kernel, groups), table,
        [(array, (rows, quarter), down) for array in (*own, *got)]
        + [(bias_grad, (1, width), fixed)]
        + [(array, (rows, width), down) for array in weights]
        + [(array, (1, width), fixed) for array in biases],
        [((capacity, width), F32, (rows, width), down)] * 3 + [((1, width), F32, (1, width), fixed)] * 3,
        grid=(steps,), after=after,
    )


def shards(
    features,
    neighbours,
    node_counts,
    row_counts,
    master_weight,
    weight_first,
    weight_second,
    master_bias,
    bias_first,
    bias_second,
    out_grad,
):
    groups = lax.axis_size("clus")
    capacity, width = master_weight.shape
    owner_ids = jnp.arange(groups, dtype=jnp.int32)
    starts = jnp.sum(jnp.where(owner_ids[None, :] < owner_ids[:, None], row_counts[None, :], 0), axis=1)
    table = jnp.concatenate(
        [
            jnp.stack([lax.axis_index("clus"), lax.axis_index("col")]).astype(jnp.int32),
            node_counts[:, 0],
            starts.astype(jnp.int32),
            row_counts,
        ]
    )
    bias_row, bias_first_row, bias_second_row = (
        array.reshape(1, width) for array in (master_bias, bias_first, bias_second)
    )

    picked = []
    for m in range(MB):
        picked.append(pick(table, features, m, picked[-1:]))
    far = [flip(array, "col", 2) for array in picked]

    matrix, scale, here, slots = front(
        table, groups, master_weight, jnp.swapaxes(neighbours, 1, 2), features, [picked[-1]]
    )
    weight, for_mate = place(table, slots, [here])
    last = for_mate
    outputs, input_grads = None, None
    mixed, pres, biases, own, away = [], [], [], [], []
    for m in range(MB):
        there, here_mate, there_mate = mix(table, m, matrix, scale, far[m], here, [last])
        mixed.append([here_mate, there, there_mate])
        outputs, grad_pre, bias_sum = layer(
            table, m, here, mixed[m], weight, bias_row, out_grad, outputs, [there]
        )
        pres.append(grad_pre)
        biases.append(bias_sum)
        own_m, *away_m = back(table, m, grad_pre, weight, for_mate, 2 if m == MB - 1 else 1, [bias_sum])
        own.append(own_m)
        away.append([flip(chunk, "col", 2) for chunk in away_m])
        last = own_m

    keep_low, keep_high, sent_low, sent_high, bias_sum = weight_gradient(
        table, here, mixed, pres, biases, [last]
    )
    *rows, bias_total = sum_over_owners(
        table, groups, capacity, (keep_low, keep_high), (sent_low, sent_high), bias_sum, [last]
    )
    last = bias_total
    for m in range(MB):
        if m == MB - 1:
            updated = adamw(
                table, groups, rows[:2], rows[2:], bias_total,
                (master_weight, weight_first, weight_second), (bias_row, bias_first_row, bias_second_row), [last],
            )
            last = updated[0]
        for chunk, got in enumerate(away[m]):
            last = input_grads = scatter(table, m, chunk, own[m], got, scale, matrix, input_grads, [last])
    return (outputs, input_grads, *updated[:3], *(row.reshape(width) for row in updated[3:]))


def solution(mesh):
    in_specs = (
        P(None, "clus", "col"),
        P(None, "clus", None),
        P(None, "clus"),
        P(),
        P("clus", "col"),
        P("clus", "col"),
        P("clus", "col"),
        P("col"),
        P("col"),
        P("col"),
        P(None, "clus", "col"),
    )
    out_specs = (
        P(None, "clus", "col"),
        P(None, "clus", "col"),
        P("clus", "col"),
        P("clus", "col"),
        P("clus", "col"),
        P("col"),
        P("col"),
        P("col"),
    )
    return jax.shard_map(shards, mesh=mesh, in_specs=in_specs, out_specs=out_specs, check_vma=False)
```

time: 344 us -> 283 us (0.82)
  waiting for transfers between devices: 63.5 us -> 0.02 us
  Pallas kernels: 210 us -> 261 us
  starting transfers between devices: 27.8 us -> 9.45 us
  local copies, waits for them, and re-layouts: 23.6 us -> 9.43 us
  between operations: 14.4 us -> 0.94 us
    ppermute x28 -> x7, waiting for transfers between devices: 63.5 us -> 0.02 us  [flip(): return lax.ppermute(values, axis, [(i, i ^ bit) for i in range(size)])]
    pallas_call x28 -> x21, Pallas kernels: 210 us -> 261 us  [launch(): return call()(*operands)]
    ppermute x28 -> x7, starting transfers between devices: 27.8 us -> 9.45 us  [flip(): return lax.ppermute(values, axis, [(i, i ^ bit) for i in range(size)])]
    unnamed x88 -> x48, local copies, waits for them, and re-layouts: 23.5 us -> 8.69 us
  transfers between devices with their start and end apart: 29 -> 7, of which waited for: 10 -> 0; matrix products, arithmetic and copies ran while one was open for 2% -> 0% of each run, Pallas kernels for 57% -> 90%
where the time goes in v2:
time: 283 us; the launch traced here: 282 us
  Pallas kernels  261 us (92%)
  starting transfers between devices  9.45 us (3%)
  local copies, waits for them, and re-layouts  9.43 us (3%)
    pallas_call x21, Pallas kernels, launch(): return call()(*operands)  261 us
    ppermute x7, starting transfers between devices, flip(): return lax.ppermute(values, axis, [(i, i ^ bit) for i in range(size)])  9.45 us
    unnamed x48, local copies, waits for them, and re-layouts  8.69 us
  transfers between devices with their start and end apart: 7, of which 0 were waited for; matrix products, arithmetic and copies ran while one was open for 0% of the time, Pallas kernels for 90%

profile of v2, /device:TPU:0, one launch (start us, length us, event | category | flops | bytes accessed | tf_op | source)
XLA Modules:
  0.0 281.7 jit_solution(17852128578899666568)
XLA Ops:
  0.6 0.8 select_reduce_fusion
  1.4 0.7 concatenate.3.table_ref
  2.2 2.0 pick0.1.refs_1_
  4.1 3.0 %collective-permute-start.2 = (bf16[1536,512]{1,0:T(8,128)(2,1)S(1)}, bf16[1536,512]{1,0:T(8,128)(2,1)S(1)}, u32[]{:S(2)}, u32[]{:S(2)}) collective-permute-start(bf16[1536,512]{1,0:T(8,128)(2,1)S(1)} %pick0.1.refs_1_), channel_id=1, source_target_pairs={{0,2},{1,3},{2,0},{3,1},{4,6},{5,7},{6,4},{7,5},{8,10},{9,11},{10,... | collective-permute-start | bytes 4718600 | tf_op jit(solution)/shard_map/ppermute | solution.py:82
  7.2 2.0 pick1.1.refs_1_
  9.1 0.0 copy-start.14
  9.1 0.0 copy-start.19
  9.1 0.1 collective-permute-start.1
  9.2 2.0 pick2.1.refs_3_
  11.2 2.1 collective-permute-start
  13.3 0.0 copy-done.14
  13.3 0.0 copy-done.19
  13.3 52.0 %front.1 = (bf16[3,1536,1536]{2,1,0:T(8,128)(2,1)}, f32[3,1536,128]{2,1,0:T(8,128)S(1)}, bf16[3,1536,512]{2,1,0:T(8,128)(2,1)}, bf16[8,512,512]{2,1,0:T(8,128)(2,1)}) custom-call(s32[21]{0:T(128)S(1)} %concatenate.3.table_ref, f32[512,512]{1,0:T(8,128)S(1)} %copy-done.14, s32[3,16,1536]{2,1,0:T(8,128)S(1)} %bitcast.10, bf16[3,1536,512]{2,1,0:T(8,128)(2,1)} %refs_2_.1, ...), custom_call_target="tpu_custom_call" | custom-call | flops 1 | bytes 1 | tf_op jit(solution)/shard_map/front/pallas_call | solution.py:70
  65.3 0.0 copy-start
  65.3 1.4 copy-done
  66.7 8.3 %place.1 = (bf16[4,512,512]{2,1,0:T(8,128)(2,1)S(1)}, bf16[2,512,512]{2,1,0:T(8,128)(2,1)S(1)}) custom-call(s32[21]{0:T(128)S(1)} %concatenate.3.table_ref, bf16[8,512,512]{2,1,0:T(8,128)(2,1)} %get-tuple-element.58.refs_0_, bf16[3,1536,512]{2,1,0:T(8,128)(2,1)} %get-tuple-element.55.refs_1_.refs_3_.refs_0_.refs_4_.refs_8_), custom_call_target="tpu_custom_call" | custom-call | flops 1 | bytes 1 | tf_op jit(solution)/shard_map/place/pallas_call | solution.py:77
  75.0 0.0 copy-start.2
  75.0 1.3 copy-done.2
  76.4 0.0 collective-permute-done.2.refs_2_
  76.4 1.1 copy-done.23
  77.5 8.7 %mix0.1 = (bf16[1536,512]{1,0:T(8,128)(2,1)S(1)}, bf16[1536,512]{1,0:T(8,128)(2,1)S(1)}, bf16[1536,512]{1,0:T(8,128)(2,1)S(1)}) custom-call(s32[21]{0:T(128)S(1)} %concatenate.3.table_ref, bf16[3,1536,1536]{2,1,0:T(8,128)(2,1)} %get-tuple-element.56.refs_0_.refs_3_, f32[3,1536,128]{2,1,0:T(8,128)} %copy-done, bf16[1536,512]{1,0:T(8,128)(2,1)} %copy-done.23, ...), custom_call_target="tpu_custom_call" | custom-call | flops 1 | bytes 1 | tf_op jit(solution)/shard_map/mix0/pallas_call | solution.py:76
  86.3 0.0 copy-start.13
  86.3 1.2 copy-done.13
  87.4 0.0 copy-done.20
  87.4 9.5 %layer0.1 = (bf16[3,1536,512]{2,1,0:T(8,128)(2,1)}, bf16[1536,512]{1,0:T(8,128)(2,1)S(1)}, f32[1,512]{1,0:T(1,128)S(1)}) custom-call(s32[21]{0:T(128)S(1)} %concatenate.3.table_ref, bf16[3,1536,512]{2,1,0:T(8,128)(2,1)} %get-tuple-element.55.refs_1_.refs_3_.refs_0_.refs_4_.refs_8_, bf16[1536,512]{1,0:T(8,128)(2,1)S(1)} %get-tuple-element.60.refs_1_, ...), custom_call_target="tpu_custom_call" | custom-call | flops 1 | bytes 1 | tf_op jit(solution)/shard_map/layer0/pallas_call | solution.py:77
  96.9 0.0 copy-done.8
  96.9 11.0 %back0.1 = (f32[1536,512]{1,0:T(8,128)}, bf16[1536,512]{1,0:T(8,128)(2,1)}) custom-call(s32[21]{0:T(128)S(1)} %concatenate.3.table_ref, bf16[1536,512]{1,0:T(8,128)(2,1)S(1)} %get-tuple-element.64.refs_0_.refs_2_.refs_12_, bf16[2,512,512]{2,1,0:T(8,128)(2,1)S(1)} %get-tuple-element.59.refs_4_.refs_1_, ...), custom_call_target="tpu_custom_call" | custom-call | flops 1 | bytes 1 | tf_op jit(solution)/shard_map/back0/pallas_call | solution.py:74
  107.9 0.0 copy-done.5
  107.9 0.6 collective-permute-start.6
  108.5 0.0 collective-permute-done.1.refs_2_
  108.5 8.3 %mix1.1 = (bf16[1536,512]{1,0:T(8,128)(2,1)S(1)}, bf16[1536,512]{1,0:T(8,128)(2,1)S(1)}, bf16[1536,512]{1,0:T(8,128)(2,1)S(1)}) custom-call(s32[21]{0:T(128)S(1)} %concatenate.3.table_ref, bf16[3,1536,1536]{2,1,0:T(8,128)(2,1)} %get-tuple-element.56.refs_0_.refs_3_, f32[3,1536,128]{2,1,0:T(8,128)} %copy-done, ...), custom_call_target="tpu_custom_call" | custom-call | flops 1 | bytes 1 | tf_op jit(solution)/shard_map/mix1/pallas_call | solution.py:76
  116.8 1.1 copy-done.10
  117.9 9.9 %layer1.1 = (bf16[3,1536,512]{2,1,0:T(8,128)(2,1)}, bf16[1536,512]{1,0:T(8,128)(2,1)S(1)}, f32[1,512]{1,0:T(1,128)S(1)}) custom-call(s32[21]{0:T(128)S(1)} %concatenate.3.table_ref, bf16[3,1536,512]{2,1,0:T(8,128)(2,1)} %get-tuple-element.55.refs_1_.refs_3_.refs_0_.refs_4_.refs_8_, ...), custom_call_target="tpu_custom_call", output_to_operand_aliasing={{0}: (8, {})} | custom-call | flops 1 | bytes 1 | tf_op jit(solution)/shard_map/layer1/pallas_call | solution.py:77
  127.8 0.0 copy-start.6
  127.8 11.0 %back1.1 = (f32[1536,512]{1,0:T(8,128)}, bf16[1536,512]{1,0:T(8,128)(2,1)}) custom-call(s32[21]{0:T(128)S(1)} %concatenate.3.table_ref, bf16[1536,512]{1,0:T(8,128)(2,1)S(1)} %get-tuple-element.71.refs_0_.refs_2_.refs_13_, bf16[2,512,512]{2,1,0:T(8,128)(2,1)S(1)} %get-tuple-element.59.refs_4_.refs_1_, ...), custom_call_target="tpu_custom_call" | custom-call | flops 1 | bytes 1 | tf_op jit(solution)/shard_map/back1/pallas_call | solution.py:74
  138.9 0.0 copy-done.6
  138.9 1.6 collective-permute-start.5
  140.5 0.0 collective-permute-done.refs_2_
  140.5 8.3 %mix2.1 = (bf16[1536,512]{1,0:T(8,128)(2,1)S(1)}, bf16[1536,512]{1,0:T(8,128)(2,1)S(1)}, bf16[1536,512]{1,0:T(8,128)(2,1)S(1)}) custom-call(s32[21]{0:T(128)S(1)} %concatenate.3.table_ref, bf16[3,1536,1536]{2,1,0:T(8,128)(2,1)} %get-tuple-element.56.refs_0_.refs_3_, f32[3,1536,128]{2,1,0:T(8,128)} %copy-done, ...), custom_call_target="tpu_custom_call" | custom-call | flops 1 | bytes 1 | tf_op jit(solution)/shard_map/mix2/pallas_call | solution.py:76
  148.8 1.2 copy-done.12
  150.0 9.9 %layer2.1 = (bf16[3,1536,512]{2,1,0:T(8,128)(2,1)}, bf16[1536,512]{1,0:T(8,128)(2,1)S(1)}, f32[1,512]{1,0:T(1,128)S(1)}) custom-call(s32[21]{0:T(128)S(1)} %concatenate.3.table_ref, bf16[3,1536,512]{2,1,0:T(8,128)(2,1)} %get-tuple-element.55.refs_1_.refs_3_.refs_0_.refs_4_.refs_8_, ...), custom_call_target="tpu_custom_call", output_to_operand_aliasing={{0}: (8, {})} | custom-call | flops 1 | bytes 1 | tf_op jit(solution)/shard_map/layer2/pallas_call | solution.py:77
  159.9 0.0 copy-start.7
  159.9 10.6 %back2.1 = (f32[1536,512]{1,0:T(8,128)}, bf16[1536,256]{1,0:T(8,128)(2,1)S(1)}, bf16[1536,256]{1,0:T(8,128)(2,1)S(1)}) custom-call(s32[21]{0:T(128)S(1)} %concatenate.3.table_ref, bf16[1536,512]{1,0:T(8,128)(2,1)S(1)} %get-tuple-element.79.refs_0_.refs_2_.refs_14_, bf16[2,512,512]{2,1,0:T(8,128)(2,1)S(1)} %get-tuple-element.59.refs_4_.refs_1_, ...), custom_call_target="tpu_custom_call" | custom-call | flops 1 | bytes 1 | tf_op jit(solution)/shard_map/back2/pallas_call | solution.py:74
  170.4 0.0 copy-done.7
  170.4 0.6 collective-permute-start.4
  171.0 1.5 collective-permute-start.3
  172.5 16.9 %weight.1 = (f32[2048,128]{1,0:T(8,128)S(1)}, f32[2048,128]{1,0:T(8,128)S(1)}, bf16[2048,128]{1,0:T(8,128)(2,1)S(1)}, bf16[2048,128]{1,0:T(8,128)(2,1)S(1)}, f32[1,512]{1,0:T(1,128)S(1)}) custom-call(s32[21]{0:T(128)S(1)} %concatenate.3.table_ref, bf16[3,1536,512]{2,1,0:T(8,128)(2,1)} %get-tuple-element.55.refs_1_.refs_3_.refs_0_.refs_4_.refs_8_, ...), custom_call_target="tpu_custom_call" | custom-call | flops 1 | bytes 1 | tf_op jit(solution)/shard_map/weight/pallas_call | solution.py:77
  189.5 0.0 copy-start.1
  189.5 59.2 %sum.1 = (f32[512,128]{1,0:T(8,128)S(1)}, f32[512,128]{1,0:T(8,128)S(1)}, bf16[512,128]{1,0:T(8,128)(2,1)S(1)}, bf16[512,128]{1,0:T(8,128)(2,1)S(1)}, f32[1,512]{1,0:T(1,128)S(1)}) custom-call(s32[21]{0:T(128)S(1)} %concatenate.3.table_ref, f32[2048,128]{1,0:T(8,128)S(1)} %get-tuple-element.86.refs_0_, f32[2048,128]{1,0:T(8,128)S(1)} %get-tuple-element.87.refs_1_, ...), custom_call_target="tpu_custom_call" | custom-call | flops 1 | bytes 1 | tf_op jit(solution)/shard_map/sum/pallas_call | solution.py:72
  248.7 0.0 collective-permute-done.6.refs_1_
  248.7 8.3 %scatter0_0.1.refs_4_ = bf16[3,1536,512]{2,1,0:T(8,128)(2,1)} custom-call(s32[21]{0:T(128)S(1)} %concatenate.3.table_ref, f32[1536,512]{1,0:T(8,128)} %get-tuple-element.66.refs_4_.refs_0_, bf16[1536,512]{1,0:T(8,128)(2,1)} %collective-permute-done.6.refs_1_, f32[3,1536,128]{2,1,0:T(8,128)S(1)} %copy-done.1, ...), custom_call_target="tpu_custom_call" | custom-call | flops 1 | bytes 1 | tf_op jit(solution)/shard_map/scatter0_0/pallas_call | solution.py:77
  257.0 0.0 copy-start.21
  257.0 0.0 copy-start.22
  257.0 0.0 collective-permute-done.5.refs_1_
  257.0 8.1 %scatter1_0.1.refs_11_.refs_4_ = bf16[3,1536,512]{2,1,0:T(8,128)(2,1)} custom-call(s32[21]{0:T(128)S(1)} %concatenate.3.table_ref, f32[1536,512]{1,0:T(8,128)} %get-tuple-element.73.refs_4_.refs_0_, bf16[1536,512]{1,0:T(8,128)(2,1)S(1)} %collective-permute-done.5.refs_1_, f32[3,1536,128]{2,1,0:T(8,128)S(1)} %copy-done.1, ...), custom_call_target="tpu_custom_call", output_to_operand_aliasing={{}: (5, {})} | custom-call | flops 1 | bytes 1 | tf_op jit(solution)/shard_map/scatter1_0/pallas_call | solution.py:77
  265.1 0.0 copy-done.17
  265.1 0.0 copy-done.21
  265.1 0.0 copy-done.22
  265.1 3.2 %adamw.1 = (f32[512,512]{1,0:T(8,128)}, f32[512,512]{1,0:T(8,128)}, f32[512,512]{1,0:T(8,128)}, f32[1,512]{1,0:T(1,128)}, f32[1,512]{1,0:T(1,128)}, /*index=5*/f32[1,512]{1,0:T(1,128)}) custom-call(s32[21]{0:T(128)S(1)} %concatenate.3.table_ref, f32[512,128]{1,0:T(8,128)S(1)} %get-tuple-element.92.refs_0_, f32[512,128]{1,0:T(8,128)S(1)} %get-tuple-element.93.refs_1_, ...), custom_call_target="tpu_custom_call" | custom-call | flops 1 | bytes 1 | tf_op jit(solution)/shard_map/adamw/pallas_call | solution.py:77
  268.3 0.0 collective-permute-done.4.refs_1_
  268.3 1.2 copy-done.18
  269.5 6.1 %scatter2_0.1.refs_4_ = bf16[3,1536,512]{2,1,0:T(8,128)(2,1)} custom-call(s32[21]{0:T(128)S(1)} %concatenate.3.table_ref, f32[1536,512]{1,0:T(8,128)} %get-tuple-element.81.refs_18_.refs_5_.refs_0_, bf16[1536,256]{1,0:T(8,128)(2,1)S(1)} %collective-permute-done.4.refs_1_, f32[3,1536,128]{2,1,0:T(8,128)S(1)} %copy-done.1, ...), custom_call_target="tpu_custom_call", output_to_operand_aliasing={{}: (5, {})} | custom-call | flops 1 | bytes 1 | tf_op jit(solution)/shard_map/scatter2_0/pallas_call | solution.py:77
  275.6 0.0 collective-permute-done.3.refs_1_
  275.6 6.1 %scatter2_1.1 = bf16[3,1536,512]{2,1,0:T(8,128)(2,1)} custom-call(s32[21]{0:T(128)S(1)} %concatenate.3.table_ref, f32[1536,512]{1,0:T(8,128)} %get-tuple-element.81.refs_18_.refs_5_.refs_0_, bf16[1536,256]{1,0:T(8,128)(2,1)S(1)} %collective-permute-done.3.refs_1_, f32[3,1536,128]{2,1,0:T(8,128)S(1)} %copy-done.1, ...), custom_call_target="tpu_custom_call", output_to_operand_aliasing={{}: (5, {})} | custom-call | flops 1 | bytes 1 | tf_op jit(solution)/shard_map/scatter2_1/pallas_call | solution.py:77
  (21 shorter events, 0.0 us)
Async XLA Ops:
  4.1 72.2 %collective-permute-start.2 = (bf16[1536,512]{1,0:T(8,128)(2,1)S(1)}, bf16[1536,512]{1,0:T(8,128)(2,1)S(1)}, u32[]{:S(2)}, u32[]{:S(2)}) collective-permute-start(bf16[1536,512]{1,0:T(8,128)(2,1)S(1)} %pick0.1.refs_1_), channel_id=1, source_target_pairs={{0,2},{1,3},{2,0},{3,1},{4,6},{5,7},{6,4},{7,5},{8,10},{9,11},{10,... | collective-permute-start | bytes 4718600 | tf_op jit(solution)/shard_map/ppermute | solution.py:82
  9.1 4.1 %copy-start.14 = (f32[512,512]{1,0:T(8,128)S(1)}, f32[512,512]{1,0:T(8,128)}, u32[]{:S(2)}) copy-start(f32[512,512]{1,0:T(8,128)} %refs_5_.1) | copy-start | bytes 3145732
  9.1 4.1 %copy-start.19 = (s32[3,1536,16]{1,2,0:T(8,128)S(1)}, s32[3,1536,16]{1,2,0:T(8,128)}, u32[]{:S(2)}) copy-start(s32[3,1536,16]{1,2,0:T(8,128)} %param.12) | copy-start | bytes 884740
  9.1 99.4 %collective-permute-start.1 = (bf16[1536,512]{1,0:T(8,128)(2,1)S(1)}, bf16[1536,512]{1,0:T(8,128)(2,1)}, u32[]{:S(2)}, u32[]{:S(2)}) collective-permute-start(bf16[1536,512]{1,0:T(8,128)(2,1)S(1)} %pick1.1.refs_1_), channel_id=1, source_target_pairs={{0,2},{1,3},{2,0},{3,1},{4,6},{5,7},{6,4},{7,5},{8,10},{9,11},{10,... | collective-permute-start | bytes 4718600 | tf_op jit(solution)/shard_map/ppermute | solution.py:82
  11.2 129.3 %collective-permute-start = (bf16[1536,512]{1,0:T(8,128)(2,1)S(1)}, bf16[1536,512]{1,0:T(8,128)(2,1)}, u32[]{:S(2)}, u32[]{:S(2)}) collective-permute-start(bf16[1536,512]{1,0:T(8,128)(2,1)S(1)} %pick2.1.refs_3_), channel_id=1, source_target_pairs={{0,2},{1,3},{2,0},{3,1},{4,6},{5,7},{6,4},{7,5},{8,10},{9,11},{10,... | collective-permute-start | bytes 4718600 | tf_op jit(solution)/shard_map/ppermute | solution.py:82
  65.3 1.4 copy-start
  75.0 1.4 copy-start.2
  76.4 1.1 copy-start.23
  77.5 9.9 %copy-start.20 = (f32[512]{0:T(512)S(1)}, f32[512]{0:T(512)}, u32[]{:S(2)}) copy-start(f32[512]{0:T(512)} %param.18) | copy-start | bytes 6148
  86.3 1.2 copy-start.13
  87.4 9.5 %copy-start.8 = (bf16[1536,512]{1,0:T(8,128)(2,1)}, bf16[1536,512]{1,0:T(8,128)(2,1)S(1)}, u32[]{:S(2)}) copy-start(bf16[1536,512]{1,0:T(8,128)(2,1)S(1)} %get-tuple-element.61.refs_2_.refs_7_) | copy-start | bytes 4718596
  96.9 11.0 %copy-start.5 = (bf16[1536,512]{1,0:T(8,128)(2,1)}, bf16[1536,512]{1,0:T(8,128)(2,1)S(1)}, u32[]{:S(2)}) copy-start(bf16[1536,512]{1,0:T(8,128)(2,1)S(1)} %get-tuple-element.64.refs_0_.refs_2_.refs_12_) | copy-start | bytes 4718596
  107.9 140.8 %collective-permute-start.6 = (bf16[1536,512]{1,0:T(8,128)(2,1)}, bf16[1536,512]{1,0:T(8,128)(2,1)}, u32[]{:S(2)}, u32[]{:S(2)}) collective-permute-start(bf16[1536,512]{1,0:T(8,128)(2,1)} %get-tuple-element.85), channel_id=1, source_target_pairs={{0,2},{1,3},{2,0},{3,1},{4,6},{5,7},{6,4},{7,5},{8,10},{9,11},{10,... | collective-permute-start | bytes 4718600 | tf_op jit(solution)/shard_map/ppermute | solution.py:82
  116.8 1.2 copy-start.10
  117.9 9.9 %copy-start.3 = (bf16[1536,512]{1,0:T(8,128)(2,1)}, bf16[1536,512]{1,0:T(8,128)(2,1)S(1)}, u32[]{:S(2)}) copy-start(bf16[1536,512]{1,0:T(8,128)(2,1)S(1)} %get-tuple-element.68.refs_2_.refs_8_.refs_6_) | copy-start | bytes 4718596
  117.9 9.9 %copy-start.9 = (bf16[1536,512]{1,0:T(8,128)(2,1)}, bf16[1536,512]{1,0:T(8,128)(2,1)S(1)}, u32[]{:S(2)}) copy-start(bf16[1536,512]{1,0:T(8,128)(2,1)S(1)} %get-tuple-element.67.refs_1_.refs_5_) | copy-start | bytes 4718596
  127.8 11.1 %copy-start.6 = (bf16[1536,512]{1,0:T(8,128)(2,1)}, bf16[1536,512]{1,0:T(8,128)(2,1)S(1)}, u32[]{:S(2)}) copy-start(bf16[1536,512]{1,0:T(8,128)(2,1)S(1)} %get-tuple-element.71.refs_0_.refs_2_.refs_13_) | copy-start | bytes 4718596
  138.9 118.1 %collective-permute-start.5 = (bf16[1536,512]{1,0:T(8,128)(2,1)}, bf16[1536,512]{1,0:T(8,128)(2,1)S(1)}, u32[]{:S(2)}, u32[]{:S(2)}) collective-permute-start(bf16[1536,512]{1,0:T(8,128)(2,1)} %get-tuple-element.84), channel_id=1, source_target_pairs={{0,2},{1,3},{2,0},{3,1},{4,6},{5,7},{6,4},{7,5},{8,10},{9,11},{10,... | collective-permute-start | bytes 4718600 | tf_op jit(solution)/shard_map/ppermute | solution.py:82
  148.8 1.2 copy-start.12
  150.0 9.9 %copy-start.4 = (bf16[1536,512]{1,0:T(8,128)(2,1)}, bf16[1536,512]{1,0:T(8,128)(2,1)S(1)}, u32[]{:S(2)}) copy-start(bf16[1536,512]{1,0:T(8,128)(2,1)S(1)} %get-tuple-element.75.refs_2_.refs_8_.refs_10_) | copy-start | bytes 4718596
  150.0 9.9 %copy-start.11 = (bf16[1536,512]{1,0:T(8,128)(2,1)}, bf16[1536,512]{1,0:T(8,128)(2,1)S(1)}, u32[]{:S(2)}) copy-start(bf16[1536,512]{1,0:T(8,128)(2,1)S(1)} %get-tuple-element.74.refs_1_.refs_9_) | copy-start | bytes 4718596
  159.9 10.6 %copy-start.7 = (bf16[1536,512]{1,0:T(8,128)(2,1)}, bf16[1536,512]{1,0:T(8,128)(2,1)S(1)}, u32[]{:S(2)}) copy-start(bf16[1536,512]{1,0:T(8,128)(2,1)S(1)} %get-tuple-element.79.refs_0_.refs_2_.refs_14_) | copy-start | bytes 4718596
  170.4 97.9 %collective-permute-start.4 = (bf16[1536,256]{1,0:T(8,128)(2,1)S(1)}, bf16[1536,256]{1,0:T(8,128)(2,1)S(1)}, u32[]{:S(2)}, u32[]{:S(2)}) collective-permute-start(bf16[1536,256]{1,0:T(8,128)(2,1)S(1)} %get-tuple-element.83), channel_id=1, source_target_pairs={{0,2},{1,3},{2,0},{3,1},{4,6},{5,7},{6,4},{7,5},{8,10},{9,11},{10,... | collective-permute-start | bytes 2359304 | tf_op jit(solution)/shard_map/ppermute | solution.py:82
  171.0 104.6 %collective-permute-start.3 = (bf16[1536,256]{1,0:T(8,128)(2,1)S(1)}, bf16[1536,256]{1,0:T(8,128)(2,1)S(1)}, u32[]{:S(2)}, u32[]{:S(2)}) collective-permute-start(bf16[1536,256]{1,0:T(8,128)(2,1)S(1)} %get-tuple-element.82), channel_id=1, source_target_pairs={{0,2},{1,3},{2,0},{3,1},{4,6},{5,7},{6,4},{7,5},{8,10},{9,11},{10,... | collective-permute-start | bytes 2359304 | tf_op jit(solution)/shard_map/ppermute | solution.py:82
  189.5 59.2 %copy-start.1 = (f32[3,1536,128]{2,1,0:T(8,128)S(1)}, f32[3,1536,128]{2,1,0:T(8,128)}, u32[]{:S(2)}) copy-start(f32[3,1536,128]{2,1,0:T(8,128)} %copy-done) | copy-start | bytes 7077892
  257.0 8.1 %copy-start.15 = (f32[512,512]{1,0:T(8,128)S(1)}, f32[512,512]{1,0:T(8,128)}, u32[]{:S(2)}) copy-start(f32[512,512]{1,0:T(8,128)} %refs_5_.1) | copy-start | bytes 3145732
  257.0 8.1 %copy-start.16 = (f32[512,512]{1,0:T(8,128)S(1)}, f32[512,512]{1,0:T(8,128)}, u32[]{:S(2)}) copy-start(f32[512,512]{1,0:T(8,128)} %refs_6_.7) | copy-start | bytes 3145732
  257.0 8.1 %copy-start.17 = (f32[512,512]{1,0:T(8,128)S(1)}, f32[512,512]{1,0:T(8,128)}, u32[]{:S(2)}) copy-start(f32[512,512]{1,0:T(8,128)} %refs_7_.1) | copy-start | bytes 3145732
  257.0 8.1 %copy-start.21 = (f32[512]{0:T(512)S(1)}, f32[512]{0:T(512)}, u32[]{:S(2)}) copy-start(f32[512]{0:T(512)} %param.19) | copy-start | bytes 6148
  257.0 8.1 %copy-start.22 = (f32[512]{0:T(512)S(1)}, f32[512]{0:T(512)}, u32[]{:S(2)}) copy-start(f32[512]{0:T(512)} %param.20) | copy-start | bytes 6148
  268.3 1.2 copy-start.18

commit v3 on v2

--- a/solution.py
+++ b/solution.py
@@ -30,7 +30,7 @@
 GROUP, COLUMN, LIMITS = 0, 1, 2
 STARTS = LIMITS + MB
 
-FRONT_ID, MIX_ID, BACK_ID, SUM_ID = 1, 2, 2 + MB, 2 + 2 * MB
+FRONT_ID, SUM_ID, BATCH_ID = 1, 2, 3
 
 F32, BF16 = jnp.float32, jnp.bfloat16
 
@@ -46,8 +46,7 @@
     def kernel(table_ref, *refs):
         body(table_ref, *refs[: len(ins)], *refs[len(ins) + len(unread) :])
 
-    call = functools.partial(
-        pl.pallas_call,
+    return pl.pallas_call(
         kernel,
         grid_spec=pltpu.PrefetchScalarGridSpec(
             num_scalar_prefetch=1,
@@ -64,17 +63,7 @@
         ),
         cost_estimate=pl.CostEstimate(flops=1, bytes_accessed=1, transcendentals=0),
         name=name,
-    )
-    operands = (table, *(array for array, _, _ in ins), *unread)
-    if barrier == FRONT_ID:
-        return call()(*operands)
-    if barrier == SUM_ID:
-        return call()(*operands)
-    if barrier is not None and barrier >= BACK_ID:
-        return call()(*operands)
-    if barrier is not None:
-        return call()(*operands)
-    return call()(*operands)
+    )(table, *(array for array, _, _ in ins), *unread)
 
 
 def flip(values, axis, bit):
@@ -344,71 +333,6 @@
     pl.semaphore_wait(barrier, 1)
 
 
-def mix_kernel(
-    m, steps, table_ref, matrix_ref, scale_ref, far_ref, here_ref, there_ref, here_mate_ref, there_mate_ref,
-    buffer_ref, send, receive,
-):
-    step = pl.program_id(0)
-    tile = there_ref.shape[0]
-    mate = partner(lax.axis_index("col"), 1)
-
-    def copy(number):
-        rows = pl.ds((number - 1) * tile, tile)
-        return pltpu.make_async_remote_copy(
-            src_ref=here_ref.at[m] if number == 0 else buffer_ref.at[rows],
-            dst_ref=here_mate_ref if number == 0 else there_mate_ref.at[rows],
-            send_sem=send.at[number],
-            recv_sem=receive.at[number],
-            device_id={"col": mate},
-            device_id_type=pl.DeviceIdType.MESH,
-        )
-
-    @pl.when(step == 0)
-    def _():
-        greet_mate(mate)
-        copy(0).start()
-
-    result = scaled(product_rows(matrix_ref[0], far_ref[...]), scale_ref[0]).astype(BF16)
-    there_ref[...] = result
-    for number in range(1, steps + 1):
-
-        @pl.when(step == number - 1)
-        def _(number=number):
-            buffer_ref[(number - 1) * tile : number * tile, :] = result
-            copy(number).start()
-
-    @pl.when(step == steps - 1)
-    def _():
-        for number in range(steps + 1):
-            copy(number).wait()
-
-
-def mix(table, m, matrix, scale, far, here, after=()):
-    nodes, width = far.shape
-    steps = nodes // WIDE
-    shape = (nodes, width)
-    return launch(
-        f"mix{m}", functools.partial(mix_kernel, m, steps), table,
-        [
-            (matrix, (1, nodes, WIDE), lambda i: (m, 0, i)),
-            (scale, (1, WIDE, LANES), lambda i: (m, i, 0)),
-            (far, shape, lambda i: (0, 0)),
-            (here, None, None),
-        ],
-        [
-            (shape, BF16, (WIDE, width), lambda i: (i, 0)),
-            (shape, BF16, None, None),
-            (shape, BF16, None, None),
-        ],
-        grid=(steps,), after=after, barrier=MIX_ID + m,
-        scratch=[
-            pltpu.VMEM(shape, BF16),
-            pltpu.SemaphoreType.DMA((steps + 1,)),
-            pltpu.SemaphoreType.DMA((steps + 1,)),
-        ],
-    )
-
-
 def place_kernel(groups, table_ref, slots_ref, weight_ref, mate_ref, rows_ref):
     owner = pl.program_id(0)
 
@@ -443,118 +367,228 @@
     )
 
 
-def layer_kernel(m, table_ref, *refs):
-    mixed_refs, (weight_ref, bias_ref, grad_ref, out_ref, pre_ref, sum_ref) = refs[:4], refs[4:]
-    tile = out_ref.shape[1]
-    preact = bias_ref[...]
-    for block in range(4):
-        mixed = mixed_refs[block][0] if block == 0 else mixed_refs[block][...]
-        preact = preact + product(mixed, weight_ref[block])
-    first_row = pl.program_id(0) * tile
-    row_ids = first_row + lax.broadcasted_iota(jnp.int32, preact.shape, 0)
-    live = row_ids < table_ref[LIMITS + m]
-    gate = jax.nn.sigmoid(preact)
-    out_ref[0] = jnp.where(live, preact * gate, 0.0).astype(BF16)
-    slope = gate * (1.0 + preact * (1.0 - gate))
-    grad_pre = jnp.where(live, grad_ref[0].astype(F32) * slope, 0.0).astype(BF16)
-    pre_ref[...] = grad_pre
-
-    @pl.when(pl.program_id(0) == 0)
-    def _():
-        sum_ref[...] = jnp.zeros_like(sum_ref)
-
-    sum_ref[...] += jnp.sum(grad_pre.astype(F32), axis=0, keepdims=True)
-
-
-def layer(table, m, here, mixed, weight, bias, out_grad, outputs, after=()):
-    _, nodes, width = here.shape
-    return launch(
-        f"layer{m}", functools.partial(layer_kernel, m), table,
-        [(here, (1, TILE, width), lambda i: (m, i, 0))]
-        + [(part, (TILE, width), lambda i: (i, 0)) for part in mixed]
-        + [
-            (weight, weight.shape, lambda i: (0, 0, 0)),
-            (bias, (1, width), lambda i: (0, 0)),
-            (out_grad, (1, TILE, width), lambda i: (m, i, 0)),
-        ],
-        [
-            ((MB, nodes, width), BF16, (1, TILE, width), lambda i: (m, i, 0)),
-            ((nodes, width), BF16, (TILE, width), lambda i: (i, 0)),
-            ((1, width), F32, (1, width), lambda i: (0, 0)),
-        ],
-        grid=(nodes // TILE,), after=after, alias=None if outputs is None else (outputs, 0),
-    )
-
-
-def back_kernel(chunks, table_ref, here_hbm, for_mate_hbm, here_ref, weight_ref, *refs):
-    own_ref, away_refs = refs[0], refs[1 : 1 + chunks]
-    mate_ref, mate_weight_ref, own_total, away_total, send, receive = refs[1 + chunks :]
-    half, step = pl.program_id(0), pl.program_id(1)
-    tile = here_ref.shape[0]
+def batch_kernel(m, chunks, table_ref, *refs):
+    matrix_hbm, scale_hbm, far_hbm, here_hbm, weight_hbm, for_mate_hbm, grad_hbm, bias_ref = refs[:8]
+    refs = refs[8:]
+    total_hbm, bias_sum_in = refs[:2] if m else (None, None)
+    refs = refs[2:] if m else refs
+    out_hbm, own_hbm = refs[:2]
+    away_hbm, refs = refs[2 : 2 + chunks], refs[2 + chunks :]
+    ended = m == MB - 1
+    results, refs = (refs[:4], refs[4:]) if ended else (refs[:1], refs[1:])
+    bias_sum_ref, refs = refs[0], refs[1:]
+    (
+        matrix_ref, scale_ref, far_ref, mixed_ref, weight_ref, mate_weight_ref, grad_ref, out_ref, pre_ref, mate_pre_ref,
+        own_ref, away_ref, total_ref, load, store, send, receive,
+    ) = refs
+    nodes, width = far_ref.shape
+    wide, narrow = nodes // WIDE, nodes // TILE
     mate = partner(lax.axis_index("col"), 1)
-    rows = pl.ds(pl.multiple_of(step * tile, tile), tile)
-
-    def copy(number):
+
+    def at(index, size):
+        return pl.ds(pl.multiple_of(index * size, size), size)
+
+    def matrix_load(i):
+        return pltpu.make_async_copy(
+            matrix_hbm.at[m, :, at(i, WIDE)], matrix_ref.at[:, at(i, WIDE)], load.at[i]
+        )
+
+    loads = [
+        pltpu.make_async_copy(source, target, load.at[wide + i])
+        for i, (source, target) in enumerate(
+            [
+                (far_hbm, far_ref),
+                (scale_hbm.at[m], scale_ref),
+                (weight_hbm, weight_ref),
+                (here_hbm.at[m], mixed_ref.at[0]),
+                (grad_hbm.at[m], grad_ref),
+            ]
+            + ([(total_hbm, total_ref)] if m else [])
+        )
+    ]
+
+    def remote(source, target, number):
         return pltpu.make_async_remote_copy(
-            src_ref=(here_hbm, for_mate_hbm)[number],
-            dst_ref=(mate_ref, mate_weight_ref)[number],
+            src_ref=source,
+            dst_ref=target,
             send_sem=send.at[number],
             recv_sem=receive.at[number],
             device_id={"col": mate},
             device_id_type=pl.DeviceIdType.MESH,
         )
 
-    @pl.when((half == 0) & (step == 0))
-    def _():
-        greet_mate(mate)
-        copy(1).start()
-        copy(0).start()
-
-    @pl.when(half == 0)
-    def _():
-        here = here_ref[...]
-        away_total[rows, :] = product_back(here, weight_ref[2])
-        own_total[rows, :] = product_back(here, weight_ref[0])
-
-    @pl.when((half == 1) & (step == 0))
-    def _():
-        copy(1).wait()
-        copy(0).wait()
-
-    @pl.when(half == 1)
-    def _():
-        mate_rows = mate_ref[rows, :]
-        away = (away_total[rows, :] + product_back(mate_rows, mate_weight_ref[1])).astype(BF16)
-        width = away.shape[1] // chunks
-        for chunk in range(chunks):
-            away_refs[chunk][...] = away[:, chunk * width : (chunk + 1) * width]
-        own_ref[...] = own_total[rows, :] + product_back(mate_rows, mate_weight_ref[0])
-
-
-def back(table, m, here, weight, for_mate, chunks, after=()):
-    nodes, width = here.shape
+    here_copy = remote(here_hbm.at[m], mixed_ref.at[1], 0)
+    weight_copy = remote(for_mate_hbm, mate_weight_ref, 1)
+
+    def there_copy(i):
+        return remote(mixed_ref.at[2, at(i, WIDE)], mixed_ref.at[3, at(i, WIDE)], 2 + i)
+
+    def pre_copy(i):
+        return remote(pre_ref.at[at(i, TILE)], mate_pre_ref.at[at(i, TILE)], 2 + wide + i)
+
+    loads[0].start()
+    matrix_load(0).start()
+    loads[1].start()
+    for i in range(1, wide):
+        matrix_load(i).start()
+    for item in loads[2:]:
+        item.start()
+    greet_mate(mate)
+    here_copy.start()
+    loads[0].wait()
+    loads[1].wait()
+
+    @pl.loop(0, wide)
+    def _(i):
+        matrix_load(i).wait()
+        rows = at(i, WIDE)
+        there = product_rows(matrix_ref[:, rows], far_ref[...])
+        mixed_ref[2, rows, :] = scaled(there, scale_ref[rows, :]).astype(BF16)
+        there_copy(i).start()
+
+    weight_copy.start()
+    for item in loads[2:5]:
+        item.wait()
+    here_copy.wait_recv()
+    bias_sum_ref[...] = bias_sum_in[...] if m else jnp.zeros_like(bias_sum_ref)
+
+    @pl.loop(0, narrow)
+    def _(i):
+        @pl.when(i % (WIDE // TILE) == 0)
+        def _():
+            there_copy(i // (WIDE // TILE)).wait_recv()
+
+        rows = at(i, TILE)
+        preact = bias_ref[...]
+        for block in range(4):
+            preact = preact + product(mixed_ref[block, rows, :], weight_ref[block])
+        row_ids = i * TILE + lax.broadcasted_iota(jnp.int32, preact.shape, 0)
+        live = row_ids < table_ref[LIMITS + m]
+        gate = jax.nn.sigmoid(preact)
+        out_ref[rows, :] = jnp.where(live, preact * gate, 0.0).astype(BF16)
+        slope = gate * (1.0 + preact * (1.0 - gate))
+        grad_pre = jnp.where(live, grad_ref[rows, :].astype(F32) * slope, 0.0).astype(BF16)
+        pre_ref[rows, :] = grad_pre
+        pre_copy(i).start()
+        bias_sum_ref[...] += jnp.sum(grad_pre.astype(F32), axis=0, keepdims=True)
+
+    stores = [pltpu.make_async_copy(out_ref, out_hbm, store.at[0])]
+    stores[0].start()
+    weight_copy.wait_recv()
+
+    @pl.loop(0, wide)
+    def _(i):
+        for part in range(WIDE // TILE):
+            pre_copy(i * (WIDE // TILE) + part).wait_recv()
+        rows = at(i, WIDE)
+        here, there = pre_ref[rows, :], mate_pre_ref[rows, :]
+        away = product_back(here, weight_ref[2]) + product_back(there, mate_weight_ref[1])
+        away_ref[rows, :] = away.astype(BF16)
+        own_ref[rows, :] = product_back(here, weight_ref[0]) + product_back(there, mate_weight_ref[0])
+
     step = width // chunks
-    down = lambda h, i: (i * h, 0)
+    for chunk in range(chunks):
+        stores.append(
+            pltpu.make_async_copy(
+                away_ref.at[:, chunk * step : (chunk + 1) * step], away_hbm[chunk], store.at[1 + chunk]
+            )
+        )
+    stores.append(pltpu.make_async_copy(own_ref, own_hbm, store.at[1 + chunks]))
+    for item in stores[1:]:
+        item.start()
+
+    if m:
+        loads[5].wait()
+
+    @pl.loop(0, 4)
+    def _(block):
+        term = product_rows(mixed_ref[block], pre_ref[...])
+        total_ref[block] = total_ref[block] + term if m else term
+
+    if ended:
+        quarter = width // 4
+        upper = lax.axis_index("clus") % 2 == 1
+        column = lax.axis_index("col")
+        for block in range(4):
+            source = partner(column, 1) if block % 2 else column
+            source = partner(source, 2) if block >= 2 else source
+            rows = at(source, width)
+            for chunk in range(2):
+                low = total_ref[block, :, chunk * quarter : (chunk + 1) * quarter]
+                high = total_ref[block, :, (2 + chunk) * quarter : (3 + chunk) * quarter]
+                results[chunk][rows, :] = jnp.where(upper, high, low)
+                results[2 + chunk][rows, :] = jnp.where(upper, low, high).astype(BF16)
+    else:
+        stores.append(pltpu.make_async_copy(total_ref, results[0], store.at[2 + chunks]))
+        stores[-1].start()
+    here_copy.wait_send()
+    weight_copy.wait_send()
+    for i in range(wide):
+        there_copy(i).wait_send()
+    for i in range(narrow):
+        pre_copy(i).wait_send()
+    for item in stores:
+        item.wait()
+
+
+def batch(table, m, matrix, scale, far, here, weight, for_mate, out_grad, bias, total, bias_sum, chunks, after=()):
+    nodes, width = far.shape
+    wide, narrow = nodes // WIDE, nodes // TILE
+    quarter = width // 4
+    flat = lambda i: (0, 0)
+    ended = m == MB - 1
+    if ended:
+        results = [((D, quarter), F32, (D, quarter), flat)] * 2 + [((D, quarter), BF16, (D, quarter), flat)] * 2
+    else:
+        results = [((4, width, width), F32, None, None)]
     return launch(
-        f"back{m}", functools.partial(back_kernel, chunks), table,
-        [
-            (here, None, None),
-            (for_mate, None, None),
-            (here, (WIDE, width), lambda h, i: (i * (1 - h) + h * (nodes // WIDE - 1), 0)),
-            (weight, weight.shape, lambda h, i: (0, 0, 0)),
+        f"batch{m}", functools.partial(batch_kernel, m, chunks), table,
+        [(array, None, None) for array in (matrix, scale, far, here, weight, for_mate, out_grad)]
+        + [(bias, (1, width), flat)]
+        + ([(total, None, None), (bias_sum, (1, width), flat)] if m else []),
+        [((nodes, width), BF16, None, None), ((nodes, width), F32, None, None)]
+        + [((nodes, width // chunks), BF16, None, None)] * chunks
+        + results
+        + [((1, width), F32, (1, width), flat)],
+        after=after, barrier=BATCH_ID + m,
+        scratch=[
+            pltpu.VMEM((nodes, nodes), BF16),
+            pltpu.VMEM((nodes, LANES), F32),
+            pltpu.VMEM((nodes, width), BF16),
+            pltpu.VMEM((4, nodes, width), BF16),
+            pltpu.VMEM(weight.shape, BF16),
+            pltpu.VMEM(for_mate.shape, BF16),
+            pltpu.VMEM((nodes, width), BF16),
+            pltpu.VMEM((nodes, width), BF16),
+            pltpu.VMEM((nodes, width), BF16),
+            pltpu.VMEM((nodes, width), BF16),
+            pltpu.VMEM((nodes, width), F32),
+            pltpu.VMEM((nodes, width), BF16),
+            pltpu.VMEM((4, width, width), F32),
+            pltpu.SemaphoreType.DMA((wide + 6,)),
+            pltpu.SemaphoreType.DMA((3 + chunks,)),
+            pltpu.SemaphoreType.DMA((2 + wide + narrow,)),
+            pltpu.SemaphoreType.DMA((2 + wide + narrow,)),
         ],
-        [((nodes, width), F32, (WIDE, width), down)]
-        + [((nodes, step), BF16, (WIDE, step), down) for _ in range(chunks)],
-        grid=(2, nodes // WIDE), after=after, barrier=BACK_ID + m,
-        scratch=[
-            pltpu.VMEM((nodes, width), BF16),
-            pltpu.VMEM(for_mate.shape, BF16),
-            pltpu.VMEM((nodes, width), F32),
-            pltpu.VMEM((nodes, width), F32),
-            pltpu.SemaphoreType.DMA((2,)),
-            pltpu.SemaphoreType.DMA((2,)),
-        ],
-    )
+    )
+
+
+def collect_kernel(table_ref, *refs):
+    sources, out_ref, semaphore = refs[:MB], refs[MB], refs[MB + 1]
+    copies = [pltpu.make_async_copy(sources[m], out_ref.at[m], semaphore.at[m]) for m in range(MB)]
+    for item in copies:
+        item.start()
+    for item in copies:
+        item.wait()
+
+
+def collect(table, arrays, after=()):
+    return launch(
+        "collect", collect_kernel, table,
+        [(array, None, None) for array in arrays],
+        [((MB, *arrays[0].shape), arrays[0].dtype, None, None)],
+        after=after, scratch=[pltpu.SemaphoreType.DMA((MB,))],
+    )[0]
 
 
 def scatter_kernel(table_ref, own_ref, got_ref, scale_ref, matrix_ref, out_ref, sum_ref):
@@ -581,67 +615,6 @@
         grid=(nodes // WIDE,), after=after, alias=None if grads is None else (grads, 0),
         scratch=[pltpu.VMEM((nodes, step), BF16)],
     )[0]
-
-
-def weight_kernel(parts, table_ref, *refs):
-    blocks = 4
-    mixed_refs, pre_refs = refs[: MB * blocks], refs[MB * blocks : MB * blocks + MB]
-    bias_refs = refs[MB * blocks + MB : MB * blocks + 2 * MB]
-    keep_refs, sent_refs = refs[MB * blocks + 2 * MB :][:2], refs[MB * blocks + 2 * MB + 2 : -2]
-    bias_out_ref, total_ref = refs[-2:]
-    step = pl.program_id(0)
-
-    for m in range(MB):
-
-        @pl.when(step // parts == m)
-        def _(m=m):
-            for block in range(blocks):
-                source = mixed_refs[m * blocks + block]
-                term = product_rows(source[0] if block == 0 else source[...], pre_refs[m][...])
-                if m == 0:
-                    term = jnp.where(step == 0, term, total_ref[block] + term)
-                else:
-                    term = total_ref[block] + term
-                total_ref[block] = term
-
-    @pl.when(step == parts * MB - 1)
-    def _():
-        bias_out_ref[...] = sum(ref[...] for ref in bias_refs)
-        width = total_ref.shape[1]
-        quarter = width // 4
-        upper = (table_ref[GROUP] & 1) == 1
-        for block in range(blocks):
-            rows = pl.ds(pl.multiple_of((table_ref[COLUMN] ^ block) * width, width), width)
-            for chunk in range(2):
-                low = total_ref[block, :, chunk * quarter : (chunk + 1) * quarter]
-                high = total_ref[block, :, (2 + chunk) * quarter : (3 + chunk) * quarter]
-                keep_refs[chunk][rows, :] = jnp.where(upper, high, low)
-                sent_refs[chunk][rows, :] = jnp.where(upper, low, high).astype(BF16)
-
-
-def weight_gradient(table, here, mixed, pres, biases, after=()):
-    nodes, width = pres[0].shape
-    parts = 2
-    rows, quarter = nodes // parts, width // 4
-
-    def turn(m):
-        return lambda i: (jnp.clip(i - m * parts, 0, parts - 1), 0)
-
-    whole = lambda i: (0, 0)
-    ins = []
-    for m in range(MB):
-        ins.append((here, (1, rows, width), lambda i, m=m: (m, *turn(m)(i))))
-        ins += [(part, (rows, width), turn(m)) for part in mixed[m]]
-    return launch(
-        "weight", functools.partial(weight_kernel, parts), table,
-        ins
-        + [(pres[m], (rows, width), turn(m)) for m in range(MB)]
-        + [(bias, (1, width), whole) for bias in biases],
-        [((D, quarter), F32, (D, quarter), whole)] * 2
-        + [((D, quarter), BF16, (D, quarter), whole)] * 2
-        + [((1, width), F32, (1, width), whole)],
-        grid=(parts * MB,), after=after, scratch=[pltpu.VMEM((4, width, width), F32)],
-    )
 
 
 def sum_kernel(groups, capacity, table_ref, *refs):
@@ -869,28 +842,25 @@
     )
     weight, for_mate = place(table, slots, [here])
     last = for_mate
-    outputs, input_grads = None, None
-    mixed, pres, biases, own, away = [], [], [], [], []
+    input_grads, total, bias_sum = None, None, None
+    outputs, own, away = [], [], []
     for m in range(MB):
-        there, here_mate, there_mate = mix(table, m, matrix, scale, far[m], here, [last])
-        mixed.append([here_mate, there, there_mate])
-        outputs, grad_pre, bias_sum = layer(
-            table, m, here, mixed[m], weight, bias_row, out_grad, outputs, [there]
-        )
-        pres.append(grad_pre)
-        biases.append(bias_sum)
-        own_m, *away_m = back(table, m, grad_pre, weight, for_mate, 2 if m == MB - 1 else 1, [bias_sum])
+        chunks = 2 if m == MB - 1 else 1
+        out_m, own_m, *rest = batch(
+            table, m, matrix, scale, far[m], here, weight, for_mate, out_grad, bias_row, total, bias_sum, chunks,
+            [last],
+        )
+        outputs.append(out_m)
         own.append(own_m)
-        away.append([flip(chunk, "col", 2) for chunk in away_m])
-        last = own_m
-
-    keep_low, keep_high, sent_low, sent_high, bias_sum = weight_gradient(
-        table, here, mixed, pres, biases, [last]
-    )
+        away.append([flip(chunk, "col", 2) for chunk in rest[:chunks]])
+        total, bias_sum = rest[chunks], rest[-1]
+        last = bias_sum
+
+    keep_low, keep_high, sent_low, sent_high, bias_sum = rest[chunks:]
     *rows, bias_total = sum_over_owners(
         table, groups, capacity, (keep_low, keep_high), (sent_low, sent_high), bias_sum, [last]
     )
-    last = bias_total
+    last = outputs = collect(table, outputs, [bias_total])
     for m in range(MB):
         if m == MB - 1:
             updated = adamw(

time: 283 us -> 240 us (0.85)
  Pallas kernels: 261 us -> 218 us
    pallas_call x21 -> x15, Pallas kernels: 261 us -> 218 us  [launch(): pl.pallas_call(kernel, grid_spec=pltpu.PrefetchScalarGridSpec(num_scalar_...]
    unnamed x48 -> x32, local copies, waits for them, and re-layouts: 8.69 us -> 7.65 us
  transfers between devices with their start and end apart: 7 -> 7, of which waited for: 0 -> 0; matrix products, arithmetic and copies ran while one was open for 0% -> 0% of each run, Pallas kernels for 90% -> 88%
where the time goes in v3:
time: 240 us; the launch traced here: 238 us
  Pallas kernels  218 us (91%)
  starting transfers between devices  9.31 us (4%)
  local copies, waits for them, and re-layouts  8.4 us (4%)
    pallas_call x15, Pallas kernels, launch(): pl.pallas_call(kernel, grid_spec=pltpu.PrefetchScalarGridSpec(num_scalar_...  218 us
    ppermute x7, starting transfers between devices, flip(): return lax.ppermute(values, axis, [(i, i ^ bit) for i in range(size)])  9.31 us
    unnamed x32, local copies, waits for them, and re-layouts  7.65 us
  transfers between devices with their start and end apart: 7, of which 0 were waited for; matrix products, arithmetic and copies ran while one was open for 0% of the time, Pallas kernels for 88%

profile of v3, /device:TPU:0, one launch (start us, length us, event | category | flops | bytes accessed | tf_op | source)
XLA Modules:
  0.0 237.5 jit_solution(16730189704834211708)
XLA Ops:
  0.6 0.8 select_reduce_fusion
  1.4 0.7 concatenate.3.table_ref
  2.2 2.0 pick0.1.refs_1_
  4.1 3.0 %collective-permute-start = (bf16[1536,512]{1,0:T(8,128)(2,1)S(1)}, bf16[1536,512]{1,0:T(8,128)(2,1)S(1)}, u32[]{:S(2)}, u32[]{:S(2)}) collective-permute-start(bf16[1536,512]{1,0:T(8,128)(2,1)S(1)} %pick0.1.refs_1_), channel_id=1, source_target_pairs={{0,2},{1,3},{2,0},{3,1},{4,6},{5,7},{6,4},{7,5},{8,10},{9,11},{10,... | collective-permute-start | bytes 4718600 | tf_op jit(solution)/shard_map/ppermute | solution.py:71
  7.2 2.0 pick1.1.refs_1_
  9.1 0.0 copy-start.3
  9.1 0.0 copy-start.12
  9.1 0.1 collective-permute-start.1
  9.2 2.0 pick2.1.refs_3_
  11.2 2.1 collective-permute-start.2
  13.3 0.0 copy-done.3
  13.3 0.0 copy-done.12
  13.3 52.0 %front.1 = (bf16[3,1536,1536]{2,1,0:T(8,128)(2,1)}, f32[3,1536,128]{2,1,0:T(8,128)S(1)}, bf16[3,1536,512]{2,1,0:T(8,128)(2,1)}, bf16[8,512,512]{2,1,0:T(8,128)(2,1)}) custom-call(s32[21]{0:T(128)S(1)} %concatenate.3.table_ref, f32[512,512]{1,0:T(8,128)S(1)} %copy-done.3, s32[3,16,1536]{2,1,0:T(8,128)S(1)} %bitcast.10, bf16[3,1536,512]{2,1,0:T(8,128)(2,1)} %refs_2_.1, ...), custom_call_target="tpu_custom_call" | custom-call | flops 1 | bytes 1 | tf_op jit(solution)/shard_map/front/pallas_call | solution.py:49
  65.3 0.0 copy-start
  65.3 1.4 copy-done
  66.7 0.0 copy-start.13
  66.7 8.3 %place.1 = (bf16[4,512,512]{2,1,0:T(8,128)(2,1)S(1)}, bf16[2,512,512]{2,1,0:T(8,128)(2,1)S(1)}) custom-call(s32[21]{0:T(128)S(1)} %concatenate.3.table_ref, bf16[8,512,512]{2,1,0:T(8,128)(2,1)} %get-tuple-element.47.refs_0_, bf16[3,1536,512]{2,1,0:T(8,128)(2,1)} %get-tuple-element.46.refs_1_.refs_3_), custom_call_target="tpu_custom_call" | custom-call | flops 1 | bytes 1 | tf_op jit(solution)/shard_map/place/pallas_call | solution.py:49
  75.0 0.0 copy-start.2
  75.0 1.3 copy-done.2
  76.3 0.0 collective-permute-done.refs_2_
  76.3 0.0 copy-done.13
  76.3 21.2 %batch0.1 = (bf16[1536,512]{1,0:T(8,128)(2,1)S(1)}, f32[1536,512]{1,0:T(8,128)}, bf16[1536,512]{1,0:T(8,128)(2,1)}, f32[4,512,512]{2,1,0:T(8,128)}, f32[1,512]{1,0:T(1,128)S(1)}) custom-call(s32[21]{0:T(128)S(1)} %concatenate.3.table_ref, bf16[3,1536,1536]{2,1,0:T(8,128)(2,1)} %get-tuple-element.44.refs_0_.refs_3_, f32[3,1536,128]{2,1,0:T(8,128)} %copy-done, ...), custom_call_target="tpu_custom_call" | custom-call | flops 1 | bytes 1 | tf_op jit(solution)/shard_map/batch0/pallas_call | solution.py:49
  97.6 0.0 copy-start.4
  97.6 1.1 copy-done.4
  98.7 0.5 collective-permute-start.6
  99.2 0.0 collective-permute-done.1.refs_2_
  99.2 21.2 %batch1.1 = (bf16[1536,512]{1,0:T(8,128)(2,1)S(1)}, f32[1536,512]{1,0:T(8,128)}, bf16[1536,512]{1,0:T(8,128)(2,1)}, f32[4,512,512]{2,1,0:T(8,128)}, f32[1,512]{1,0:T(1,128)S(1)}) custom-call(s32[21]{0:T(128)S(1)} %concatenate.3.table_ref, bf16[3,1536,1536]{2,1,0:T(8,128)(2,1)} %get-tuple-element.44.refs_0_.refs_3_, f32[3,1536,128]{2,1,0:T(8,128)} %copy-done, ...), custom_call_target="tpu_custom_call" | custom-call | flops 1 | bytes 1 | tf_op jit(solution)/shard_map/batch1/pallas_call | solution.py:49
  120.4 0.0 copy-start.6
  120.5 1.1 copy-done.6
  121.6 1.5 collective-permute-start.5
  123.1 0.0 collective-permute-done.2.refs_2_
  123.1 19.9 %batch2.1 = (bf16[1536,512]{1,0:T(8,128)(2,1)}, f32[1536,512]{1,0:T(8,128)}, bf16[1536,256]{1,0:T(8,128)(2,1)}, bf16[1536,256]{1,0:T(8,128)(2,1)}, f32[2048,128]...) custom-call(s32[21]{0:T(128)S(1)} %concatenate.3.table_ref, ...), custom_call_target="tpu_custom_call" | custom-call | flops 1 | bytes 1 | tf_op jit(solution)/shard_map/batch2/pallas_call | solution.py:49
  143.1 0.0 copy-start.5
  143.1 0.0 copy-start.7
  143.1 0.6 collective-permute-start.4
  143.6 1.5 collective-permute-start.3
  145.2 55.7 %sum.1 = (f32[512,128]{1,0:T(8,128)S(1)}, f32[512,128]{1,0:T(8,128)S(1)}, bf16[512,128]{1,0:T(8,128)(2,1)S(1)}, bf16[512,128]{1,0:T(8,128)(2,1)S(1)}, f32[1,512]{1,0:T(1,128)S(1)}) custom-call(s32[21]{0:T(128)S(1)} %concatenate.3.table_ref, f32[2048,128]{1,0:T(8,128)S(1)} %get-tuple-element.57.refs_0_, f32[2048,128]{1,0:T(8,128)S(1)} %get-tuple-element.58.refs_1_, ...), custom_call_target="tpu_custom_call" | custom-call | flops 1 | bytes 1 | tf_op jit(solution)/shard_map/sum/pallas_call | solution.py:49
  200.8 0.0 copy-done.5
  200.8 0.0 copy-done.7
  200.9 0.0 copy-start.8
  200.9 1.4 copy-done.8
  202.3 0.0 copy-start.1
  202.3 2.7 %collect.1.refs_4_ = bf16[3,1536,512]{2,1,0:T(8,128)(2,1)} custom-call(s32[21]{0:T(128)S(1)} %concatenate.3.table_ref, bf16[1536,512]{1,0:T(8,128)(2,1)S(1)} %copy-done.5, bf16[1536,512]{1,0:T(8,128)(2,1)S(1)} %copy-done.7, bf16[1536,512]{1,0:T(8,128)(2,1)S(1)} %copy-done.8, f32[1,512]{1,0:T(1,128)S(1)} %get-tuple-element.62.refs_3_.refs_4_), custom_call_target="tpu_custom_call" | custom-call | flops 1 | bytes 1 | tf_op jit(solution)/shard_map/collect/pallas_call | solution.py:49
  205.0 0.0 collective-permute-done.6.refs_1_
  205.0 0.0 copy-done.1
  205.0 7.8 %scatter0_0.1.refs_4_ = bf16[3,1536,512]{2,1,0:T(8,128)(2,1)} custom-call(s32[21]{0:T(128)S(1)} %concatenate.3.table_ref, f32[1536,512]{1,0:T(8,128)} %get-tuple-element.68.refs_0_, bf16[1536,512]{1,0:T(8,128)(2,1)S(1)} %collective-permute-done.6.refs_1_, f32[3,1536,128]{2,1,0:T(8,128)S(1)} %copy-done.1, ...), custom_call_target="tpu_custom_call" | custom-call | flops 1 | bytes 1 | tf_op jit(solution)/shard_map/scatter0_0/pallas_call | solution.py:49
  212.8 0.0 collective-permute-done.5.refs_1_
  212.8 0.0 copy-start.9
  212.8 0.0 copy-start.10
  212.9 0.0 copy-start.14
  212.9 0.0 copy-start.15
  212.9 7.9 %scatter1_0.1.refs_11_.refs_4_ = bf16[3,1536,512]{2,1,0:T(8,128)(2,1)} custom-call(s32[21]{0:T(128)S(1)} %concatenate.3.table_ref, f32[1536,512]{1,0:T(8,128)} %get-tuple-element.66.refs_0_, bf16[1536,512]{1,0:T(8,128)(2,1)S(1)} %collective-permute-done.5.refs_1_, f32[3,1536,128]{2,1,0:T(8,128)S(1)} %copy-done.1, ...), custom_call_target="tpu_custom_call", output_to_operand_aliasing={{}: (5, {})} | custom-call | flops 1 | bytes 1 | tf_op jit(solution)/shard_map/scatter1_0/pallas_call | solution.py:49
  220.7 0.0 copy-done.9
  220.7 0.0 copy-done.10
  220.7 0.0 copy-done.14
  220.7 0.0 copy-done.15
  220.8 3.2 %adamw.1 = (f32[512,512]{1,0:T(8,128)}, f32[512,512]{1,0:T(8,128)}, f32[512,512]{1,0:T(8,128)}, f32[1,512]{1,0:T(1,128)}, f32[1,512]{1,0:T(1,128)}, /*index=5*/f32[1,512]{1,0:T(1,128)}) custom-call(s32[21]{0:T(128)S(1)} %concatenate.3.table_ref, f32[512,128]{1,0:T(8,128)S(1)} %get-tuple-element.70.refs_0_, f32[512,128]{1,0:T(8,128)S(1)} %get-tuple-element.71.refs_1_, ...), custom_call_target="tpu_custom_call" | custom-call | flops 1 | bytes 1 | tf_op jit(solution)/shard_map/adamw/pallas_call | solution.py:49
  223.9 0.0 collective-permute-done.4.refs_1_
  223.9 0.0 copy-start.11
  223.9 1.2 copy-done.11
  225.1 6.3 %scatter2_0.1.refs_4_ = bf16[3,1536,512]{2,1,0:T(8,128)(2,1)} custom-call(s32[21]{0:T(128)S(1)} %concatenate.3.table_ref, f32[1536,512]{1,0:T(8,128)} %get-tuple-element.63.refs_0_, bf16[1536,256]{1,0:T(8,128)(2,1)} %collective-permute-done.4.refs_1_, f32[3,1536,128]{2,1,0:T(8,128)S(1)} %copy-done.1, ...), custom_call_target="tpu_custom_call", output_to_operand_aliasing={{}: (5, {})} | custom-call | flops 1 | bytes 1 | tf_op jit(solution)/shard_map/scatter2_0/pallas_call | solution.py:49
  231.4 0.0 collective-permute-done.3.refs_1_
  231.4 6.1 %scatter2_1.1 = bf16[3,1536,512]{2,1,0:T(8,128)(2,1)} custom-call(s32[21]{0:T(128)S(1)} %concatenate.3.table_ref, f32[1536,512]{1,0:T(8,128)} %get-tuple-element.63.refs_0_, bf16[1536,256]{1,0:T(8,128)(2,1)S(1)} %collective-permute-done.3.refs_1_, f32[3,1536,128]{2,1,0:T(8,128)S(1)} %copy-done.1, ...), custom_call_target="tpu_custom_call", output_to_operand_aliasing={{}: (5, {})} | custom-call | flops 1 | bytes 1 | tf_op jit(solution)/shard_map/scatter2_1/pallas_call | solution.py:49
Async XLA Ops:
  4.1 72.2 %collective-permute-start = (bf16[1536,512]{1,0:T(8,128)(2,1)S(1)}, bf16[1536,512]{1,0:T(8,128)(2,1)S(1)}, u32[]{:S(2)}, u32[]{:S(2)}) collective-permute-start(bf16[1536,512]{1,0:T(8,128)(2,1)S(1)} %pick0.1.refs_1_), channel_id=1, source_target_pairs={{0,2},{1,3},{2,0},{3,1},{4,6},{5,7},{6,4},{7,5},{8,10},{9,11},{10,... | collective-permute-start | bytes 4718600 | tf_op jit(solution)/shard_map/ppermute | solution.py:71
  9.1 4.1 %copy-start.3 = (f32[512,512]{1,0:T(8,128)S(1)}, f32[512,512]{1,0:T(8,128)}, u32[]{:S(2)}) copy-start(f32[512,512]{1,0:T(8,128)} %refs_5_.1) | copy-start | bytes 3145732
  9.1 4.1 %copy-start.12 = (s32[3,1536,16]{1,2,0:T(8,128)S(1)}, s32[3,1536,16]{1,2,0:T(8,128)}, u32[]{:S(2)}) copy-start(s32[3,1536,16]{1,2,0:T(8,128)} %param.12) | copy-start | bytes 884740
  9.1 90.1 %collective-permute-start.1 = (bf16[1536,512]{1,0:T(8,128)(2,1)S(1)}, bf16[1536,512]{1,0:T(8,128)(2,1)S(1)}, u32[]{:S(2)}, u32[]{:S(2)}) collective-permute-start(bf16[1536,512]{1,0:T(8,128)(2,1)S(1)} %pick1.1.refs_1_), channel_id=1, source_target_pairs={{0,2},{1,3},{2,0},{3,1},{4,6},{5,7},{6,4},{7,5},{8,10},{9,11},{10,... | collective-permute-start | bytes 4718600 | tf_op jit(solution)/shard_map/ppermute | solution.py:71
  11.2 111.9 %collective-permute-start.2 = (bf16[1536,512]{1,0:T(8,128)(2,1)S(1)}, bf16[1536,512]{1,0:T(8,128)(2,1)}, u32[]{:S(2)}, u32[]{:S(2)}) collective-permute-start(bf16[1536,512]{1,0:T(8,128)(2,1)S(1)} %pick2.1.refs_3_), channel_id=1, source_target_pairs={{0,2},{1,3},{2,0},{3,1},{4,6},{5,7},{6,4},{7,5},{8,10},{9,11},{10,... | collective-permute-start | bytes 4718600 | tf_op jit(solution)/shard_map/ppermute | solution.py:71
  65.3 1.4 copy-start
  66.7 9.6 %copy-start.13 = (f32[512]{0:T(512)S(1)}, f32[512]{0:T(512)}, u32[]{:S(2)}) copy-start(f32[512]{0:T(512)} %param.18) | copy-start | bytes 6148
  75.0 1.3 copy-start.2
  97.6 1.1 copy-start.4
  98.7 106.3 %collective-permute-start.6 = (bf16[1536,512]{1,0:T(8,128)(2,1)}, bf16[1536,512]{1,0:T(8,128)(2,1)S(1)}, u32[]{:S(2)}, u32[]{:S(2)}) collective-permute-start(bf16[1536,512]{1,0:T(8,128)(2,1)} %get-tuple-element.69), channel_id=1, source_target_pairs={{0,2},{1,3},{2,0},{3,1},{4,6},{5,7},{6,4},{7,5},{8,10},{9,11},{10,... | collective-permute-start | bytes 4718600 | tf_op jit(solution)/shard_map/ppermute | solution.py:71
  120.4 1.1 copy-start.6
  121.6 91.3 %collective-permute-start.5 = (bf16[1536,512]{1,0:T(8,128)(2,1)}, bf16[1536,512]{1,0:T(8,128)(2,1)S(1)}, u32[]{:S(2)}, u32[]{:S(2)}) collective-permute-start(bf16[1536,512]{1,0:T(8,128)(2,1)} %get-tuple-element.67), channel_id=1, source_target_pairs={{0,2},{1,3},{2,0},{3,1},{4,6},{5,7},{6,4},{7,5},{8,10},{9,11},{10,... | collective-permute-start | bytes 4718600 | tf_op jit(solution)/shard_map/ppermute | solution.py:71
  143.1 57.8 %copy-start.5 = (bf16[1536,512]{1,0:T(8,128)(2,1)S(1)}, bf16[1536,512]{1,0:T(8,128)(2,1)}, u32[]{:S(2)}) copy-start(bf16[1536,512]{1,0:T(8,128)(2,1)} %copy-done.4) | copy-start | bytes 4718596
  143.1 57.8 %copy-start.7 = (bf16[1536,512]{1,0:T(8,128)(2,1)S(1)}, bf16[1536,512]{1,0:T(8,128)(2,1)}, u32[]{:S(2)}) copy-start(bf16[1536,512]{1,0:T(8,128)(2,1)} %copy-done.6) | copy-start | bytes 4718596
  143.1 80.8 %collective-permute-start.4 = (bf16[1536,256]{1,0:T(8,128)(2,1)}, bf16[1536,256]{1,0:T(8,128)(2,1)}, u32[]{:S(2)}, u32[]{:S(2)}) collective-permute-start(bf16[1536,256]{1,0:T(8,128)(2,1)} %get-tuple-element.65), channel_id=1, source_target_pairs={{0,2},{1,3},{2,0},{3,1},{4,6},{5,7},{6,4},{7,5},{8,10},{9,11},{10,... | collective-permute-start | bytes 2359304 | tf_op jit(solution)/shard_map/ppermute | solution.py:71
  143.6 87.8 %collective-permute-start.3 = (bf16[1536,256]{1,0:T(8,128)(2,1)}, bf16[1536,256]{1,0:T(8,128)(2,1)S(1)}, u32[]{:S(2)}, u32[]{:S(2)}) collective-permute-start(bf16[1536,256]{1,0:T(8,128)(2,1)} %get-tuple-element.64), channel_id=1, source_target_pairs={{0,2},{1,3},{2,0},{3,1},{4,6},{5,7},{6,4},{7,5},{8,10},{9,11},{10,... | collective-permute-start | bytes 2359304 | tf_op jit(solution)/shard_map/ppermute | solution.py:71
  200.9 1.4 copy-start.8
  202.3 2.8 %copy-start.1 = (f32[3,1536,128]{2,1,0:T(8,128)S(1)}, f32[3,1536,128]{2,1,0:T(8,128)}, u32[]{:S(2)}) copy-start(f32[3,1536,128]{2,1,0:T(8,128)} %copy-done) | copy-start | bytes 7077892
  212.8 7.9 %copy-start.9 = (f32[512,512]{1,0:T(8,128)S(1)}, f32[512,512]{1,0:T(8,128)}, u32[]{:S(2)}) copy-start(f32[512,512]{1,0:T(8,128)} %refs_6_.7) | copy-start | bytes 3145732
  212.8 7.9 %copy-start.10 = (f32[512,512]{1,0:T(8,128)S(1)}, f32[512,512]{1,0:T(8,128)}, u32[]{:S(2)}) copy-start(f32[512,512]{1,0:T(8,128)} %refs_7_.1) | copy-start | bytes 3145732
  212.9 7.9 %copy-start.14 = (f32[512]{0:T(512)S(1)}, f32[512]{0:T(512)}, u32[]{:S(2)}) copy-start(f32[512]{0:T(512)} %param.19) | copy-start | bytes 6148
  212.9 7.9 %copy-start.15 = (f32[512]{0:T(512)S(1)}, f32[512]{0:T(512)}, u32[]{:S(2)}) copy-start(f32[512]{0:T(512)} %param.20) | copy-start | bytes 6148
  223.9 1.2 copy-start.11

commit v4 on v3

v4 whole, which is shorter than its diff:
```python
import functools

import jax
import jax.numpy as jnp
from jax import lax
from jax.experimental import pallas as pl
from jax.experimental.pallas import tpu as pltpu
from jax.sharding import PartitionSpec as P

D = 2048
MB = 3
STEP = 10

BETA_ONE = 0.9
BETA_TWO = 0.95
EPSILON = 1e-08
DECAY = 0.1
RATE_WEIGHT = 0.06
RATE_BIAS = 0.6

LANES = 128
DIGIT_BITS = 5
DIGITS = 6
STRIP = 32
SUBLANES = 8
TILE = 256
WIDE = 512
HALVES = 2
PIECES = 4
UNROLL = 3
CHUNKS = 8
MIB = 1024 * 1024
SMALL = 1 << 16

GROUP, COLUMN, LIMITS = 0, 1, 2
STARTS = LIMITS + MB

FRONT_ID, SUM_ID, BATCH_ID = 1, 2, 3

F32, BF16 = jnp.float32, jnp.bfloat16


class Kept:
    def __init__(self, array, space=pltpu.VMEM):
        self.array, self.space = array, space


def located(item):
    if isinstance(item, Kept):
        return pltpu.with_memory_space_constraint(item.array, item.space) if item.space else item.array
    return pltpu.with_memory_space_constraint(item, pltpu.HBM) if item.size > SMALL else item


def launch(name, body, table, ins, outs, grid=(1,), after=(), alias=None, scratch=(), barrier=None, vmem=16):
    tables = [] if table is None else [table]

    def spec(block, index):
        if block is None:
            return pl.BlockSpec(memory_space=pl.ANY)
        return pl.BlockSpec(block, lambda *a: index(*a[: len(grid)]))

    unread = ([alias[0]] if alias else []) + [array for array in after if alias is None or array is not alias[0]]

    def kernel(*refs):
        table_refs, refs = refs[: len(tables)], refs[len(tables) :]
        body(*table_refs, *refs[: len(ins)], *refs[len(ins) + len(unread) :])

    return pl.pallas_call(
        kernel,
        grid_spec=pltpu.PrefetchScalarGridSpec(
            num_scalar_prefetch=len(tables),
            grid=grid,
            in_specs=[spec(block, index) for _, block, index in ins]
            + [pl.BlockSpec(memory_space=pl.ANY)] * len(unread),
            out_specs=[spec(out[2], out[3]) for out in outs],
            scratch_shapes=list(scratch),
        ),
        out_shape=[
            pltpu.HBM(out[0], out[1]) if out[2] is None else (out[4] if len(out) > 4 else jax.ShapeDtypeStruct)(out[0], out[1])
            for out in outs
        ],
        input_output_aliases={len(tables) + len(ins): alias[1]} if alias else {},
        compiler_params=pltpu.CompilerParams(
            vmem_limit_bytes=vmem * MIB, collective_id=barrier, has_side_effects=barrier is not None
        ),
        cost_estimate=pl.CostEstimate(flops=1, bytes_accessed=1, transcendentals=0),
        name=name,
    )(*tables, *(located(item[0]) for item in ins), *(located(item) for item in unread))


def flip(values, axis, bit):
    size = lax.axis_size(axis)
    return lax.ppermute(values, axis, [(i, i ^ bit) for i in range(size)])


def partner(index, bit):
    return index + bit * (1 - 2 * ((index // bit) % 2))


def product(left, right):
    return jnp.dot(left, right, preferred_element_type=F32)


def product_back(left, right):
    return lax.dot_general(left, right, (((1,), (1,)), ((), ())), preferred_element_type=F32)


def product_rows(left, right):
    return lax.dot_general(left, right, (((0,), (0,)), ((), ())), preferred_element_type=F32)


def scaled(values, scale):
    return values * jnp.concatenate([scale] * (values.shape[1] // LANES), axis=1)


def put_rows(ref, first, rows):
    base = pl.multiple_of((first // SUBLANES) * SUBLANES, SUBLANES)
    offset = first - base
    moved = jnp.concatenate([rows, jnp.zeros((SUBLANES, rows.shape[1]), rows.dtype)], axis=0)
    wanted = jnp.broadcast_to(offset, moved.shape)
    for bit in (1, 2, 4):
        moved = jnp.where((wanted & bit) != 0, pltpu.roll(moved, bit, 0), moved)
    head = ref[pl.ds(base, SUBLANES), :]
    row_ids = lax.broadcasted_iota(jnp.int32, head.shape, 0)
    ref[pl.ds(base, SUBLANES), :] = jnp.where(row_ids < offset, head, moved[:SUBLANES])
    ref[pl.ds(pl.multiple_of(base + SUBLANES, SUBLANES), rows.shape[0]), :] = moved[SUBLANES:]


def take_rows(ref, first, count, largest):
    bit = 1 << (largest.bit_length() - 1)
    rows = ref[...]
    while bit:
        length = count + max(bit, SUBLANES)
        if bit >= SUBLANES:
            moved = rows[bit : bit + length]
            missing = length - moved.shape[0]
            if missing:
                moved = jnp.concatenate([moved, jnp.zeros((missing, rows.shape[1]), rows.dtype)], axis=0)
        else:
            moved = pltpu.roll(rows, length - bit, 0)
        chosen = (jnp.broadcast_to(first, (length, rows.shape[1])) & bit) != 0
        rows = jnp.where(chosen, moved, rows[:length])
        bit //= 2
    return rows[:count]


def relay(sources, targets, buffers, load, store):
    def piece(ref, i):
        rows = ref.shape[0] // PIECES
        return ref.at[pl.ds(i * rows, rows)]

    loads, stores = [], []
    for number, (source, target, buffer) in enumerate(zip(sources, targets, buffers)):
        for i in range(PIECES):
            place = number * PIECES + i
            loads.append(pltpu.make_async_copy(piece(source, i), piece(buffer, i), load.at[place]))
            stores.append(pltpu.make_async_copy(piece(buffer, i), piece(target, i), store.at[place]))
    return loads, stores


def pick_kernel(batches, source_ref, *refs):
    targets, (buffer_ref, load, store) = refs[:-3], refs[-3:]
    loads, stores = relay(
        [source_ref.at[m] for m in batches], targets, [buffer_ref.at[i] for i in range(len(batches))], load, store
    )
    for item in loads:
        item.start()
    for item, onward in zip(loads, stores):
        item.wait()
        onward.start()
    for item in stores:
        item.wait()


def pick(stacked, batches, after=()):
    count = len(batches)
    return launch(
        f"pick{batches[0]}", functools.partial(pick_kernel, batches), None,
        [(stacked, None, None)], [(stacked.shape[1:], stacked.dtype, None, None)] * count,
        after=after,
        scratch=[
            pltpu.VMEM((count, *stacked.shape[1:]), stacked.dtype),
            pltpu.SemaphoreType.DMA((count * PIECES,)),
            pltpu.SemaphoreType.DMA((count * PIECES,)),
        ],
    )


def count_tile(limit, first, neighbour_ref, matrix_ref, scale_ref, lanes):
    nodes = matrix_ref.shape[1]
    words = -(-(nodes // LANES) // DIGITS)
    entries = neighbour_ref[0, :, lanes]
    node_ids = first + lax.broadcasted_iota(jnp.int32, entries.shape, 1)
    valid = (entries < limit) & (node_ids < limit)
    low = entries & (LANES - 1)
    high = entries >> 7
    digits = []
    for word in range(words):
        inside = valid & (high >= word * DIGITS) & (high < (word + 1) * DIGITS)
        shift = jnp.where(inside, (high - word * DIGITS) * DIGIT_BITS, 0)
        digits.append(jnp.where(inside, jnp.left_shift(1, shift), 0))
    for strip in range(LANES // STRIP):
        row_ids = strip * STRIP + lax.broadcasted_iota(jnp.int32, (STRIP, LANES), 0)
        sums = [jnp.zeros((STRIP, LANES), jnp.int32) for _ in range(words)]
        for entry in range(entries.shape[0]):
            hit = row_ids == low[entry : entry + 1, :]
            for word in range(words):
                sums[word] = sums[word] + jnp.where(hit, digits[word][entry : entry + 1, :], 0)
        for block in range(nodes // LANES):
            word, digit = block // DIGITS, block % DIGITS
            count = jnp.right_shift(sums[word], digit * DIGIT_BITS) & ((1 << DIGIT_BITS) - 1)
            rows = slice(block * LANES + strip * STRIP, block * LANES + (strip + 1) * STRIP)
            matrix_ref[0, rows, lanes] = count.astype(F32).astype(BF16)
    rows = pl.ds(pl.multiple_of(first, LANES), LANES)
    square = matrix_ref[0, rows, lanes].astype(F32)
    on_diagonal = lax.broadcasted_iota(jnp.int32, square.shape, 0) == lax.broadcasted_iota(jnp.int32, square.shape, 1)
    matrix_ref[0, rows, lanes] = jnp.where(on_diagonal, 2.0 * square + 2.0, square).astype(BF16)
    degree = 1.0 + jnp.sum(valid.astype(F32), axis=0, keepdims=True)
    factor = (node_ids[:1] < limit).astype(F32) / degree
    scale_ref[0, lanes, :] = jnp.transpose(jnp.broadcast_to(factor, (LANES, LANES)))


def front_kernel(
    groups, total, table_ref, master_ref, neighbour_ref, feature_ref, matrix_ref, scale_ref, mixed_ref, slots_ref,
    block_ref, local_semaphore, line_send, line_receive, pair_send, pair_receive,
):
    batch, tile_id = pl.program_id(0), pl.program_id(1)
    tiles = pl.num_programs(1)
    step = batch * tiles + tile_id
    own = lax.axis_index("clus")
    place, side = own // 2, own % 2
    pairs = groups // 2
    other = partner(own, 1)

    def rows_of(half):
        size = block_ref.shape[0] // HALVES
        return pl.ds(half * size, size)

    def remote(source, target, sent, received, device):
        return pltpu.make_async_remote_copy(
            src_ref=source,
            dst_ref=target,
            send_sem=sent,
            recv_sem=received,
            device_id={"clus": device},
            device_id_type=pl.DeviceIdType.MESH,
        )

    def origin_of(direction, hop):
        return place - 1 - hop if direction == 0 else place + 1 + hop

    def line_copy(direction, hop, half):
        slot = (place - hop if direction == 0 else place + hop) * 2 + side
        target = slots_ref.at[slot, rows_of(half)]
        return remote(
            block_ref.at[rows_of(half)] if hop == 0 else target, target,
            line_send.at[direction, hop, half], line_receive.at[direction, hop, half],
            own + 2 if direction == 0 else own - 2,
        )

    def sends(direction, hop):
        if direction == 0:
            return (place - hop >= 0) & (place + 1 < pairs)
        return (place + hop < pairs) & (place - 1 >= 0)

    def arrives(direction, hop):
        return place - 1 - hop >= 0 if direction == 0 else place + 1 + hop < pairs

    def arrival(direction, hop, half):
        target = slots_ref.at[origin_of(direction, hop) * 2 + side, rows_of(half)]
        return remote(
            target, target, line_send.at[direction, hop, half], line_receive.at[direction, hop, half], other
        )

    def pair_copy(direction, hop, half):
        slot = own if hop < 0 else origin_of(direction, hop) * 2 + side
        number = 0 if hop < 0 else 1 + 2 * hop + direction
        target = slots_ref.at[slot, rows_of(half)]
        return remote(
            block_ref.at[rows_of(half)] if hop < 0 else target, target,
            pair_send.at[number, half], pair_receive.at[number, half], other,
        )

    def pair_arrival(direction, hop, half):
        slot = other if hop < 0 else origin_of(direction, hop) * 2 + 1 - side
        number = 0 if hop < 0 else 1 + 2 * hop + direction
        target = slots_ref.at[slot, rows_of(half)]
        return remote(target, target, pair_send.at[number, half], pair_receive.at[number, half], other)

    local_copy = pltpu.make_async_copy(block_ref, slots_ref.at[own], local_semaphore)
    hops = pairs - 1

    @pl.when(step == 0)
    def _():
        barrier = pltpu.get_barrier_semaphore()

        def greet(index):
            pl.semaphore_signal(barrier, inc=1, device_id={"clus": index}, device_id_type=pl.DeviceIdType.MESH)

        greet(other)

        @pl.when(place + 1 < pairs)
        def _():
            greet(own + 2)

        @pl.when(place - 1 >= 0)
        def _():
            greet(own - 2)

        pl.semaphore_wait(barrier, 1 + jnp.where(place + 1 < pairs, 1, 0) + jnp.where(place - 1 >= 0, 1, 0))
        block_ref[...] = master_ref[...].astype(BF16)
        for half in range(HALVES):
            for direction in range(2):
                pl.when(sends(direction, 0))(line_copy(direction, 0, half).start)
            pair_copy(0, -1, half).start()
        local_copy.start()

    limit = table_ref[LIMITS + batch]
    tile = mixed_ref.shape[1]
    for part in range(tile // LANES):
        first = tile_id * tile + part * LANES
        count_tile(limit, first, neighbour_ref, matrix_ref, scale_ref, slice(part * LANES, (part + 1) * LANES))
    mixed_ref[0] = scaled(product_rows(matrix_ref[0], feature_ref[0]), scale_ref[0]).astype(BF16)

    for event in range(hops * HALVES):
        hop, half = event // HALVES, event % HALVES

        @pl.when(step == min(total - 1, ((event + 1) * total) // (hops * HALVES)))
        def _(hop=hop, half=half):
            for direction in range(2):

                @pl.when(arrives(direction, hop))
                def _(direction=direction):
                    arrival(direction, hop, half).wait_recv()
                    pair_copy(direction, hop, half).start()

                if hop + 1 < hops:
                    pl.when(sends(direction, hop + 1))(line_copy(direction, hop + 1, half).start)

    @pl.when(step == total - 1)
    def _():
        local_copy.wait()
        for half in range(HALVES):
            pair_copy(0, -1, half).wait_send()
            pair_arrival(0, -1, half).wait_recv()
            for hop in range(hops):
                for direction in range(2):
                    pl.when(sends(direction, hop))(line_copy(direction, hop, half).wait_send)

                    @pl.when(arrives(direction, hop))
                    def _(direction=direction, hop=hop, half=half):
                        pair_copy(direction, hop, half).wait_send()
                        pair_arrival(direction, hop, half).wait_recv()


def front(table, groups, master, neighbours, features, after=()):
    _, entries, nodes = neighbours.shape
    capacity, width = master.shape
    hops = groups // 2 - 1
    steps = MB * (nodes // TILE)
    return launch(
        "front", functools.partial(front_kernel, groups, steps), table,
        [
            (master, (capacity, width), lambda b, i: (0, 0)),
            (neighbours, (1, entries, TILE), lambda b, i: (b, 0, i)),
            (features, (1, nodes, width), lambda b, i: (b, 0, 0)),
        ],
        [
            ((MB, nodes, nodes), BF16, (1, nodes, TILE), lambda b, i: (b, 0, i), pltpu.HBM),
            ((MB, nodes, LANES), F32, (1, TILE, LANES), lambda b, i: (b, i, 0), pltpu.VMEM),
            ((MB, nodes, width), BF16, (1, TILE, width), lambda b, i: (b, i, 0), pltpu.VMEM),
            ((groups, capacity, width), BF16, None, None),
        ],
        grid=(MB, nodes // TILE), after=after, barrier=FRONT_ID, vmem=20,
        scratch=[
            pltpu.VMEM((capacity, width), BF16),
            pltpu.SemaphoreType.DMA,
            pltpu.SemaphoreType.DMA((2, hops, HALVES)),
            pltpu.SemaphoreType.DMA((2, hops, HALVES)),
            pltpu.SemaphoreType.DMA((1 + 2 * hops, HALVES)),
            pltpu.SemaphoreType.DMA((1 + 2 * hops, HALVES)),
        ],
    )


def greet_mate(mate):
    barrier = pltpu.get_barrier_semaphore()
    pl.semaphore_signal(barrier, inc=1, device_id={"col": mate}, device_id_type=pl.DeviceIdType.MESH)
    pl.semaphore_wait(barrier, 1)


def place_kernel(groups, table_ref, slots_ref, weight_ref, mate_ref, rows_ref):
    owner = pl.program_id(0)

    @pl.when(owner == 0)
    def _():
        rows_ref[...] = jnp.zeros_like(rows_ref)

    put_rows(rows_ref, table_ref[STARTS + owner], slots_ref[0].astype(F32))

    @pl.when(owner == groups - 1)
    def _():
        width = weight_ref.shape[2]
        for block in range(weight_ref.shape[0]):
            source = pl.multiple_of((table_ref[COLUMN] ^ block) * width, width)
            rows = rows_ref[pl.ds(source, width), :].astype(BF16)
            weight_ref[block] = rows
            if block % 2:
                mate_ref[block // 2] = rows


def place(table, slots, after=()):
    groups, capacity, width = slots.shape
    blocks = D // width
    return launch(
        "place", functools.partial(place_kernel, groups), table,
        [(slots, (1, capacity, width), lambda i: (i, 0, 0))],
        [
            ((blocks, width, width), BF16, (blocks, width, width), lambda i: (0, 0, 0), pltpu.VMEM),
            ((blocks // 2, width, width), BF16, (blocks // 2, width, width), lambda i: (0, 0, 0), pltpu.VMEM),
        ],
        grid=(groups,), after=after, vmem=24, scratch=[pltpu.VMEM((D + capacity + SUBLANES, width), F32)],
    )


def batch_kernel(m, chunks, table_ref, *refs):
    matrix_hbm, scale_hbm, far_hbm, here_hbm, weight_hbm, for_mate_hbm, grad_hbm, bias_ref = refs[:8]
    refs = refs[8:]
    total_hbm, bias_sum_in = refs[:2] if m else (None, None)
    refs = refs[2:] if m else refs
    out_hbm, pre_hbm, mate_pre_hbm, mate_weight_hbm = refs[:4]
    away_hbm, refs = refs[4 : 4 + chunks], refs[4 + chunks :]
    ended = m == MB - 1
    results, refs = (refs[:2], refs[2:]) if ended else (refs[:1], refs[1:])
    bias_sum_ref, refs = refs[0], refs[1:]
    (
        matrix_ref, scale_ref, far_ref, mixed_ref, weight_ref, mate_weight_ref, grad_ref, out_ref, pre_ref, mate_pre_ref,
        away_ref, total_ref, load, store, send, receive,
    ) = refs[:16]
    parts = refs[16:]
    nodes, width = far_ref.shape
    wide, narrow = nodes // WIDE, nodes // TILE
    mate = partner(lax.axis_index("col"), 1)

    def at(index, size):
        return pl.ds(pl.multiple_of(index * size, size), size)

    def matrix_load(i):
        return pltpu.make_async_copy(
            matrix_hbm.at[m, :, at(i, WIDE)], matrix_ref.at[:, at(i, WIDE)], load.at[i]
        )

    loads = [
        pltpu.make_async_copy(source, target, load.at[wide + i])
        for i, (source, target) in enumerate(
            [
                (far_hbm, far_ref),
                (scale_hbm.at[m], scale_ref),
                (weight_hbm, weight_ref),
                (here_hbm.at[m], mixed_ref.at[0]),
                (grad_hbm.at[m], grad_ref),
            ]
            + ([(total_hbm, total_ref)] if m else [])
        )
    ]
    started = []

    def save(source, target):
        started.append(pltpu.make_async_copy(source, target, store.at[len(started)]))
        started[-1].start()

    def remote(source, target, number):
        return pltpu.make_async_remote_copy(
            src_ref=source,
            dst_ref=target,
            send_sem=send.at[number],
            recv_sem=receive.at[number],
            device_id={"col": mate},
            device_id_type=pl.DeviceIdType.MESH,
        )

    here_copy = remote(here_hbm.at[m], mixed_ref.at[1], 0)
    weight_copy = remote(for_mate_hbm, mate_weight_ref, 1)

    def there_copy(i):
        return remote(mixed_ref.at[2, at(i, WIDE)], mixed_ref.at[3, at(i, WIDE)], 2 + i)

    def pre_copy(i):
        return remote(pre_ref.at[at(i, TILE)], mate_pre_ref.at[at(i, TILE)], 2 + wide + i)

    loads[0].start()
    matrix_load(0).start()
    loads[1].start()
    for i in range(1, wide):
        matrix_load(i).start()
    for item in loads[2:]:
        item.start()
    greet_mate(mate)
    here_copy.start()
    loads[0].wait()
    loads[1].wait()

    @pl.loop(0, wide)
    def _(i):
        matrix_load(i).wait()
        rows = at(i, WIDE)
        there = product_rows(matrix_ref[:, rows], far_ref[...])
        mixed_ref[2, rows, :] = scaled(there, scale_ref[rows, :]).astype(BF16)
        there_copy(i).start()

    weight_copy.start()
    for item in loads[2:5]:
        item.wait()
    here_copy.wait_recv()
    bias_sum_ref[...] = bias_sum_in[...] if m else jnp.zeros_like(bias_sum_ref)
    for i in range(wide):
        there_copy(i).wait_recv()

    @pl.loop(0, narrow, unroll=UNROLL)
    def _(i):
        rows = at(i, TILE)
        preact = bias_ref[...]
        for block in range(4):
            preact = preact + product(mixed_ref[block, rows, :], weight_ref[block])
        row_ids = i * TILE + lax.broadcasted_iota(jnp.int32, preact.shape, 0)
        live = row_ids < table_ref[LIMITS + m]
        gate = jax.nn.sigmoid(preact)
        out_ref[rows, :] = jnp.where(live, preact * gate, 0.0).astype(BF16)
        slope = gate * (1.0 + preact * (1.0 - gate))
        grad_pre = jnp.where(live, grad_ref[rows, :].astype(F32) * slope, 0.0).astype(BF16)
        pre_ref[rows, :] = grad_pre
        pre_copy(i).start()
        bias_sum_ref[...] += jnp.sum(grad_pre.astype(F32), axis=0, keepdims=True)

    save(pre_ref, pre_hbm)
    save(out_ref, out_hbm)
    if m:
        loads[5].wait()

    @pl.loop(0, 4)
    def _(block):
        term = product_rows(mixed_ref[block], pre_ref[...])
        total_ref[block] = total_ref[block] + term if m else term

    if ended:
        half = width // 2
        upper = lax.axis_index("clus") % 2 == 1
        column = lax.axis_index("col")
        for block in range(4):
            source = partner(column, 1) if block % 2 else column
            source = partner(source, 2) if block >= 2 else source
            rows = at(source, width)
            low, high = total_ref[block, :, :half], total_ref[block, :, half:]
            parts[0][rows, :] = jnp.where(upper, high, low)
            parts[1][rows, :] = jnp.where(upper, low, high).astype(BF16)
        for part, result in zip(parts, results):
            save(part, result)
    else:
        save(total_ref, results[0])

    weight_copy.wait_recv()
    for i in range(narrow):
        pre_copy(i).wait_recv()
    step = width // chunks
    for i in range(wide):
        rows = slice(i * WIDE, (i + 1) * WIDE)
        away = product_back(pre_ref[rows, :], weight_ref[2]) + product_back(mate_pre_ref[rows, :], mate_weight_ref[1])
        away_ref[rows, :] = away.astype(BF16)
        for chunk in range(chunks):
            columns = slice(chunk * step, (chunk + 1) * step)
            save(away_ref.at[rows, columns], away_hbm[chunk].at[rows])
    save(mate_pre_ref, mate_pre_hbm)
    save(mate_weight_ref, mate_weight_hbm)
    here_copy.wait_send()
    weight_copy.wait_send()
    for i in range(wide):
        there_copy(i).wait_send()
    for i in range(narrow):
        pre_copy(i).wait_send()
    for item in started:
        item.wait()


def batch(table, m, matrix, scale, far, here, weight, for_mate, out_grad, bias, total, bias_sum, chunks, after=()):
    nodes, width = far.array.shape
    wide, narrow = nodes // WIDE, nodes // TILE
    flat = lambda i: (0, 0)
    ended = m == MB - 1
    parts = [((D, width // 2), F32), ((D, width // 2), BF16)] if ended else []
    results = [(*part, None, None) for part in parts]
    if not ended:
        results = [((4, width, width), F32, None, None)]
    return launch(
        f"batch{m}", functools.partial(batch_kernel, m, chunks), table,
        [(array, None, None) for array in (matrix, scale, far, here, weight, for_mate, out_grad)]
        + [(bias, (1, width), flat)]
        + ([(total, None, None), (bias_sum, (1, width), flat)] if m else []),
        [((nodes, width), BF16, None, None)] * 3
        + [(for_mate.array.shape, BF16, None, None)]
        + [((nodes, width // chunks), BF16, None, None)] * chunks
        + results
        + [((1, width), F32, (1, width), flat)],
        after=after, barrier=BATCH_ID + m, vmem=34,
        scratch=[
            pltpu.VMEM((nodes, nodes), BF16),
            pltpu.VMEM((nodes, LANES), F32),
            pltpu.VMEM((nodes, width), BF16),
            pltpu.VMEM((4, nodes, width), BF16),
            pltpu.VMEM(weight.array.shape, BF16),
            pltpu.VMEM(for_mate.array.shape, BF16),
            pltpu.VMEM((nodes, width), BF16),
            pltpu.VMEM((nodes, width), BF16),
            pltpu.VMEM((nodes, width), BF16),
            pltpu.VMEM((nodes, width), BF16),
            pltpu.VMEM((nodes, width), BF16),
            pltpu.VMEM((4, width, width), F32),
            pltpu.SemaphoreType.DMA((wide + 6,)),
            pltpu.SemaphoreType.DMA((6 + wide * chunks,)),
            pltpu.SemaphoreType.DMA((2 + wide + narrow,)),
            pltpu.SemaphoreType.DMA((2 + wide + narrow,)),
        ]
        + [pltpu.VMEM(*part) for part in parts],
    )


def scatter_job(m, columns, own_hbm, got_hbm, scale_hbm, matrix_hbm, grads_hbm, scratch, semaphores):
    own_ref, got_ref, scale_ref, matrix_ref, sum_ref, grad_ref = scratch
    steps = matrix_ref.shape[0] // WIDE
    loads = [
        pltpu.make_async_copy(source, target, semaphores.at[i])
        for i, (source, target) in enumerate(
            [(own_hbm.at[m, :, columns], own_ref), (got_hbm, got_ref), (scale_hbm.at[m], scale_ref)]
        )
    ]
    tiles, stores = [], []
    for i in range(steps):
        rows = pl.ds(i * WIDE, WIDE)
        tiles.append(pltpu.make_async_copy(matrix_hbm.at[m, rows], matrix_ref.at[rows], semaphores.at[3 + i]))
        stores.append(
            pltpu.make_async_copy(grad_ref.at[rows], grads_hbm.at[m, rows, columns], semaphores.at[3 + steps + i])
        )

    def work():
        for item in loads:
            item.wait()
        grad_mixed = (own_ref[...] + got_ref[...].astype(F32)).astype(BF16)
        sum_ref[...] = scaled(grad_mixed.astype(F32), scale_ref[...]).astype(BF16)
        for i in range(steps):
            tiles[i].wait()
            rows = slice(i * WIDE, (i + 1) * WIDE)
            grad_ref[rows, :] = product(matrix_ref[rows, :], sum_ref[...]).astype(BF16)
            stores[i].start()

    return loads + tiles, work, stores


def scatter_scratch(nodes, width):
    return [
        pltpu.VMEM((nodes, width), F32),
        pltpu.VMEM((nodes, width), BF16),
        pltpu.VMEM((nodes, LANES), F32),
        pltpu.VMEM((nodes, nodes), BF16),
        pltpu.VMEM((nodes, width), BF16),
        pltpu.VMEM((nodes, width), BF16),
        pltpu.SemaphoreType.DMA((3 + 2 * (nodes // WIDE),)),
    ]


def scatter_kernel(m, chunk, own_hbm, got_hbm, scale_hbm, matrix_hbm, grads_hbm, *refs):
    width = got_hbm.shape[1]
    loads, work, stores = scatter_job(
        m, pl.ds(chunk * width, width), own_hbm, got_hbm, scale_hbm, matrix_hbm, grads_hbm, refs[:6], refs[6]
    )
    for item in loads:
        item.start()
    work()
    for item in stores:
        item.wait()


def scatter(m, chunk, own, got, scale, matrix, grads, after=()):
    _, nodes, width = own.shape
    return launch(
        f"scatter{m}_{chunk}", functools.partial(scatter_kernel, m, chunk), None,
        [(array, None, None) for array in (own, got, scale, matrix)],
        [((MB, nodes, width), BF16, None, None)],
        after=after, alias=(grads, 0), scratch=scatter_scratch(nodes, got.array.shape[1]),
    )[0]


def sum_kernel(groups, capacity, table_ref, *refs):
    keep_hbm, sent_hbm, bias_ref, weight_hbm, mate_weight_hbm = refs[:5]
    pre_hbm, mate_hbm, refs = refs[5 : 5 + MB], refs[5 + MB : 5 + 2 * MB], refs[5 + 2 * MB :]
    own_ref, got_ref, bias_out_ref, back_hbm, refs = *refs[:4], refs[4:]
    pre_ref, mate_ref, weights_ref, back_ref, load, store, refs = *refs[:6], refs[6:]
    keep_ref, pair_ref, land_ref, out_ref, total_ref, end_out_ref, end_in_ref, row_ref = refs[:8]
    pair_send, pair_receive, line_send, line_receive, row_send, row_receive = refs[8:]
    own = lax.axis_index("clus")
    place, pairs = own // 2, groups // 2
    other = partner(own, 1)
    rows = keep_ref.shape[0]
    size = rows // CHUNKS
    ahead, behind = place + 1 < pairs, place >= 1

    def remote(source, target, sent, received, device):
        return pltpu.make_async_remote_copy(
            src_ref=source,
            dst_ref=target,
            send_sem=sent,
            recv_sem=received,
            device_id={"clus": device},
            device_id_type=pl.DeviceIdType.MESH,
        )

    def part(chunk):
        return pl.ds(pl.multiple_of(chunk * size, size), size)

    def pair_copy(chunk):
        return remote(
            sent_hbm.at[part(chunk)], pair_ref.at[part(chunk)], pair_send.at[chunk], pair_receive.at[chunk], other
        )

    def line_copy(direction, chunk):
        return remote(
            out_ref.at[direction, part(chunk)], land_ref.at[direction, part(chunk)],
            line_send.at[direction, chunk], line_receive.at[direction, chunk],
            own + 2 if direction == 0 else own - 2,
        )

    def row_copy(number):
        device = (other, own + 2, own - 2)[number]
        return remote(row_ref.at[number], row_ref.at[3 + number], row_send.at[number], row_receive.at[number], device)

    end_copy = remote(end_out_ref, end_in_ref, pair_send.at[CHUNKS], pair_receive.at[CHUNKS], other)

    nodes = pre_ref.shape[1]
    tiles = nodes // WIDE
    loads = [
        pltpu.make_async_copy(source, target, load.at[i])
        for i, (source, target) in enumerate(
            [(keep_hbm, keep_ref), (weight_hbm.at[0], weights_ref.at[0]), (mate_weight_hbm.at[0], weights_ref.at[1])]
            + [(source, pre_ref.at[m]) for m, source in enumerate(pre_hbm)]
            + [(source, mate_ref.at[m]) for m, source in enumerate(mate_hbm)]
        )
    ]
    stores = [pltpu.make_async_copy(back_ref.at[m], back_hbm.at[m], store.at[m]) for m in range(MB)]

    def back(number):
        m, i = number // tiles, number % tiles
        if i == 0:
            loads[3 + m].wait()
            loads[3 + MB + m].wait()
        down = slice(i * WIDE, (i + 1) * WIDE)
        back_ref[m, down, :] = product_back(pre_ref[m, down, :], weights_ref[0]) + product_back(
            mate_ref[m, down, :], weights_ref[1]
        )
        if i == tiles - 1:
            stores[m].start()

    land_ref[...] = jnp.zeros_like(land_ref)
    row_ref[...] = jnp.zeros_like(row_ref)
    row_ref[0] = bias_ref[...]
    for item in loads:
        item.start()
    barrier = pltpu.get_barrier_semaphore()

    def greet(index):
        pl.semaphore_signal(barrier, inc=1, device_id={"clus": index}, device_id_type=pl.DeviceIdType.MESH)

    greet(other)

    @pl.when(ahead)
    def _():
        greet(own + 2)

    @pl.when(behind)
    def _():
        greet(own - 2)

    pl.semaphore_wait(barrier, 1 + jnp.where(ahead, 1, 0) + jnp.where(behind, 1, 0))
    row_copy(0).start()
    for chunk in range(CHUNKS):
        pair_copy(chunk).start()
    for item in loads[:3]:
        item.wait()

    def pass_on(direction, chunk, first):
        sums = keep_ref[part(chunk), :]
        if not first:
            sums = sums + land_ref[direction, part(chunk), :].astype(F32)
        out_ref[direction, part(chunk), :] = sums.astype(BF16)
        line_copy(direction, chunk).start()

    def pass_row(direction, first):
        row_ref[1 + direction] = row_ref[0] if first else row_ref[0] + row_ref[4 + direction]
        row_copy(1 + direction).start()

    steps = CHUNKS + pairs - 1
    for step in range(steps):
        if step < CHUNKS:
            pair_copy(step).wait_recv()
            keep_ref[part(step), :] += pair_ref[part(step), :].astype(F32)
            if step == 0:
                row_copy(0).wait()
                row_ref[0] += row_ref[3]
            for direction, (here, there) in enumerate(((behind, ahead), (ahead, behind))):

                @pl.when(jnp.logical_not(here) & there)
                def _(direction=direction, step=step):
                    pass_on(direction, step, True)
                    if step == 0:
                        pass_row(direction, True)

        for direction, (here, there) in enumerate(((behind, ahead), (ahead, behind))):
            chunk = step - (place if direction == 0 else pairs - 1 - place)

            @pl.when(here & (chunk >= 0) & (chunk < CHUNKS))
            def _(direction=direction, chunk=chunk, there=there):
                line_copy(direction, chunk).wait_recv()

                @pl.when(there)
                def _():
                    pass_on(direction, chunk, False)

                @pl.when(chunk == 0)
                def _():
                    row_copy(1 + direction).wait_recv()

                    @pl.when(there)
                    def _():
                        pass_row(direction, False)

        for number in range(step * MB * tiles // steps, (step + 1) * MB * tiles // steps):
            back(number)

    total_ref[:rows, :] = keep_ref[...] + (land_ref[0].astype(F32) + land_ref[1].astype(F32))
    total_ref[rows:, :] = jnp.zeros((capacity + SUBLANES, keep_ref.shape[1]), F32)
    end_out_ref[...] = take_rows(total_ref, table_ref[STARTS + other], capacity, rows - 1).astype(BF16)
    end_copy.start()
    own_ref[...] = take_rows(total_ref, table_ref[STARTS + own], capacity, rows - 1)
    bias_out_ref[...] = row_ref[0] + (row_ref[4] + row_ref[5])
    end_copy.wait()
    got_ref[...] = end_in_ref[...]
    for chunk in range(CHUNKS):
        pair_copy(chunk).wait_send()
    for direction, there in enumerate((ahead, behind)):

        @pl.when(there)
        def _(direction=direction):
            row_copy(1 + direction).wait_send()
            for chunk in range(CHUNKS):
                line_copy(direction, chunk).wait_send()

    for item in stores:
        item.wait()


def sum_over_owners(table, groups, capacity, keep, sent, bias, weight, mate_weight, pres, mates, after=()):
    rows, half = keep.shape
    nodes, width = pres[0].shape
    flat = lambda i: (0, 0)
    shape = (capacity, half)
    return launch(
        "sum", functools.partial(sum_kernel, groups, capacity), table,
        [(array, None, None) for array in (keep, sent)]
        + [(bias, bias.shape, flat)]
        + [(array, None, None) for array in (weight, mate_weight, *pres, *mates)],
        [
            (shape, F32, shape, flat),
            (shape, BF16, shape, flat),
            (bias.shape, F32, bias.shape, flat),
            ((MB, nodes, width), F32, None, None),
        ],
        after=after, barrier=SUM_ID, vmem=38,
        scratch=[
            pltpu.VMEM((MB, nodes, width), BF16),
            pltpu.VMEM((MB, nodes, width), BF16),
            pltpu.VMEM((2, width, width), BF16),
            pltpu.VMEM((MB, nodes, width), F32),
            pltpu.SemaphoreType.DMA((3 + 2 * MB,)),
            pltpu.SemaphoreType.DMA((MB,)),
            pltpu.VMEM((rows, half), F32),
            pltpu.VMEM((rows, half), BF16),
            pltpu.VMEM((2, rows, half), BF16),
            pltpu.VMEM((2, rows, half), BF16),
            pltpu.VMEM((rows + capacity + SUBLANES, half), F32),
            pltpu.VMEM(shape, BF16),
            pltpu.VMEM(shape, BF16),
            pltpu.VMEM((6, 1, width), F32),
            pltpu.SemaphoreType.DMA((CHUNKS + 1,)),
            pltpu.SemaphoreType.DMA((CHUNKS + 1,)),
            pltpu.SemaphoreType.DMA((2, CHUNKS)),
            pltpu.SemaphoreType.DMA((2, CHUNKS)),
            pltpu.SemaphoreType.DMA((3,)),
            pltpu.SemaphoreType.DMA((3,)),
        ],
    )


def adamw_update(current, first_moment, second_moment, gradient, step_rate):
    first_new = BETA_ONE * first_moment + (1.0 - BETA_ONE) * gradient
    second_new = BETA_TWO * second_moment + (1.0 - BETA_TWO) * gradient * gradient
    fixed_first = first_new / (1.0 - BETA_ONE**STEP)
    fixed_second = second_new / (1.0 - BETA_TWO**STEP)
    updated = current - step_rate * (
        fixed_first / (jnp.sqrt(fixed_second) + EPSILON) + DECAY * current
    )
    return (updated, first_new, second_new)


def finish_kernel(groups, table_ref, *refs):
    done = MB - 1
    own_ref, got_ref, bias_grad_ref, biases = refs[0], refs[1], refs[2], refs[3:6]
    weights_hbm, out_parts, refs = refs[6:9], refs[9 : 9 + MB], refs[9 + MB :]
    back_hbm, gots, (scale_hbm, matrix_hbm), refs = refs[0], refs[1 : 1 + done], refs[1 + done : 3 + done], refs[3 + done :]
    updated_hbm, bias_outs, (out_hbm, grads_hbm), refs = refs[:3], refs[3:6], refs[6:8], refs[8:]
    weights, buffers, (weight_load, weight_store, load, store), refs = refs[:3], refs[3], refs[4:8], refs[8:]
    jobs = [
        scatter_job(
            m, pl.ds(0, back_hbm.shape[2]), back_hbm, gots[m], scale_hbm, matrix_hbm, grads_hbm,
            refs[7 * m : 7 * m + 6], refs[7 * m + 6],
        )
        for m in range(done)
    ]
    weight_loads = [
        pltpu.make_async_copy(source, target, weight_load.at[i])
        for i, (source, target) in enumerate(zip(weights_hbm, weights))
    ]
    weight_stores = [
        pltpu.make_async_copy(source, target, weight_store.at[i])
        for i, (source, target) in enumerate(zip(weights, updated_hbm))
    ]
    out_loads, out_stores = relay(
        out_parts, [out_hbm.at[m] for m in range(MB)], [buffers.at[m] for m in range(MB)], load, store
    )
    for item in jobs[0][0] + weight_loads:
        item.start()
    for later, _, _ in jobs[1:]:
        for item in later:
            item.start()
    for item in out_loads:
        item.start()
    jobs[0][1]()

    for item in weight_loads:
        item.wait()
    rows, width = weights[0].shape
    half = width // 2
    strip = min(rows, TILE // 2)
    own = table_ref[GROUP]
    for first in range(0, rows, strip):
        row_ids = first + lax.broadcasted_iota(jnp.int32, (strip, half), 0)
        used = row_ids < table_ref[STARTS + groups + own]
        down = slice(first, first + strip)
        for side in range(2):
            mine = (own & 1) == side
            here, there = own_ref[down, :], got_ref[down, :].astype(F32)
            columns = slice(side * half, (side + 1) * half)
            results = adamw_update(*(ref[down, columns] for ref in weights), jnp.where(mine, here, there), RATE_WEIGHT)
            for ref, result in zip(weights, results):
                ref[down, columns] = jnp.where(used, result, 0.0)
    for item in weight_stores:
        item.start()
    results = adamw_update(*(ref[...] for ref in biases), bias_grad_ref[...], RATE_BIAS)
    for ref, result in zip(bias_outs, results):
        ref[...] = result

    for _, work, _ in jobs[1:]:
        work()
    for item, onward in zip(out_loads, out_stores):
        item.wait()
        onward.start()
    for item in weight_stores + out_stores:
        item.wait()
    for _, _, stores in jobs:
        for item in stores:
            item.wait()


def finish(table, groups, mine, other, bias_grad, biases, weights, outputs, backs, gots, scale, matrix, after=()):
    capacity, width = weights[0].shape
    nodes = outputs[0].shape[0]
    fixed = lambda i: (0, 0)
    scratch = [pltpu.VMEM((capacity, width), F32)] * 3 + [
        pltpu.VMEM((MB, nodes, width), BF16),
        pltpu.SemaphoreType.DMA((3,)),
        pltpu.SemaphoreType.DMA((3,)),
        pltpu.SemaphoreType.DMA((MB * PIECES,)),
        pltpu.SemaphoreType.DMA((MB * PIECES,)),
    ]
    for _ in gots:
        scratch += scatter_scratch(nodes, width)
    return launch(
        "finish", functools.partial(finish_kernel, groups), table,
        [(array, array.shape, fixed) for array in (mine, other)]
        + [(array, (1, width), fixed) for array in (bias_grad, *biases)]
        + [(array, None, None) for array in (*weights, *outputs, backs, *gots, scale, matrix)],
        [((capacity, width), F32, None, None)] * 3
        + [((1, width), F32, (1, width), fixed)] * 3
        + [((MB, nodes, width), BF16, None, None)] * 2,
        after=after, scratch=scratch, vmem=35,
    )


def shards(
    features,
    neighbours,
    node_counts,
    row_counts,
    master_weight,
    weight_first,
    weight_second,
    master_bias,
    bias_first,
    bias_second,
    out_grad,
):
    groups = lax.axis_size("clus")
    capacity, width = master_weight.shape
    owner_ids = jnp.arange(groups, dtype=jnp.int32)
    starts = jnp.sum(jnp.where(owner_ids[None, :] < owner_ids[:, None], row_counts[None, :], 0), axis=1)
    table = jnp.concatenate(
        [
            jnp.stack([lax.axis_index("clus"), lax.axis_index("col")]).astype(jnp.int32),
            node_counts[:, 0],
            starts.astype(jnp.int32),
            row_counts,
        ]
    )
    bias_row, bias_first_row, bias_second_row = (
        array.reshape(1, width) for array in (master_bias, bias_first, bias_second)
    )

    picked = pick(features, (0,))
    picked = picked + pick(features, tuple(range(1, MB)), picked)
    far = [Kept(flip(array, "col", 2), None) for array in picked]

    matrix, *kept, slots = front(table, groups, master_weight, jnp.swapaxes(neighbours, 1, 2), features, [picked[-1]])
    scale, here = (Kept(array) for array in kept)
    weight, for_mate = (Kept(array) for array in place(table, slots))
    last = for_mate
    total, bias_sum = None, None
    outputs, pres, mates, away = [], [], [], []
    for m in range(MB):
        chunks = 2 if m == MB - 1 else 1
        out_m, pre_m, mate_m, mate_weight, *rest = batch(
            table, m, matrix, scale, far[m], here, weight, for_mate, out_grad, bias_row, total, bias_sum, chunks,
            [last],
        )
        outputs.append(out_m)
        pres.append(pre_m)
        mates.append(mate_m)
        away.append([Kept(flip(chunk, "col", 2), None) for chunk in rest[:chunks]])
        total, bias_sum = rest[chunks], rest[-1]
        last = bias_sum

    keep, sent, bias_sum = rest[chunks:]
    mine, other, bias_total, backs = sum_over_owners(
        table, groups, capacity, keep, sent, bias_sum, weight, mate_weight, pres, mates, [last]
    )
    *updated, outputs, input_grads = finish(
        table, groups, mine, other, bias_total, (bias_row, bias_first_row, bias_second_row),
        (master_weight, weight_first, weight_second), outputs, backs, [part[0] for part in away[:-1]],
        scale, matrix, [bias_total],
    )
    for chunk, got in enumerate(away[-1]):
        input_grads = scatter(MB - 1, chunk, backs, got, scale, matrix, input_grads)
    return (outputs, input_grads, *updated[:3], *(row.reshape(width) for row in updated[3:]))


def solution(mesh):
    in_specs = (
        P(None, "clus", "col"),
        P(None, "clus", None),
        P(None, "clus"),
        P(),
        P("clus", "col"),
        P("clus", "col"),
        P("clus", "col"),
        P("col"),
        P("col"),
        P("col"),
        P(None, "clus", "col"),
    )
    out_specs = (
        P(None, "clus", "col"),
        P(None, "clus", "col"),
        P("clus", "col"),
        P("clus", "col"),
        P("clus", "col"),
        P("col"),
        P("col"),
        P("col"),
    )
    return jax.shard_map(shards, mesh=mesh, in_specs=in_specs, out_specs=out_specs, check_vma=False)
```

time: 240 us -> 218 us (0.908)
  Pallas kernels: 218 us -> 205 us
  local copies, waits for them, and re-layouts: 8.4 us -> 1.58 us
    pallas_call x15 -> x11, Pallas kernels: 218 us -> 205 us  [launch(): pl.pallas_call(kernel, grid_spec=pltpu.PrefetchScalarGridSpec(num_scalar_...]
    unnamed x32 -> x14, local copies, waits for them, and re-layouts: 7.65 us -> 1.5 us
  transfers between devices with their start and end apart: 7 -> 7, of which waited for: 0 -> 0; matrix products, arithmetic and copies ran while one was open for 0% -> 0% of each run, Pallas kernels for 88% -> 91%
where the time goes in v4:
time: 218 us; the launch traced here: 217 us
  Pallas kernels  205 us (94%)
  starting transfers between devices  9.4 us (4%)
    pallas_call x11, Pallas kernels, launch(): pl.pallas_call(kernel, grid_spec=pltpu.PrefetchScalarGridSpec(num_scalar_...  205 us
    ppermute x7, starting transfers between devices, flip(): return lax.ppermute(values, axis, [(i, i ^ bit) for i in range(size)])  9.4 us
  transfers between devices with their start and end apart: 7, of which 0 were waited for; matrix products, arithmetic and copies ran while one was open for 0% of the time, Pallas kernels for 91%

profile of v4, /device:TPU:0, one launch (start us, length us, event | category | flops | bytes accessed | tf_op | source)
XLA Modules:
  0.0 217.5 jit_solution(9447271524004372188)
XLA Ops:
  0.6 2.2 %pick0.1.refs_1_ = bf16[1536,512]{1,0:T(8,128)(2,1)} custom-call(bf16[3,1536,512]{2,1,0:T(8,128)(2,1)} %refs_3_.1), custom_call_target="tpu_custom_call" | custom-call | flops 1 | bytes 1 | tf_op jit(solution)/shard_map/pick0/pallas_call | solution.py:68
  2.8 0.0 copy-start.6
  2.9 0.0 copy-start.5
  2.9 3.0 %collective-permute-start.2 = (bf16[1536,512]{1,0:T(8,128)(2,1)}, bf16[1536,512]{1,0:T(8,128)(2,1)}, u32[]{:S(2)}, u32[]{:S(2)}) collective-permute-start(bf16[1536,512]{1,0:T(8,128)(2,1)} %pick0.1.refs_1_), channel_id=1, source_target_pairs={{0,2},{1,3},{2,0},{3,1},{4,6},{5,7},{6,4},{7,5},{8,10},{9,11},{10,... | collective-permute-start | bytes 4718600 | tf_op jit(solution)/shard_map/ppermute | solution.py:93
  5.9 2.8 %pick1.1 = (bf16[1536,512]{1,0:T(8,128)(2,1)}, bf16[1536,512]{1,0:T(8,128)(2,1)}) custom-call(bf16[3,1536,512]{2,1,0:T(8,128)(2,1)} %refs_3_.1, bf16[1536,512]{1,0:T(8,128)(2,1)} %pick0.1.refs_1_), custom_call_target="tpu_custom_call" | custom-call | flops 1 | bytes 1 | tf_op jit(solution)/shard_map/pick1/pallas_call | solution.py:68
  8.7 0.1 collective-permute-start.1
  8.8 2.0 collective-permute-start
  10.8 0.0 copy-done.6
  10.8 0.1 select_reduce_fusion
  10.9 0.0 copy-done.5
  10.9 0.1 concatenate.3.refs_0_
  11.0 51.5 %front.1 = (bf16[3,1536,1536]{2,1,0:T(8,128)(2,1)}, f32[3,1536,128]{2,1,0:T(8,128)S(1)}, bf16[3,1536,512]{2,1,0:T(8,128)(2,1)S(1)}, bf16[8,512,512]{2,1,0:T(8,128)(2,1)}) custom-call(s32[21]{0:T(128)S(1)} %concatenate.3.refs_0_, f32[512,512]{1,0:T(8,128)} %refs_7_.7, s32[3,16,1536]{2,1,0:T(8,128)} %bitcast.16, bf16[3,1536,512]{2,1,0:T(8,128)(2,1)} %refs_3_.1, ...), custom_call_target="tpu_custom_call" | custom-call | flops 1 | bytes 1 | tf_op jit(solution)/shard_map/front/pallas_call | solution.py:68
  62.5 0.0 copy-start.2
  62.5 7.2 %place.1 = (bf16[4,512,512]{2,1,0:T(8,128)(2,1)S(1)}, bf16[2,512,512]{2,1,0:T(8,128)(2,1)S(1)}) custom-call(s32[21]{0:T(128)S(1)} %concatenate.3.refs_0_, bf16[8,512,512]{2,1,0:T(8,128)(2,1)} %get-tuple-element.53.refs_1_), custom_call_target="tpu_custom_call" | custom-call | flops 1 | bytes 1 | tf_op jit(solution)/shard_map/place/pallas_call | solution.py:68
  69.7 0.0 collective-permute-done.2.refs_3_
  69.7 0.0 copy-done.2
  69.7 20.0 %batch0.1 = (bf16[1536,512]{1,0:T(8,128)(2,1)}, bf16[1536,512]{1,0:T(8,128)(2,1)}, bf16[1536,512]{1,0:T(8,128)(2,1)}, bf16[2,512,512]{2,1,0:T(8,128)(2,1)}, bf16...) custom-call(s32[21]{0:T(128)S(1)} %concatenate.3.refs_0_, ...), custom_call_target="tpu_custom_call" | custom-call | flops 1 | bytes 1 | tf_op jit(solution)/shard_map/batch0/pallas_call | solution.py:68
  89.7 0.6 collective-permute-start.3
  90.3 0.0 collective-permute-done.1.refs_3_
  90.3 20.5 %batch1.1 = (bf16[1536,512]{1,0:T(8,128)(2,1)}, bf16[1536,512]{1,0:T(8,128)(2,1)}, bf16[1536,512]{1,0:T(8,128)(2,1)}, bf16[2,512,512]{2,1,0:T(8,128)(2,1)}, bf16...) custom-call(s32[21]{0:T(128)S(1)} %concatenate.3.refs_0_, ...), custom_call_target="tpu_custom_call" | custom-call | flops 1 | bytes 1 | tf_op jit(solution)/shard_map/batch1/pallas_call | solution.py:68
  110.8 1.6 collective-permute-start.4
  112.4 0.0 collective-permute-done.refs_3_
  112.4 20.4 %batch2.1 = (bf16[1536,512]{1,0:T(8,128)(2,1)}, bf16[1536,512]{1,0:T(8,128)(2,1)}, bf16[1536,512]{1,0:T(8,128)(2,1)}, bf16[2,512,512]{2,1,0:T(8,128)(2,1)}, bf16...) custom-call(s32[21]{0:T(128)S(1)} %concatenate.3.refs_0_, ...), custom_call_target="tpu_custom_call" | custom-call | flops 1 | bytes 1 | tf_op jit(solution)/shard_map/batch2/pallas_call | solution.py:68
  132.8 0.6 collective-permute-start.6
  133.3 1.5 collective-permute-start.5
  134.9 0.0 copy-start.3
  134.9 0.0 copy-start.4
  134.9 54.7 %sum.1 = (f32[512,256]{1,0:T(8,128)S(1)}, bf16[512,256]{1,0:T(8,128)(2,1)S(1)}, f32[1,512]{1,0:T(1,128)S(1)}, f32[3,1536,512]{2,1,0:T(8,128)}) custom-call(s32[21]{0:T(128)S(1)} %concatenate.3.refs_0_, f32[2048,256]{1,0:T(8,128)} %get-tuple-element.61.refs_1_, bf16[2048,256]{1,0:T(8,128)(2,1)} %get-tuple-element.62.refs_2_, ...), custom_call_target="tpu_custom_call" | custom-call | flops 1 | bytes 1 | tf_op jit(solution)/shard_map/sum/pallas_call | solution.py:68
  189.6 0.0 copy-start
  189.6 0.8 copy-done
  190.4 0.0 copy-start.1
  190.4 0.7 copy-done.1
  191.1 0.0 collective-permute-done.3.refs_14_
  191.1 0.0 collective-permute-done.4.refs_15_
  191.1 0.0 copy-done.3
  191.1 0.0 copy-done.4
  191.1 15.8 %finish.1 = (f32[512,512]{1,0:T(8,128)}, f32[512,512]{1,0:T(8,128)}, f32[512,512]{1,0:T(8,128)}, f32[1,512]{1,0:T(1,128)}, f32[1,512]{1,0:T(1,128)}, /*index=5*/...) custom-call(s32[21]{0:T(128)S(1)} %concatenate.3.refs_0_, f32[512,256]{1,0:T(8,128)} %copy-done, ...), custom_call_target="tpu_custom_call" | custom-call | flops 1 | bytes 1 | tf_op jit(solution)/shard_map/finish/pallas_call | solution.py:68
  206.9 0.0 collective-permute-done.6.refs_1_
  206.9 5.2 %scatter2_0.1.refs_4_ = bf16[3,1536,512]{2,1,0:T(8,128)(2,1)} custom-call(f32[3,1536,512]{2,1,0:T(8,128)} %get-tuple-element.77.refs_13_.refs_0_, bf16[1536,256]{1,0:T(8,128)(2,1)S(1)} %collective-permute-done.6.refs_1_, f32[3,1536,128]{2,1,0:T(8,128)S(1)} %get-tuple-element.51.refs_2_.refs_16_, ...), custom_call_target="tpu_custom_call", output_to_operand_aliasing={{}: (4, {})} | custom-call | flops 1 | bytes 1 | tf_op jit(solution)/shard_map/scatter2_0/pallas_call | solution.py:68
  212.1 0.0 collective-permute-done.5.refs_1_
  212.1 5.2 %scatter2_1.1 = bf16[3,1536,512]{2,1,0:T(8,128)(2,1)} custom-call(f32[3,1536,512]{2,1,0:T(8,128)} %get-tuple-element.77.refs_13_.refs_0_, bf16[1536,256]{1,0:T(8,128)(2,1)S(1)} %collective-permute-done.5.refs_1_, f32[3,1536,128]{2,1,0:T(8,128)S(1)} %get-tuple-element.51.refs_2_.refs_16_, ...), custom_call_target="tpu_custom_call", output_to_operand_aliasing={{}: (4, {})} | custom-call | flops 1 | bytes 1 | tf_op jit(solution)/shard_map/scatter2_1/pallas_call | solution.py:68
Async XLA Ops:
  2.8 8.0 %copy-start.6 = (s32[8]{0:T(128)S(1)}, s32[8]{0:T(128)}, u32[]{:S(2)}) copy-start(s32[8]{0:T(128)} %param.14) | copy-start | bytes 100
  2.9 8.1 %copy-start.5 = (s32[3,1]{0,1:T(1,128)S(1)}, s32[3,1]{0,1:T(1,128)}, u32[]{:S(2)}) copy-start(s32[3,1]{0,1:T(1,128)} %param.13) | copy-start | bytes 40
  2.9 66.9 %collective-permute-start.2 = (bf16[1536,512]{1,0:T(8,128)(2,1)}, bf16[1536,512]{1,0:T(8,128)(2,1)}, u32[]{:S(2)}, u32[]{:S(2)}) collective-permute-start(bf16[1536,512]{1,0:T(8,128)(2,1)} %pick0.1.refs_1_), channel_id=1, source_target_pairs={{0,2},{1,3},{2,0},{3,1},{4,6},{5,7},{6,4},{7,5},{8,10},{9,11},{10,... | collective-permute-start | bytes 4718600 | tf_op jit(solution)/shard_map/ppermute | solution.py:93
  8.7 81.6 %collective-permute-start.1 = (bf16[1536,512]{1,0:T(8,128)(2,1)}, bf16[1536,512]{1,0:T(8,128)(2,1)S(1)}, u32[]{:S(2)}, u32[]{:S(2)}) collective-permute-start(bf16[1536,512]{1,0:T(8,128)(2,1)} %get-tuple-element.56), channel_id=1, source_target_pairs={{0,2},{1,3},{2,0},{3,1},{4,6},{5,7},{6,4},{7,5},{8,10},{9,11},{10,... | collective-permute-start | bytes 4718600 | tf_op jit(solution)/shard_map/ppermute | solution.py:93
  8.8 103.6 %collective-permute-start = (bf16[1536,512]{1,0:T(8,128)(2,1)}, bf16[1536,512]{1,0:T(8,128)(2,1)S(1)}, u32[]{:S(2)}, u32[]{:S(2)}) collective-permute-start(bf16[1536,512]{1,0:T(8,128)(2,1)} %get-tuple-element.49.refs_4_), channel_id=1, source_target_pairs={{0,2},{1,3},{2,0},{3,1},{4,6},{5,7},{6,4},{7,5},{8,10},{9,11},{10,... | collective-permute-start | bytes 4718600 | tf_op jit(solution)/shard_map/ppermute | solution.py:93
  62.5 7.3 %copy-start.2 = (f32[512]{0:T(512)S(1)}, f32[512]{0:T(512)}, u32[]{:S(2)}) copy-start(f32[512]{0:T(512)} %param.18) | copy-start | bytes 6148
  89.7 101.4 %collective-permute-start.3 = (bf16[1536,512]{1,0:T(8,128)(2,1)}, bf16[1536,512]{1,0:T(8,128)(2,1)S(1)}, u32[]{:S(2)}, u32[]{:S(2)}) collective-permute-start(bf16[1536,512]{1,0:T(8,128)(2,1)} %get-tuple-element.78), channel_id=1, source_target_pairs={{0,2},{1,3},{2,0},{3,1},{4,6},{5,7},{6,4},{7,5},{8,10},{9,11},{10,... | collective-permute-start | bytes 4718600 | tf_op jit(solution)/shard_map/ppermute | solution.py:93
  110.8 80.3 %collective-permute-start.4 = (bf16[1536,512]{1,0:T(8,128)(2,1)}, bf16[1536,512]{1,0:T(8,128)(2,1)S(1)}, u32[]{:S(2)}, u32[]{:S(2)}) collective-permute-start(bf16[1536,512]{1,0:T(8,128)(2,1)} %get-tuple-element.79), channel_id=1, source_target_pairs={{0,2},{1,3},{2,0},{3,1},{4,6},{5,7},{6,4},{7,5},{8,10},{9,11},{10,... | collective-permute-start | bytes 4718600 | tf_op jit(solution)/shard_map/ppermute | solution.py:93
  132.8 74.1 %collective-permute-start.6 = (bf16[1536,256]{1,0:T(8,128)(2,1)}, bf16[1536,256]{1,0:T(8,128)(2,1)S(1)}, u32[]{:S(2)}, u32[]{:S(2)}) collective-permute-start(bf16[1536,256]{1,0:T(8,128)(2,1)} %get-tuple-element.82), channel_id=1, source_target_pairs={{0,2},{1,3},{2,0},{3,1},{4,6},{5,7},{6,4},{7,5},{8,10},{9,11},{10,... | collective-permute-start | bytes 2359304 | tf_op jit(solution)/shard_map/ppermute | solution.py:93
  133.3 78.7 %collective-permute-start.5 = (bf16[1536,256]{1,0:T(8,128)(2,1)}, bf16[1536,256]{1,0:T(8,128)(2,1)S(1)}, u32[]{:S(2)}, u32[]{:S(2)}) collective-permute-start(bf16[1536,256]{1,0:T(8,128)(2,1)} %get-tuple-element.81), channel_id=1, source_target_pairs={{0,2},{1,3},{2,0},{3,1},{4,6},{5,7},{6,4},{7,5},{8,10},{9,11},{10,... | collective-permute-start | bytes 2359304 | tf_op jit(solution)/shard_map/ppermute | solution.py:93
  134.9 56.2 %copy-start.3 = (f32[512]{0:T(512)S(1)}, f32[512]{0:T(512)}, u32[]{:S(2)}) copy-start(f32[512]{0:T(512)} %param.19) | copy-start | bytes 6148
  134.9 56.2 %copy-start.4 = (f32[512]{0:T(512)S(1)}, f32[512]{0:T(512)}, u32[]{:S(2)}) copy-start(f32[512]{0:T(512)} %param.20) | copy-start | bytes 6148
  189.6 0.8 copy-start
  190.4 0.7 copy-start.1

commit v5 on v4

--- a/solution.py
+++ b/solution.py
@@ -76,7 +76,7 @@
             scratch_shapes=list(scratch),
         ),
         out_shape=[
-            pltpu.HBM(out[0], out[1]) if out[2] is None else (out[4] if len(out) > 4 else jax.ShapeDtypeStruct)(out[0], out[1])
+            (out[4] if len(out) > 4 else pltpu.HBM if out[2] is None else jax.ShapeDtypeStruct)(out[0], out[1])
             for out in outs
         ],
         input_output_aliases={len(tables) + len(ins): alias[1]} if alias else {},
@@ -428,9 +428,10 @@
     refs = refs[8:]
     total_hbm, bias_sum_in = refs[:2] if m else (None, None)
     refs = refs[2:] if m else refs
-    out_hbm, pre_hbm, mate_pre_hbm, mate_weight_hbm = refs[:4]
-    away_hbm, refs = refs[4 : 4 + chunks], refs[4 + chunks :]
     ended = m == MB - 1
+    out_hbm, pre_hbm, mate_pre_hbm = refs[:3]
+    away_hbm, refs = refs[3 : 3 + chunks], refs[3 + chunks :]
+    mate_weight_hbm, refs = (refs[0], refs[1:]) if ended else (None, refs)
     results, refs = (refs[:2], refs[2:]) if ended else (refs[:1], refs[1:])
     bias_sum_ref, refs = refs[0], refs[1:]
     (
@@ -561,6 +562,9 @@
     weight_copy.wait_recv()
     for i in range(narrow):
         pre_copy(i).wait_recv()
+    save(mate_pre_ref, mate_pre_hbm)
+    if ended:
+        save(mate_weight_ref, mate_weight_hbm)
     step = width // chunks
     for i in range(wide):
         rows = slice(i * WIDE, (i + 1) * WIDE)
@@ -569,8 +573,6 @@
         for chunk in range(chunks):
             columns = slice(chunk * step, (chunk + 1) * step)
             save(away_ref.at[rows, columns], away_hbm[chunk].at[rows])
-    save(mate_pre_ref, mate_pre_hbm)
-    save(mate_weight_ref, mate_weight_hbm)
     here_copy.wait_send()
     weight_copy.wait_send()
     for i in range(wide):
@@ -589,18 +591,19 @@
     parts = [((D, width // 2), F32), ((D, width // 2), BF16)] if ended else []
     results = [(*part, None, None) for part in parts]
     if not ended:
-        results = [((4, width, width), F32, None, None)]
+        results = [((4, width, width), F32, None, None, pltpu.VMEM)]
     return launch(
         f"batch{m}", functools.partial(batch_kernel, m, chunks), table,
         [(array, None, None) for array in (matrix, scale, far, here, weight, for_mate, out_grad)]
         + [(bias, (1, width), flat)]
         + ([(total, None, None), (bias_sum, (1, width), flat)] if m else []),
-        [((nodes, width), BF16, None, None)] * 3
-        + [(for_mate.array.shape, BF16, None, None)]
+        [((nodes, width), BF16, None, None, pltpu.VMEM)]
+        + [((nodes, width), BF16, None, None)] * 2
         + [((nodes, width // chunks), BF16, None, None)] * chunks
+        + ([(for_mate.array.shape, BF16, None, None)] if ended else [])
         + results
         + [((1, width), F32, (1, width), flat)],
-        after=after, barrier=BATCH_ID + m, vmem=34,
+        after=after, barrier=BATCH_ID + m, vmem=34 if m == MB - 1 else 32,
         scratch=[
             pltpu.VMEM((nodes, nodes), BF16),
             pltpu.VMEM((nodes, LANES), F32),
@@ -623,19 +626,19 @@
     )
 
 
-def scatter_job(m, columns, own_hbm, got_hbm, scale_hbm, matrix_hbm, grads_hbm, scratch, semaphores):
+def scatter_job(m, columns, own_source, got_source, scale_source, matrix_source, grads_hbm, scratch, semaphores):
     own_ref, got_ref, scale_ref, matrix_ref, sum_ref, grad_ref = scratch
     steps = matrix_ref.shape[0] // WIDE
     loads = [
         pltpu.make_async_copy(source, target, semaphores.at[i])
         for i, (source, target) in enumerate(
-            [(own_hbm.at[m, :, columns], own_ref), (got_hbm, got_ref), (scale_hbm.at[m], scale_ref)]
+            [(own_source.at[:, columns], own_ref), (got_source, got_ref), (scale_source.at[m], scale_ref)]
         )
     ]
     tiles, stores = [], []
     for i in range(steps):
         rows = pl.ds(i * WIDE, WIDE)
-        tiles.append(pltpu.make_async_copy(matrix_hbm.at[m, rows], matrix_ref.at[rows], semaphores.at[3 + i]))
+        tiles.append(pltpu.make_async_copy(matrix_source.at[rows], matrix_ref.at[rows], semaphores.at[3 + i]))
         stores.append(
             pltpu.make_async_copy(grad_ref.at[rows], grads_hbm.at[m, rows, columns], semaphores.at[3 + steps + i])
         )
@@ -643,7 +646,7 @@
     def work():
         for item in loads:
             item.wait()
-        grad_mixed = (own_ref[...] + got_ref[...].astype(F32)).astype(BF16)
+        grad_mixed = (own_ref[...].astype(F32) + got_ref[...].astype(F32)).astype(BF16)
         sum_ref[...] = scaled(grad_mixed.astype(F32), scale_ref[...]).astype(BF16)
         for i in range(steps):
             tiles[i].wait()
@@ -656,7 +659,7 @@
 
 def scatter_scratch(nodes, width):
     return [
-        pltpu.VMEM((nodes, width), F32),
+        pltpu.VMEM((nodes, width), BF16),
         pltpu.VMEM((nodes, width), BF16),
         pltpu.VMEM((nodes, LANES), F32),
         pltpu.VMEM((nodes, nodes), BF16),
@@ -679,7 +682,7 @@
 
 
 def scatter(m, chunk, own, got, scale, matrix, grads, after=()):
-    _, nodes, width = own.shape
+    nodes, width = own.array.shape
     return launch(
         f"scatter{m}_{chunk}", functools.partial(scatter_kernel, m, chunk), None,
         [(array, None, None) for array in (own, got, scale, matrix)],
@@ -751,9 +754,8 @@
             loads[3 + m].wait()
             loads[3 + MB + m].wait()
         down = slice(i * WIDE, (i + 1) * WIDE)
-        back_ref[m, down, :] = product_back(pre_ref[m, down, :], weights_ref[0]) + product_back(
-            mate_ref[m, down, :], weights_ref[1]
-        )
+        term = product_back(pre_ref[m, down, :], weights_ref[0]) + product_back(mate_ref[m, down, :], weights_ref[1])
+        back_ref[m, down, :] = term.astype(BF16)
         if i == tiles - 1:
             stores[m].start()
 
@@ -869,14 +871,14 @@
             (shape, F32, shape, flat),
             (shape, BF16, shape, flat),
             (bias.shape, F32, bias.shape, flat),
-            ((MB, nodes, width), F32, None, None),
+            ((MB, nodes, width), BF16, None, None),
         ],
-        after=after, barrier=SUM_ID, vmem=38,
+        after=after, barrier=SUM_ID, vmem=34,
         scratch=[
             pltpu.VMEM((MB, nodes, width), BF16),
             pltpu.VMEM((MB, nodes, width), BF16),
             pltpu.VMEM((2, width, width), BF16),
-            pltpu.VMEM((MB, nodes, width), F32),
+            pltpu.VMEM((MB, nodes, width), BF16),
             pltpu.SemaphoreType.DMA((3 + 2 * MB,)),
             pltpu.SemaphoreType.DMA((MB,)),
             pltpu.VMEM((rows, half), F32),
@@ -913,11 +915,11 @@
     own_ref, got_ref, bias_grad_ref, biases = refs[0], refs[1], refs[2], refs[3:6]
     weights_hbm, out_parts, refs = refs[6:9], refs[9 : 9 + MB], refs[9 + MB :]
     back_hbm, gots, (scale_hbm, matrix_hbm), refs = refs[0], refs[1 : 1 + done], refs[1 + done : 3 + done], refs[3 + done :]
-    updated_hbm, bias_outs, (out_hbm, grads_hbm), refs = refs[:3], refs[3:6], refs[6:8], refs[8:]
-    weights, buffers, (weight_load, weight_store, load, store), refs = refs[:3], refs[3], refs[4:8], refs[8:]
+    updated_hbm, bias_outs, (out_hbm, grads_hbm, last_back_ref, last_matrix_ref), refs = refs[:3], refs[3:6], refs[6:10], refs[10:]
+    weights, (weight_load, weight_store, store), refs = refs[:3], refs[3:6], refs[6:]
     jobs = [
         scatter_job(
-            m, pl.ds(0, back_hbm.shape[2]), back_hbm, gots[m], scale_hbm, matrix_hbm, grads_hbm,
+            m, pl.ds(0, back_hbm.shape[2]), back_hbm.at[m], gots[m], scale_hbm, matrix_hbm.at[m], grads_hbm,
             refs[7 * m : 7 * m + 6], refs[7 * m + 6],
         )
         for m in range(done)
@@ -930,15 +932,19 @@
         pltpu.make_async_copy(source, target, weight_store.at[i])
         for i, (source, target) in enumerate(zip(weights, updated_hbm))
     ]
-    out_loads, out_stores = relay(
-        out_parts, [out_hbm.at[m] for m in range(MB)], [buffers.at[m] for m in range(MB)], load, store
-    )
+    moves = [
+        pltpu.make_async_copy(source, target, store.at[i])
+        for i, (source, target) in enumerate(
+            [(part, out_hbm.at[m]) for m, part in enumerate(out_parts)]
+            + [(back_hbm.at[done], last_back_ref), (matrix_hbm.at[done], last_matrix_ref)]
+        )
+    ]
     for item in jobs[0][0] + weight_loads:
         item.start()
     for later, _, _ in jobs[1:]:
         for item in later:
             item.start()
-    for item in out_loads:
+    for item in moves:
         item.start()
     jobs[0][1]()
 
@@ -967,10 +973,7 @@
 
     for _, work, _ in jobs[1:]:
         work()
-    for item, onward in zip(out_loads, out_stores):
-        item.wait()
-        onward.start()
-    for item in weight_stores + out_stores:
+    for item in weight_stores + moves:
         item.wait()
     for _, _, stores in jobs:
         for item in stores:
@@ -979,26 +982,25 @@
 
 def finish(table, groups, mine, other, bias_grad, biases, weights, outputs, backs, gots, scale, matrix, after=()):
     capacity, width = weights[0].shape
-    nodes = outputs[0].shape[0]
+    nodes = outputs[0].array.shape[0]
     fixed = lambda i: (0, 0)
     scratch = [pltpu.VMEM((capacity, width), F32)] * 3 + [
-        pltpu.VMEM((MB, nodes, width), BF16),
         pltpu.SemaphoreType.DMA((3,)),
         pltpu.SemaphoreType.DMA((3,)),
-        pltpu.SemaphoreType.DMA((MB * PIECES,)),
-        pltpu.SemaphoreType.DMA((MB * PIECES,)),
+        pltpu.SemaphoreType.DMA((MB + 2,)),
     ]
     for _ in gots:
         scratch += scatter_scratch(nodes, width)
     return launch(
         "finish", functools.partial(finish_kernel, groups), table,
-        [(array, array.shape, fixed) for array in (mine, other)]
+        [(array, array.array.shape, fixed) for array in (mine, other)]
         + [(array, (1, width), fixed) for array in (bias_grad, *biases)]
         + [(array, None, None) for array in (*weights, *outputs, backs, *gots, scale, matrix)],
         [((capacity, width), F32, None, None)] * 3
         + [((1, width), F32, (1, width), fixed)] * 3
-        + [((MB, nodes, width), BF16, None, None)] * 2,
-        after=after, scratch=scratch, vmem=35,
+        + [((MB, nodes, width), BF16, None, None)] * 2
+        + [((nodes, width), BF16, None, None, pltpu.VMEM), ((nodes, nodes), BF16, None, None, pltpu.VMEM)],
+        after=after, scratch=scratch, vmem=32,
     )
 
 
@@ -1043,28 +1045,28 @@
     outputs, pres, mates, away = [], [], [], []
     for m in range(MB):
         chunks = 2 if m == MB - 1 else 1
-        out_m, pre_m, mate_m, mate_weight, *rest = batch(
+        out_m, pre_m, mate_m, *rest = batch(
             table, m, matrix, scale, far[m], here, weight, for_mate, out_grad, bias_row, total, bias_sum, chunks,
             [last],
         )
-        outputs.append(out_m)
+        outputs.append(Kept(out_m))
         pres.append(pre_m)
         mates.append(mate_m)
         away.append([Kept(flip(chunk, "col", 2), None) for chunk in rest[:chunks]])
-        total, bias_sum = rest[chunks], rest[-1]
+        total, bias_sum = Kept(rest[chunks]), rest[-1]
         last = bias_sum
 
-    keep, sent, bias_sum = rest[chunks:]
+    mate_weight, keep, sent, bias_sum = rest[chunks:]
     mine, other, bias_total, backs = sum_over_owners(
         table, groups, capacity, keep, sent, bias_sum, weight, mate_weight, pres, mates, [last]
     )
-    *updated, outputs, input_grads = finish(
-        table, groups, mine, other, bias_total, (bias_row, bias_first_row, bias_second_row),
+    *updated, outputs, input_grads, last_back, last_matrix = finish(
+        table, groups, Kept(mine, None), Kept(other, None), bias_total, (bias_row, bias_first_row, bias_second_row),
         (master_weight, weight_first, weight_second), outputs, backs, [part[0] for part in away[:-1]],
         scale, matrix, [bias_total],
     )
     for chunk, got in enumerate(away[-1]):
-        input_grads = scatter(MB - 1, chunk, backs, got, scale, matrix, input_grads)
+        input_grads = scatter(MB - 1, chunk, Kept(last_back), got, scale, Kept(last_matrix), input_grads)
     return (outputs, input_grads, *updated[:3], *(row.reshape(width) for row in updated[3:]))
 
 

time: 218 us -> 217 us (level)
  Pallas kernels: 205 us -> 201 us
  local copies, waits for them, and re-layouts: 1.58 us -> 5.19 us
    pallas_call x11, Pallas kernels: 205 us -> 201 us  [launch(): pl.pallas_call(kernel, grid_spec=pltpu.PrefetchScalarGridSpec(num_scalar_...]
    unnamed x14 -> x18, local copies, waits for them, and re-layouts: 1.5 us -> 5.11 us
  transfers between devices with their start and end apart: 7 -> 7, of which waited for: 0 -> 0; matrix products, arithmetic and copies ran while one was open for 0% -> 0% of each run, Pallas kernels for 91% -> 90%
where the time goes in v5:
time: 217 us; the launch traced here: 216 us
  Pallas kernels  201 us (93%)
  starting transfers between devices  9.37 us (4%)
  local copies, waits for them, and re-layouts  5.19 us (2%)
    pallas_call x11, Pallas kernels, launch(): pl.pallas_call(kernel, grid_spec=pltpu.PrefetchScalarGridSpec(num_scalar_...  201 us
    ppermute x7, starting transfers between devices, flip(): return lax.ppermute(values, axis, [(i, i ^ bit) for i in range(size)])  9.37 us
    unnamed x18, local copies, waits for them, and re-layouts  5.11 us
  transfers between devices with their start and end apart: 7, of which 0 were waited for; matrix products, arithmetic and copies ran while one was open for 0% of the time, Pallas kernels for 90%

profile of v5, /device:TPU:0, one launch (start us, length us, event | category | flops | bytes accessed | tf_op | source)
XLA Modules:
  0.0 216.4 jit_solution(3382353406617183904)
XLA Ops:
  0.6 2.2 %pick0.1.refs_1_ = bf16[1536,512]{1,0:T(8,128)(2,1)} custom-call(bf16[3,1536,512]{2,1,0:T(8,128)(2,1)} %refs_3_.1), custom_call_target="tpu_custom_call" | custom-call | flops 1 | bytes 1 | tf_op jit(solution)/shard_map/pick0/pallas_call | solution.py:68
  2.8 0.0 copy-start.8
  2.9 0.0 copy-start.7
  2.9 3.0 %collective-permute-start.2 = (bf16[1536,512]{1,0:T(8,128)(2,1)}, bf16[1536,512]{1,0:T(8,128)(2,1)S(1)}, u32[]{:S(2)}, u32[]{:S(2)}) collective-permute-start(bf16[1536,512]{1,0:T(8,128)(2,1)} %pick0.1.refs_1_), channel_id=1, source_target_pairs={{0,2},{1,3},{2,0},{3,1},{4,6},{5,7},{6,4},{7,5},{8,10},{9,11},{10,... | collective-permute-start | bytes 4718600 | tf_op jit(solution)/shard_map/ppermute | solution.py:93
  5.9 2.8 %pick1.1 = (bf16[1536,512]{1,0:T(8,128)(2,1)}, bf16[1536,512]{1,0:T(8,128)(2,1)}) custom-call(bf16[3,1536,512]{2,1,0:T(8,128)(2,1)} %refs_3_.1, bf16[1536,512]{1,0:T(8,128)(2,1)} %pick0.1.refs_1_), custom_call_target="tpu_custom_call" | custom-call | flops 1 | bytes 1 | tf_op jit(solution)/shard_map/pick1/pallas_call | solution.py:68
  8.7 0.1 collective-permute-start.1
  8.8 2.0 collective-permute-start
  10.8 0.0 copy-done.8
  10.8 0.1 select_reduce_fusion
  10.9 0.0 copy-done.7
  10.9 0.1 concatenate.3.refs_0_
  11.0 51.5 %front.1 = (bf16[3,1536,1536]{2,1,0:T(8,128)(2,1)}, f32[3,1536,128]{2,1,0:T(8,128)S(1)}, bf16[3,1536,512]{2,1,0:T(8,128)(2,1)S(1)}, bf16[8,512,512]{2,1,0:T(8,128)(2,1)}) custom-call(s32[21]{0:T(128)S(1)} %concatenate.3.refs_0_, f32[512,512]{1,0:T(8,128)} %refs_7_.7, s32[3,16,1536]{2,1,0:T(8,128)} %bitcast.16, bf16[3,1536,512]{2,1,0:T(8,128)(2,1)} %refs_3_.1, ...), custom_call_target="tpu_custom_call" | custom-call | flops 1 | bytes 1 | tf_op jit(solution)/shard_map/front/pallas_call | solution.py:68
  62.5 0.0 copy-start.4
  62.5 7.2 %place.1 = (bf16[4,512,512]{2,1,0:T(8,128)(2,1)S(1)}, bf16[2,512,512]{2,1,0:T(8,128)(2,1)S(1)}) custom-call(s32[21]{0:T(128)S(1)} %concatenate.3.refs_0_, bf16[8,512,512]{2,1,0:T(8,128)(2,1)} %get-tuple-element.55.refs_1_), custom_call_target="tpu_custom_call" | custom-call | flops 1 | bytes 1 | tf_op jit(solution)/shard_map/place/pallas_call | solution.py:68
  69.7 0.0 collective-permute-done.2.refs_3_
  69.7 0.0 copy-start.2
  69.7 1.1 copy-done.2
  70.9 0.0 copy-done.4
  70.9 0.0 copy-start.3
  70.9 1.4 copy-done.3
  72.3 19.6 %batch0.1 = (bf16[1536,512]{1,0:T(8,128)(2,1)S(1)}, bf16[1536,512]{1,0:T(8,128)(2,1)}, bf16[1536,512]{1,0:T(8,128)(2,1)}, bf16[1536,512]{1,0:T(8,128)(2,1)}, f32...) custom-call(s32[21]{0:T(128)S(1)} %concatenate.3.refs_0_, bf16[3,1536,1536]{2,1,0:T(8,128)(2,1)} %get-tuple-element.52.refs_1_.refs_17_, ...), custom_call_target="tpu_custom_call" | custom-call | flops 1 | bytes 1 | tf_op jit(solution)/shard_map/batch0/pallas_call | solution.py:68
  91.9 0.6 collective-permute-start.3
  92.5 0.0 collective-permute-done.1.refs_3_
  92.5 19.9 %batch1.1 = (bf16[1536,512]{1,0:T(8,128)(2,1)S(1)}, bf16[1536,512]{1,0:T(8,128)(2,1)}, bf16[1536,512]{1,0:T(8,128)(2,1)}, bf16[1536,512]{1,0:T(8,128)(2,1)}, f32...) custom-call(s32[21]{0:T(128)S(1)} %concatenate.3.refs_0_, bf16[3,1536,1536]{2,1,0:T(8,128)(2,1)} %get-tuple-element.52.refs_1_.refs_17_, ...), custom_call_target="tpu_custom_call" | custom-call | flops 1 | bytes 1 | tf_op jit(solution)/shard_map/batch1/pallas_call | solution.py:68
  112.4 1.6 collective-permute-start.4
  114.0 0.0 collective-permute-done.refs_3_
  114.0 20.3 %batch2.1 = (bf16[1536,512]{1,0:T(8,128)(2,1)S(1)}, bf16[1536,512]{1,0:T(8,128)(2,1)}, bf16[1536,512]{1,0:T(8,128)(2,1)}, bf16[1536,256]{1,0:T(8,128)(2,1)}, bf1...) custom-call(s32[21]{0:T(128)S(1)} %concatenate.3.refs_0_, ...), custom_call_target="tpu_custom_call" | custom-call | flops 1 | bytes 1 | tf_op jit(solution)/shard_map/batch2/pallas_call | solution.py:68
  134.3 0.6 collective-permute-start.6
  134.9 1.5 collective-permute-start.5
  136.4 0.0 copy-start.5
  136.4 0.0 copy-start.6
  136.4 54.8 %sum.1 = (f32[512,256]{1,0:T(8,128)S(1)}, bf16[512,256]{1,0:T(8,128)(2,1)S(1)}, f32[1,512]{1,0:T(1,128)S(1)}, bf16[3,1536,512]{2,1,0:T(8,128)(2,1)}) custom-call(s32[21]{0:T(128)S(1)} %concatenate.3.refs_0_, f32[2048,256]{1,0:T(8,128)} %get-tuple-element.63.refs_1_, bf16[2048,256]{1,0:T(8,128)(2,1)} %get-tuple-element.64.refs_2_, ...), custom_call_target="tpu_custom_call" | custom-call | flops 1 | bytes 1 | tf_op jit(solution)/shard_map/sum/pallas_call | solution.py:68
  191.2 0.0 collective-permute-done.3.refs_14_
  191.2 0.0 copy-start
  191.2 1.1 copy-done
  192.4 0.0 collective-permute-done.4.refs_15_
  192.4 0.0 copy-done.5
  192.4 0.0 copy-done.6
  192.4 0.0 copy-start.1
  192.4 1.4 copy-done.1
  193.8 13.8 %finish.1 = (f32[512,512]{1,0:T(8,128)}, f32[512,512]{1,0:T(8,128)}, f32[512,512]{1,0:T(8,128)}, f32[1,512]{1,0:T(1,128)}, f32[1,512]{1,0:T(1,128)}, /*index=5*/...) custom-call(s32[21]{0:T(128)S(1)} %concatenate.3.refs_0_, ...), custom_call_target="tpu_custom_call" | custom-call | flops 1 | bytes 1 | tf_op jit(solution)/shard_map/finish/pallas_call | solution.py:68
  207.6 0.0 collective-permute-done.6.refs_1_
  207.6 4.3 %scatter2_0.1.refs_4_ = bf16[3,1536,512]{2,1,0:T(8,128)(2,1)} custom-call(bf16[1536,512]{1,0:T(8,128)(2,1)S(1)} %get-tuple-element.83.refs_0_, bf16[1536,256]{1,0:T(8,128)(2,1)S(1)} %collective-permute-done.6.refs_1_, f32[3,1536,128]{2,1,0:T(8,128)S(1)} %get-tuple-element.53.refs_2_.refs_16_, ...), custom_call_target="tpu_custom_call", output_to_operand_aliasing={{}: (4, {})} | custom-call | flops 1 | bytes 1 | tf_op jit(solution)/shard_map/scatter2_0/pallas_call | solution.py:68
  211.9 0.0 collective-permute-done.5.refs_1_
  211.9 4.3 %scatter2_1.1 = bf16[3,1536,512]{2,1,0:T(8,128)(2,1)} custom-call(bf16[1536,512]{1,0:T(8,128)(2,1)S(1)} %get-tuple-element.83.refs_0_, bf16[1536,256]{1,0:T(8,128)(2,1)S(1)} %collective-permute-done.5.refs_1_, f32[3,1536,128]{2,1,0:T(8,128)S(1)} %get-tuple-element.53.refs_2_.refs_16_, ...), custom_call_target="tpu_custom_call", output_to_operand_aliasing={{}: (4, {})} | custom-call | flops 1 | bytes 1 | tf_op jit(solution)/shard_map/scatter2_1/pallas_call | solution.py:68
Async XLA Ops:
  2.8 7.9 %copy-start.8 = (s32[8]{0:T(128)S(1)}, s32[8]{0:T(128)}, u32[]{:S(2)}) copy-start(s32[8]{0:T(128)} %param.14) | copy-start | bytes 100
  2.9 8.0 %copy-start.7 = (s32[3,1]{0,1:T(1,128)S(1)}, s32[3,1]{0,1:T(1,128)}, u32[]{:S(2)}) copy-start(s32[3,1]{0,1:T(1,128)} %param.13) | copy-start | bytes 40
  2.9 66.9 %collective-permute-start.2 = (bf16[1536,512]{1,0:T(8,128)(2,1)}, bf16[1536,512]{1,0:T(8,128)(2,1)S(1)}, u32[]{:S(2)}, u32[]{:S(2)}) collective-permute-start(bf16[1536,512]{1,0:T(8,128)(2,1)} %pick0.1.refs_1_), channel_id=1, source_target_pairs={{0,2},{1,3},{2,0},{3,1},{4,6},{5,7},{6,4},{7,5},{8,10},{9,11},{10,... | collective-permute-start | bytes 4718600 | tf_op jit(solution)/shard_map/ppermute | solution.py:93
  8.7 83.8 %collective-permute-start.1 = (bf16[1536,512]{1,0:T(8,128)(2,1)}, bf16[1536,512]{1,0:T(8,128)(2,1)}, u32[]{:S(2)}, u32[]{:S(2)}) collective-permute-start(bf16[1536,512]{1,0:T(8,128)(2,1)} %get-tuple-element.58), channel_id=1, source_target_pairs={{0,2},{1,3},{2,0},{3,1},{4,6},{5,7},{6,4},{7,5},{8,10},{9,11},{10,... | collective-permute-start | bytes 4718600 | tf_op jit(solution)/shard_map/ppermute | solution.py:93
  8.8 105.2 %collective-permute-start = (bf16[1536,512]{1,0:T(8,128)(2,1)}, bf16[1536,512]{1,0:T(8,128)(2,1)}, u32[]{:S(2)}, u32[]{:S(2)}) collective-permute-start(bf16[1536,512]{1,0:T(8,128)(2,1)} %get-tuple-element.51.refs_4_), channel_id=1, source_target_pairs={{0,2},{1,3},{2,0},{3,1},{4,6},{5,7},{6,4},{7,5},{8,10},{9,11},{10,... | collective-permute-start | bytes 4718600 | tf_op jit(solution)/shard_map/ppermute | solution.py:93
  62.5 8.4 %copy-start.4 = (f32[512]{0:T(512)S(1)}, f32[512]{0:T(512)}, u32[]{:S(2)}) copy-start(f32[512]{0:T(512)} %param.18) | copy-start | bytes 6148
  69.7 1.1 copy-start.2
  70.9 1.4 copy-start.3
  91.9 99.3 %collective-permute-start.3 = (bf16[1536,512]{1,0:T(8,128)(2,1)}, bf16[1536,512]{1,0:T(8,128)(2,1)S(1)}, u32[]{:S(2)}, u32[]{:S(2)}) collective-permute-start(bf16[1536,512]{1,0:T(8,128)(2,1)} %get-tuple-element.80), channel_id=1, source_target_pairs={{0,2},{1,3},{2,0},{3,1},{4,6},{5,7},{6,4},{7,5},{8,10},{9,11},{10,... | collective-permute-start | bytes 4718600 | tf_op jit(solution)/shard_map/ppermute | solution.py:93
  112.4 79.9 %collective-permute-start.4 = (bf16[1536,512]{1,0:T(8,128)(2,1)}, bf16[1536,512]{1,0:T(8,128)(2,1)S(1)}, u32[]{:S(2)}, u32[]{:S(2)}) collective-permute-start(bf16[1536,512]{1,0:T(8,128)(2,1)} %get-tuple-element.81), channel_id=1, source_target_pairs={{0,2},{1,3},{2,0},{3,1},{4,6},{5,7},{6,4},{7,5},{8,10},{9,11},{10,... | collective-permute-start | bytes 4718600 | tf_op jit(solution)/shard_map/ppermute | solution.py:93
  134.3 73.3 %collective-permute-start.6 = (bf16[1536,256]{1,0:T(8,128)(2,1)}, bf16[1536,256]{1,0:T(8,128)(2,1)S(1)}, u32[]{:S(2)}, u32[]{:S(2)}) collective-permute-start(bf16[1536,256]{1,0:T(8,128)(2,1)} %get-tuple-element.86), channel_id=1, source_target_pairs={{0,2},{1,3},{2,0},{3,1},{4,6},{5,7},{6,4},{7,5},{8,10},{9,11},{10,... | collective-permute-start | bytes 2359304 | tf_op jit(solution)/shard_map/ppermute | solution.py:93
  134.9 77.0 %collective-permute-start.5 = (bf16[1536,256]{1,0:T(8,128)(2,1)}, bf16[1536,256]{1,0:T(8,128)(2,1)S(1)}, u32[]{:S(2)}, u32[]{:S(2)}) collective-permute-start(bf16[1536,256]{1,0:T(8,128)(2,1)} %get-tuple-element.84), channel_id=1, source_target_pairs={{0,2},{1,3},{2,0},{3,1},{4,6},{5,7},{6,4},{7,5},{8,10},{9,11},{10,... | collective-permute-start | bytes 2359304 | tf_op jit(solution)/shard_map/ppermute | solution.py:93
  136.4 55.9 %copy-start.5 = (f32[512]{0:T(512)S(1)}, f32[512]{0:T(512)}, u32[]{:S(2)}) copy-start(f32[512]{0:T(512)} %param.19) | copy-start | bytes 6148
  136.4 55.9 %copy-start.6 = (f32[512]{0:T(512)S(1)}, f32[512]{0:T(512)}, u32[]{:S(2)}) copy-start(f32[512]{0:T(512)} %param.20) | copy-start | bytes 6148
  191.2 1.1 copy-start
  192.4 1.4 copy-start.1

commit v6 on v5

--- a/solution.py
+++ b/solution.py
@@ -156,6 +156,20 @@
             loads.append(pltpu.make_async_copy(piece(source, i), piece(buffer, i), load.at[place]))
             stores.append(pltpu.make_async_copy(piece(buffer, i), piece(target, i), store.at[place]))
     return loads, stores
+
+
+def first_kernel(source_hbm, target_ref, semaphore):
+    copy = pltpu.make_async_copy(source_hbm.at[0], target_ref, semaphore)
+    copy.start()
+    copy.wait()
+
+
+def pick_first(stacked):
+    return launch(
+        "first", first_kernel, None,
+        [(stacked, None, None)], [(stacked.shape[1:], stacked.dtype, None, None, pltpu.VMEM)],
+        scratch=[pltpu.SemaphoreType.DMA],
+    )
 
 
 def pick_kernel(batches, source_ref, *refs):
@@ -368,7 +382,7 @@
         [
             ((MB, nodes, nodes), BF16, (1, nodes, TILE), lambda b, i: (b, 0, i), pltpu.HBM),
             ((MB, nodes, LANES), F32, (1, TILE, LANES), lambda b, i: (b, i, 0), pltpu.VMEM),
-            ((MB, nodes, width), BF16, (1, TILE, width), lambda b, i: (b, i, 0), pltpu.VMEM),
+            ((MB, nodes, width), BF16, (1, TILE, width), lambda b, i: (b, i, 0), pltpu.HBM),
             ((groups, capacity, width), BF16, None, None),
         ],
         grid=(MB, nodes // TILE), after=after, barrier=FRONT_ID, vmem=20,
@@ -1033,12 +1047,14 @@
         array.reshape(1, width) for array in (master_bias, bias_first, bias_second)
     )
 
-    picked = pick(features, (0,))
-    picked = picked + pick(features, tuple(range(1, MB)), picked)
+    picked = pick_first(features)
+    picked = picked + pick(features, tuple(range(1, MB)), [Kept(picked[0])])
     far = [Kept(flip(array, "col", 2), None) for array in picked]
 
-    matrix, *kept, slots = front(table, groups, master_weight, jnp.swapaxes(neighbours, 1, 2), features, [picked[-1]])
-    scale, here = (Kept(array) for array in kept)
+    matrix, scale, here, slots = front(
+        table, groups, master_weight, jnp.swapaxes(neighbours, 1, 2), features, [picked[-1]]
+    )
+    scale = Kept(scale)
     weight, for_mate = (Kept(array) for array in place(table, slots))
     last = for_mate
     total, bias_sum = None, None

time: 217 us -> 213 us (0.982)
  local copies, waits for them, and re-layouts: 5.19 us -> 0.11 us
    unnamed x18 -> x10, local copies, waits for them, and re-layouts: 5.11 us -> 0.03 us
  transfers between devices with their start and end apart: 7 -> 7, of which waited for: 0 -> 1; matrix products, arithmetic and copies ran while one was open for 0% -> 0% of each run, Pallas kernels for 90% -> 91%
where the time goes in v6:
time: 213 us
  Pallas kernels  200 us (94%)
  starting transfers between devices  9.37 us (4%)
    pallas_call x11, Pallas kernels, launch(): pl.pallas_call(kernel, grid_spec=pltpu.PrefetchScalarGridSpec(num_scalar_...  200 us
    ppermute x7, starting transfers between devices, flip(): return lax.ppermute(values, axis, [(i, i ^ bit) for i in range(size)])  9.37 us
  transfers between devices with their start and end apart: 7, of which 1 were waited for; matrix products, arithmetic and copies ran while one was open for 0% of the time, Pallas kernels for 91%

profile of v6, /device:TPU:0, one launch (start us, length us, event | category | flops | bytes accessed | tf_op | source)
XLA Modules:
  0.0 212.5 jit_solution(15604185188602863165)
XLA Ops:
  0.6 1.4 first.1.refs_1_
  2.1 0.0 copy-start.4
  2.1 0.0 copy-start.3
  2.1 3.0 %collective-permute-start.2 = (bf16[1536,512]{1,0:T(8,128)(2,1)S(1)}, bf16[1536,512]{1,0:T(8,128)(2,1)}, u32[]{:S(2)}, u32[]{:S(2)}) collective-permute-start(bf16[1536,512]{1,0:T(8,128)(2,1)S(1)} %first.1.refs_1_), channel_id=1, source_target_pairs={{0,2},{1,3},{2,0},{3,1},{4,6},{5,7},{6,4},{7,5},{8,10},{9,11},{10,... | collective-permute-start | bytes 4718600 | tf_op jit(solution)/shard_map/ppermute | solution.py:93
  5.1 2.8 %pick1.1 = (bf16[1536,512]{1,0:T(8,128)(2,1)}, bf16[1536,512]{1,0:T(8,128)(2,1)}) custom-call(bf16[3,1536,512]{2,1,0:T(8,128)(2,1)} %refs_3_.1, bf16[1536,512]{1,0:T(8,128)(2,1)S(1)} %first.1.refs_1_), custom_call_target="tpu_custom_call" | custom-call | flops 1 | bytes 1 | tf_op jit(solution)/shard_map/pick1/pallas_call | solution.py:68
  7.9 0.1 collective-permute-start.1
  8.0 2.0 collective-permute-start
  10.0 0.0 copy-done.4
  10.0 0.1 select_reduce_fusion
  10.1 0.0 copy-done.3
  10.1 0.1 concatenate.3.refs_0_
  10.2 51.5 %front.1 = (bf16[3,1536,1536]{2,1,0:T(8,128)(2,1)}, f32[3,1536,128]{2,1,0:T(8,128)S(1)}, bf16[3,1536,512]{2,1,0:T(8,128)(2,1)}, bf16[8,512,512]{2,1,0:T(8,128)(2,1)}) custom-call(s32[21]{0:T(128)S(1)} %concatenate.3.refs_0_, f32[512,512]{1,0:T(8,128)} %refs_7_.7, s32[3,16,1536]{2,1,0:T(8,128)} %bitcast.16, bf16[3,1536,512]{2,1,0:T(8,128)(2,1)} %refs_3_.1, ...), custom_call_target="tpu_custom_call" | custom-call | flops 1 | bytes 1 | tf_op jit(solution)/shard_map/front/pallas_call | solution.py:68
  61.7 0.0 copy-start
  61.7 7.2 %place.1 = (bf16[4,512,512]{2,1,0:T(8,128)(2,1)S(1)}, bf16[2,512,512]{2,1,0:T(8,128)(2,1)S(1)}) custom-call(s32[21]{0:T(128)S(1)} %concatenate.3.refs_0_, bf16[8,512,512]{2,1,0:T(8,128)(2,1)} %get-tuple-element.55.refs_1_), custom_call_target="tpu_custom_call" | custom-call | flops 1 | bytes 1 | tf_op jit(solution)/shard_map/place/pallas_call | solution.py:68
  69.0 0.0 collective-permute-done.2.refs_3_
  69.0 0.0 copy-done
  69.0 19.4 %batch0.1 = (bf16[1536,512]{1,0:T(8,128)(2,1)S(1)}, bf16[1536,512]{1,0:T(8,128)(2,1)}, bf16[1536,512]{1,0:T(8,128)(2,1)}, bf16[1536,512]{1,0:T(8,128)(2,1)}, f32...) custom-call(s32[21]{0:T(128)S(1)} %concatenate.3.refs_0_, bf16[3,1536,1536]{2,1,0:T(8,128)(2,1)} %get-tuple-element.52.refs_1_.refs_17_, ...), custom_call_target="tpu_custom_call" | custom-call | flops 1 | bytes 1 | tf_op jit(solution)/shard_map/batch0/pallas_call | solution.py:68
  88.4 0.6 collective-permute-start.3
  89.0 0.0 collective-permute-done.1.refs_3_
  89.0 20.5 %batch1.1 = (bf16[1536,512]{1,0:T(8,128)(2,1)S(1)}, bf16[1536,512]{1,0:T(8,128)(2,1)}, bf16[1536,512]{1,0:T(8,128)(2,1)}, bf16[1536,512]{1,0:T(8,128)(2,1)}, f32...) custom-call(s32[21]{0:T(128)S(1)} %concatenate.3.refs_0_, bf16[3,1536,1536]{2,1,0:T(8,128)(2,1)} %get-tuple-element.52.refs_1_.refs_17_, ...), custom_call_target="tpu_custom_call" | custom-call | flops 1 | bytes 1 | tf_op jit(solution)/shard_map/batch1/pallas_call | solution.py:68
  109.5 1.6 collective-permute-start.4
  111.1 0.0 collective-permute-done.refs_3_
  111.1 20.2 %batch2.1 = (bf16[1536,512]{1,0:T(8,128)(2,1)S(1)}, bf16[1536,512]{1,0:T(8,128)(2,1)}, bf16[1536,512]{1,0:T(8,128)(2,1)}, bf16[1536,256]{1,0:T(8,128)(2,1)}, bf1...) custom-call(s32[21]{0:T(128)S(1)} %concatenate.3.refs_0_, ...), custom_call_target="tpu_custom_call" | custom-call | flops 1 | bytes 1 | tf_op jit(solution)/shard_map/batch2/pallas_call | solution.py:68
  131.3 0.6 collective-permute-start.6
  131.9 1.5 collective-permute-start.5
  133.4 0.0 copy-start.1
  133.4 0.0 copy-start.2
  133.4 54.5 %sum.1 = (f32[512,256]{1,0:T(8,128)S(1)}, bf16[512,256]{1,0:T(8,128)(2,1)S(1)}, f32[1,512]{1,0:T(1,128)S(1)}, bf16[3,1536,512]{2,1,0:T(8,128)(2,1)}) custom-call(s32[21]{0:T(128)S(1)} %concatenate.3.refs_0_, f32[2048,256]{1,0:T(8,128)} %get-tuple-element.63.refs_1_, bf16[2048,256]{1,0:T(8,128)(2,1)} %get-tuple-element.64.refs_2_, ...), custom_call_target="tpu_custom_call" | custom-call | flops 1 | bytes 1 | tf_op jit(solution)/shard_map/sum/pallas_call | solution.py:68
  187.9 0.0 collective-permute-done.3.refs_14_
  187.9 0.0 collective-permute-done.4.refs_15_
  187.9 0.0 copy-done.1
  187.9 0.0 copy-done.2
  187.9 13.9 %finish.1 = (f32[512,512]{1,0:T(8,128)}, f32[512,512]{1,0:T(8,128)}, f32[512,512]{1,0:T(8,128)}, f32[1,512]{1,0:T(1,128)}, f32[1,512]{1,0:T(1,128)}, /*index=5*/...) custom-call(s32[21]{0:T(128)S(1)} %concatenate.3.refs_0_, ...), custom_call_target="tpu_custom_call" | custom-call | flops 1 | bytes 1 | tf_op jit(solution)/shard_map/finish/pallas_call | solution.py:68
  201.8 0.0 collective-permute-done.6.refs_1_
  201.8 4.3 %scatter2_0.1.refs_4_ = bf16[3,1536,512]{2,1,0:T(8,128)(2,1)} custom-call(bf16[1536,512]{1,0:T(8,128)(2,1)S(1)} %get-tuple-element.83.refs_0_, bf16[1536,256]{1,0:T(8,128)(2,1)S(1)} %collective-permute-done.6.refs_1_, f32[3,1536,128]{2,1,0:T(8,128)S(1)} %get-tuple-element.53.refs_2_.refs_16_, ...), custom_call_target="tpu_custom_call", output_to_operand_aliasing={{}: (4, {})} | custom-call | flops 1 | bytes 1 | tf_op jit(solution)/shard_map/scatter2_0/pallas_call | solution.py:68
  206.1 1.9 collective-permute-done.5.refs_1_
  208.0 4.3 %scatter2_1.1 = bf16[3,1536,512]{2,1,0:T(8,128)(2,1)} custom-call(bf16[1536,512]{1,0:T(8,128)(2,1)S(1)} %get-tuple-element.83.refs_0_, bf16[1536,256]{1,0:T(8,128)(2,1)S(1)} %collective-permute-done.5.refs_1_, f32[3,1536,128]{2,1,0:T(8,128)S(1)} %get-tuple-element.53.refs_2_.refs_16_, ...), custom_call_target="tpu_custom_call", output_to_operand_aliasing={{}: (4, {})} | custom-call | flops 1 | bytes 1 | tf_op jit(solution)/shard_map/scatter2_1/pallas_call | solution.py:68
Async XLA Ops:
  2.1 7.9 %copy-start.4 = (s32[8]{0:T(128)S(1)}, s32[8]{0:T(128)}, u32[]{:S(2)}) copy-start(s32[8]{0:T(128)} %param.14) | copy-start | bytes 100
  2.1 8.0 %copy-start.3 = (s32[3,1]{0,1:T(1,128)S(1)}, s32[3,1]{0,1:T(1,128)}, u32[]{:S(2)}) copy-start(s32[3,1]{0,1:T(1,128)} %param.13) | copy-start | bytes 40
  2.1 66.9 %collective-permute-start.2 = (bf16[1536,512]{1,0:T(8,128)(2,1)S(1)}, bf16[1536,512]{1,0:T(8,128)(2,1)}, u32[]{:S(2)}, u32[]{:S(2)}) collective-permute-start(bf16[1536,512]{1,0:T(8,128)(2,1)S(1)} %first.1.refs_1_), channel_id=1, source_target_pairs={{0,2},{1,3},{2,0},{3,1},{4,6},{5,7},{6,4},{7,5},{8,10},{9,11},{10,... | collective-permute-start | bytes 4718600 | tf_op jit(solution)/shard_map/ppermute | solution.py:93
  7.9 81.1 %collective-permute-start.1 = (bf16[1536,512]{1,0:T(8,128)(2,1)}, bf16[1536,512]{1,0:T(8,128)(2,1)}, u32[]{:S(2)}, u32[]{:S(2)}) collective-permute-start(bf16[1536,512]{1,0:T(8,128)(2,1)} %get-tuple-element.58), channel_id=1, source_target_pairs={{0,2},{1,3},{2,0},{3,1},{4,6},{5,7},{6,4},{7,5},{8,10},{9,11},{10,... | collective-permute-start | bytes 4718600 | tf_op jit(solution)/shard_map/ppermute | solution.py:93
  8.0 103.1 %collective-permute-start = (bf16[1536,512]{1,0:T(8,128)(2,1)}, bf16[1536,512]{1,0:T(8,128)(2,1)S(1)}, u32[]{:S(2)}, u32[]{:S(2)}) collective-permute-start(bf16[1536,512]{1,0:T(8,128)(2,1)} %get-tuple-element.51.refs_4_), channel_id=1, source_target_pairs={{0,2},{1,3},{2,0},{3,1},{4,6},{5,7},{6,4},{7,5},{8,10},{9,11},{10,... | collective-permute-start | bytes 4718600 | tf_op jit(solution)/shard_map/ppermute | solution.py:93
  61.7 7.3 %copy-start = (f32[512]{0:T(512)S(1)}, f32[512]{0:T(512)}, u32[]{:S(2)}) copy-start(f32[512]{0:T(512)} %param.18) | copy-start | bytes 6148
  88.4 99.5 %collective-permute-start.3 = (bf16[1536,512]{1,0:T(8,128)(2,1)}, bf16[1536,512]{1,0:T(8,128)(2,1)S(1)}, u32[]{:S(2)}, u32[]{:S(2)}) collective-permute-start(bf16[1536,512]{1,0:T(8,128)(2,1)} %get-tuple-element.80), channel_id=1, source_target_pairs={{0,2},{1,3},{2,0},{3,1},{4,6},{5,7},{6,4},{7,5},{8,10},{9,11},{10,... | collective-permute-start | bytes 4718600 | tf_op jit(solution)/shard_map/ppermute | solution.py:93
  109.5 78.4 %collective-permute-start.4 = (bf16[1536,512]{1,0:T(8,128)(2,1)}, bf16[1536,512]{1,0:T(8,128)(2,1)S(1)}, u32[]{:S(2)}, u32[]{:S(2)}) collective-permute-start(bf16[1536,512]{1,0:T(8,128)(2,1)} %get-tuple-element.81), channel_id=1, source_target_pairs={{0,2},{1,3},{2,0},{3,1},{4,6},{5,7},{6,4},{7,5},{8,10},{9,11},{10,... | collective-permute-start | bytes 4718600 | tf_op jit(solution)/shard_map/ppermute | solution.py:93
  131.3 70.5 %collective-permute-start.6 = (bf16[1536,256]{1,0:T(8,128)(2,1)}, bf16[1536,256]{1,0:T(8,128)(2,1)S(1)}, u32[]{:S(2)}, u32[]{:S(2)}) collective-permute-start(bf16[1536,256]{1,0:T(8,128)(2,1)} %get-tuple-element.86), channel_id=1, source_target_pairs={{0,2},{1,3},{2,0},{3,1},{4,6},{5,7},{6,4},{7,5},{8,10},{9,11},{10,... | collective-permute-start | bytes 2359304 | tf_op jit(solution)/shard_map/ppermute | solution.py:93
  131.9 76.1 %collective-permute-start.5 = (bf16[1536,256]{1,0:T(8,128)(2,1)}, bf16[1536,256]{1,0:T(8,128)(2,1)S(1)}, u32[]{:S(2)}, u32[]{:S(2)}) collective-permute-start(bf16[1536,256]{1,0:T(8,128)(2,1)} %get-tuple-element.84), channel_id=1, source_target_pairs={{0,2},{1,3},{2,0},{3,1},{4,6},{5,7},{6,4},{7,5},{8,10},{9,11},{10,... | collective-permute-start | bytes 2359304 | tf_op jit(solution)/shard_map/ppermute | solution.py:93
  133.4 54.5 %copy-start.1 = (f32[512]{0:T(512)S(1)}, f32[512]{0:T(512)}, u32[]{:S(2)}) copy-start(f32[512]{0:T(512)} %param.19) | copy-start | bytes 6148
  133.4 54.5 %copy-start.2 = (f32[512]{0:T(512)S(1)}, f32[512]{0:T(512)}, u32[]{:S(2)}) copy-start(f32[512]{0:T(512)} %param.20) | copy-start | bytes 6148

commit v7 on v6

--- a/solution.py
+++ b/solution.py
@@ -640,9 +640,9 @@
     )
 
 
-def scatter_job(m, columns, own_source, got_source, scale_source, matrix_source, grads_hbm, scratch, semaphores):
+def scatter_job(m, tile, columns, own_source, got_source, scale_source, matrix_source, grads_hbm, scratch, semaphores):
     own_ref, got_ref, scale_ref, matrix_ref, sum_ref, grad_ref = scratch
-    steps = matrix_ref.shape[0] // WIDE
+    steps = matrix_ref.shape[0] // tile
     loads = [
         pltpu.make_async_copy(source, target, semaphores.at[i])
         for i, (source, target) in enumerate(
@@ -651,7 +651,7 @@
     ]
     tiles, stores = [], []
     for i in range(steps):
-        rows = pl.ds(i * WIDE, WIDE)
+        rows = pl.ds(i * tile, tile)
         tiles.append(pltpu.make_async_copy(matrix_source.at[rows], matrix_ref.at[rows], semaphores.at[3 + i]))
         stores.append(
             pltpu.make_async_copy(grad_ref.at[rows], grads_hbm.at[m, rows, columns], semaphores.at[3 + steps + i])
@@ -664,7 +664,7 @@
         sum_ref[...] = scaled(grad_mixed.astype(F32), scale_ref[...]).astype(BF16)
         for i in range(steps):
             tiles[i].wait()
-            rows = slice(i * WIDE, (i + 1) * WIDE)
+            rows = slice(i * tile, (i + 1) * tile)
             grad_ref[rows, :] = product(matrix_ref[rows, :], sum_ref[...]).astype(BF16)
             stores[i].start()
 
@@ -686,7 +686,7 @@
 def scatter_kernel(m, chunk, own_hbm, got_hbm, scale_hbm, matrix_hbm, grads_hbm, *refs):
     width = got_hbm.shape[1]
     loads, work, stores = scatter_job(
-        m, pl.ds(chunk * width, width), own_hbm, got_hbm, scale_hbm, matrix_hbm, grads_hbm, refs[:6], refs[6]
+        m, own_hbm.shape[0], pl.ds(chunk * width, width), own_hbm, got_hbm, scale_hbm, matrix_hbm, grads_hbm, refs[:6], refs[6]
     )
     for item in loads:
         item.start()
@@ -933,7 +933,7 @@
     weights, (weight_load, weight_store, store), refs = refs[:3], refs[3:6], refs[6:]
     jobs = [
         scatter_job(
-            m, pl.ds(0, back_hbm.shape[2]), back_hbm.at[m], gots[m], scale_hbm, matrix_hbm.at[m], grads_hbm,
+            m, WIDE, pl.ds(0, back_hbm.shape[2]), back_hbm.at[m], gots[m], scale_hbm, matrix_hbm.at[m], grads_hbm,
             refs[7 * m : 7 * m + 6], refs[7 * m + 6],
         )
         for m in range(done)

time: 213 us -> 212 us (level)
  no operation moved by 1% of the time
where the time goes in v7:
time: 212 us
  Pallas kernels  198 us (93%)
  starting transfers between devices  9.37 us (4%)
  waiting for transfers between devices  2.94 us (1%)
    pallas_call x11, Pallas kernels, launch(): pl.pallas_call(kernel, grid_spec=pltpu.PrefetchScalarGridSpec(num_scalar_...  198 us
    ppermute x7, starting transfers between devices, flip(): return lax.ppermute(values, axis, [(i, i ^ bit) for i in range(size)])  9.37 us
  transfers between devices with their start and end apart: 7, of which 1 were waited for; matrix products, arithmetic and copies ran while one was open for 0% of the time, Pallas kernels for 91%

profile of v7, /device:TPU:0, one launch (start us, length us, event | category | flops | bytes accessed | tf_op | source)
XLA Modules:
  0.0 211.6 jit_solution(7440314790486657084)
XLA Ops:
  0.6 1.4 first.1.refs_1_
  2.1 0.0 copy-start.4
  2.1 0.0 copy-start.3
  2.1 3.0 %collective-permute-start.2 = (bf16[1536,512]{1,0:T(8,128)(2,1)S(1)}, bf16[1536,512]{1,0:T(8,128)(2,1)}, u32[]{:S(2)}, u32[]{:S(2)}) collective-permute-start(bf16[1536,512]{1,0:T(8,128)(2,1)S(1)} %first.1.refs_1_), channel_id=1, source_target_pairs={{0,2},{1,3},{2,0},{3,1},{4,6},{5,7},{6,4},{7,5},{8,10},{9,11},{10,... | collective-permute-start | bytes 4718600 | tf_op jit(solution)/shard_map/ppermute | solution.py:93
  5.1 2.8 %pick1.1 = (bf16[1536,512]{1,0:T(8,128)(2,1)}, bf16[1536,512]{1,0:T(8,128)(2,1)}) custom-call(bf16[3,1536,512]{2,1,0:T(8,128)(2,1)} %refs_3_.1, bf16[1536,512]{1,0:T(8,128)(2,1)S(1)} %first.1.refs_1_), custom_call_target="tpu_custom_call" | custom-call | flops 1 | bytes 1 | tf_op jit(solution)/shard_map/pick1/pallas_call | solution.py:68
  7.9 0.1 collective-permute-start.1
  8.0 2.0 collective-permute-start
  10.0 0.0 copy-done.4
  10.0 0.1 select_reduce_fusion
  10.1 0.0 copy-done.3
  10.1 0.1 concatenate.3.refs_0_
  10.2 51.5 %front.1 = (bf16[3,1536,1536]{2,1,0:T(8,128)(2,1)}, f32[3,1536,128]{2,1,0:T(8,128)S(1)}, bf16[3,1536,512]{2,1,0:T(8,128)(2,1)}, bf16[8,512,512]{2,1,0:T(8,128)(2,1)}) custom-call(s32[21]{0:T(128)S(1)} %concatenate.3.refs_0_, f32[512,512]{1,0:T(8,128)} %refs_7_.7, s32[3,16,1536]{2,1,0:T(8,128)} %bitcast.16, bf16[3,1536,512]{2,1,0:T(8,128)(2,1)} %refs_3_.1, ...), custom_call_target="tpu_custom_call" | custom-call | flops 1 | bytes 1 | tf_op jit(solution)/shard_map/front/pallas_call | solution.py:68
  61.7 0.0 copy-start
  61.7 7.2 %place.1 = (bf16[4,512,512]{2,1,0:T(8,128)(2,1)S(1)}, bf16[2,512,512]{2,1,0:T(8,128)(2,1)S(1)}) custom-call(s32[21]{0:T(128)S(1)} %concatenate.3.refs_0_, bf16[8,512,512]{2,1,0:T(8,128)(2,1)} %get-tuple-element.55.refs_1_), custom_call_target="tpu_custom_call" | custom-call | flops 1 | bytes 1 | tf_op jit(solution)/shard_map/place/pallas_call | solution.py:68
  69.0 0.0 collective-permute-done.2.refs_3_
  69.0 0.0 copy-done
  69.0 19.4 %batch0.1 = (bf16[1536,512]{1,0:T(8,128)(2,1)S(1)}, bf16[1536,512]{1,0:T(8,128)(2,1)}, bf16[1536,512]{1,0:T(8,128)(2,1)}, bf16[1536,512]{1,0:T(8,128)(2,1)}, f32...) custom-call(s32[21]{0:T(128)S(1)} %concatenate.3.refs_0_, bf16[3,1536,1536]{2,1,0:T(8,128)(2,1)} %get-tuple-element.52.refs_1_.refs_17_, ...), custom_call_target="tpu_custom_call" | custom-call | flops 1 | bytes 1 | tf_op jit(solution)/shard_map/batch0/pallas_call | solution.py:68
  88.4 0.6 collective-permute-start.3
  89.0 0.0 collective-permute-done.1.refs_3_
  89.0 20.5 %batch1.1 = (bf16[1536,512]{1,0:T(8,128)(2,1)S(1)}, bf16[1536,512]{1,0:T(8,128)(2,1)}, bf16[1536,512]{1,0:T(8,128)(2,1)}, bf16[1536,512]{1,0:T(8,128)(2,1)}, f32...) custom-call(s32[21]{0:T(128)S(1)} %concatenate.3.refs_0_, bf16[3,1536,1536]{2,1,0:T(8,128)(2,1)} %get-tuple-element.52.refs_1_.refs_17_, ...), custom_call_target="tpu_custom_call" | custom-call | flops 1 | bytes 1 | tf_op jit(solution)/shard_map/batch1/pallas_call | solution.py:68
  109.5 1.6 collective-permute-start.4
  111.1 0.0 collective-permute-done.refs_3_
  111.1 20.2 %batch2.1 = (bf16[1536,512]{1,0:T(8,128)(2,1)S(1)}, bf16[1536,512]{1,0:T(8,128)(2,1)}, bf16[1536,512]{1,0:T(8,128)(2,1)}, bf16[1536,256]{1,0:T(8,128)(2,1)}, bf1...) custom-call(s32[21]{0:T(128)S(1)} %concatenate.3.refs_0_, ...), custom_call_target="tpu_custom_call" | custom-call | flops 1 | bytes 1 | tf_op jit(solution)/shard_map/batch2/pallas_call | solution.py:68
  131.3 0.6 collective-permute-start.6
  131.9 1.5 collective-permute-start.5
  133.4 0.0 copy-start.1
  133.4 0.0 copy-start.2
  133.4 54.5 %sum.1 = (f32[512,256]{1,0:T(8,128)S(1)}, bf16[512,256]{1,0:T(8,128)(2,1)S(1)}, f32[1,512]{1,0:T(1,128)S(1)}, bf16[3,1536,512]{2,1,0:T(8,128)(2,1)}) custom-call(s32[21]{0:T(128)S(1)} %concatenate.3.refs_0_, f32[2048,256]{1,0:T(8,128)} %get-tuple-element.63.refs_1_, bf16[2048,256]{1,0:T(8,128)(2,1)} %get-tuple-element.64.refs_2_, ...), custom_call_target="tpu_custom_call" | custom-call | flops 1 | bytes 1 | tf_op jit(solution)/shard_map/sum/pallas_call | solution.py:68
  187.9 0.0 collective-permute-done.3.refs_14_
  187.9 0.0 collective-permute-done.4.refs_15_
  187.9 0.0 copy-done.1
  187.9 0.0 copy-done.2
  187.9 13.8 %finish.1 = (f32[512,512]{1,0:T(8,128)}, f32[512,512]{1,0:T(8,128)}, f32[512,512]{1,0:T(8,128)}, f32[1,512]{1,0:T(1,128)}, f32[1,512]{1,0:T(1,128)}, /*index=5*/...) custom-call(s32[21]{0:T(128)S(1)} %concatenate.3.refs_0_, ...), custom_call_target="tpu_custom_call" | custom-call | flops 1 | bytes 1 | tf_op jit(solution)/shard_map/finish/pallas_call | solution.py:68
  201.7 0.0 collective-permute-done.6.refs_1_
  201.8 3.4 %scatter2_0.1.refs_4_ = bf16[3,1536,512]{2,1,0:T(8,128)(2,1)} custom-call(bf16[1536,512]{1,0:T(8,128)(2,1)S(1)} %get-tuple-element.83.refs_0_, bf16[1536,256]{1,0:T(8,128)(2,1)S(1)} %collective-permute-done.6.refs_1_, f32[3,1536,128]{2,1,0:T(8,128)S(1)} %get-tuple-element.53.refs_2_.refs_16_, ...), custom_call_target="tpu_custom_call", output_to_operand_aliasing={{}: (4, {})} | custom-call | flops 1 | bytes 1 | tf_op jit(solution)/shard_map/scatter2_0/pallas_call | solution.py:68
  205.1 2.9 %collective-permute-done.5.refs_1_ = bf16[1536,256]{1,0:T(8,128)(2,1)S(1)} collective-permute-done((bf16[1536,256]{1,0:T(8,128)(2,1)}, bf16[1536,256]{1,0:T(8,128)(2,1)S(1)}, u32[]{:S(2)}, u32[]{:S(2)}) %collective-permute-start.5) | collective-permute-done | bytes 786464 | tf_op jit(solution)/shard_map/ppermute | solution.py:93
  208.0 3.3 %scatter2_1.1 = bf16[3,1536,512]{2,1,0:T(8,128)(2,1)} custom-call(bf16[1536,512]{1,0:T(8,128)(2,1)S(1)} %get-tuple-element.83.refs_0_, bf16[1536,256]{1,0:T(8,128)(2,1)S(1)} %collective-permute-done.5.refs_1_, f32[3,1536,128]{2,1,0:T(8,128)S(1)} %get-tuple-element.53.refs_2_.refs_16_, ...), custom_call_target="tpu_custom_call", output_to_operand_aliasing={{}: (4, {})} | custom-call | flops 1 | bytes 1 | tf_op jit(solution)/shard_map/scatter2_1/pallas_call | solution.py:68
Async XLA Ops:
  2.1 7.9 %copy-start.4 = (s32[8]{0:T(128)S(1)}, s32[8]{0:T(128)}, u32[]{:S(2)}) copy-start(s32[8]{0:T(128)} %param.14) | copy-start | bytes 100
  2.1 8.0 %copy-start.3 = (s32[3,1]{0,1:T(1,128)S(1)}, s32[3,1]{0,1:T(1,128)}, u32[]{:S(2)}) copy-start(s32[3,1]{0,1:T(1,128)} %param.13) | copy-start | bytes 40
  2.1 66.9 %collective-permute-start.2 = (bf16[1536,512]{1,0:T(8,128)(2,1)S(1)}, bf16[1536,512]{1,0:T(8,128)(2,1)}, u32[]{:S(2)}, u32[]{:S(2)}) collective-permute-start(bf16[1536,512]{1,0:T(8,128)(2,1)S(1)} %first.1.refs_1_), channel_id=1, source_target_pairs={{0,2},{1,3},{2,0},{3,1},{4,6},{5,7},{6,4},{7,5},{8,10},{9,11},{10,... | collective-permute-start | bytes 4718600 | tf_op jit(solution)/shard_map/ppermute | solution.py:93
  7.9 81.1 %collective-permute-start.1 = (bf16[1536,512]{1,0:T(8,128)(2,1)}, bf16[1536,512]{1,0:T(8,128)(2,1)}, u32[]{:S(2)}, u32[]{:S(2)}) collective-permute-start(bf16[1536,512]{1,0:T(8,128)(2,1)} %get-tuple-element.58), channel_id=1, source_target_pairs={{0,2},{1,3},{2,0},{3,1},{4,6},{5,7},{6,4},{7,5},{8,10},{9,11},{10,... | collective-permute-start | bytes 4718600 | tf_op jit(solution)/shard_map/ppermute | solution.py:93
  8.0 103.1 %collective-permute-start = (bf16[1536,512]{1,0:T(8,128)(2,1)}, bf16[1536,512]{1,0:T(8,128)(2,1)S(1)}, u32[]{:S(2)}, u32[]{:S(2)}) collective-permute-start(bf16[1536,512]{1,0:T(8,128)(2,1)} %get-tuple-element.51.refs_4_), channel_id=1, source_target_pairs={{0,2},{1,3},{2,0},{3,1},{4,6},{5,7},{6,4},{7,5},{8,10},{9,11},{10,... | collective-permute-start | bytes 4718600 | tf_op jit(solution)/shard_map/ppermute | solution.py:93
  61.7 7.3 %copy-start = (f32[512]{0:T(512)S(1)}, f32[512]{0:T(512)}, u32[]{:S(2)}) copy-start(f32[512]{0:T(512)} %param.18) | copy-start | bytes 6148
  88.4 99.5 %collective-permute-start.3 = (bf16[1536,512]{1,0:T(8,128)(2,1)}, bf16[1536,512]{1,0:T(8,128)(2,1)S(1)}, u32[]{:S(2)}, u32[]{:S(2)}) collective-permute-start(bf16[1536,512]{1,0:T(8,128)(2,1)} %get-tuple-element.80), channel_id=1, source_target_pairs={{0,2},{1,3},{2,0},{3,1},{4,6},{5,7},{6,4},{7,5},{8,10},{9,11},{10,... | collective-permute-start | bytes 4718600 | tf_op jit(solution)/shard_map/ppermute | solution.py:93
  109.5 78.4 %collective-permute-start.4 = (bf16[1536,512]{1,0:T(8,128)(2,1)}, bf16[1536,512]{1,0:T(8,128)(2,1)S(1)}, u32[]{:S(2)}, u32[]{:S(2)}) collective-permute-start(bf16[1536,512]{1,0:T(8,128)(2,1)} %get-tuple-element.81), channel_id=1, source_target_pairs={{0,2},{1,3},{2,0},{3,1},{4,6},{5,7},{6,4},{7,5},{8,10},{9,11},{10,... | collective-permute-start | bytes 4718600 | tf_op jit(solution)/shard_map/ppermute | solution.py:93
  131.3 70.4 %collective-permute-start.6 = (bf16[1536,256]{1,0:T(8,128)(2,1)}, bf16[1536,256]{1,0:T(8,128)(2,1)S(1)}, u32[]{:S(2)}, u32[]{:S(2)}) collective-permute-start(bf16[1536,256]{1,0:T(8,128)(2,1)} %get-tuple-element.86), channel_id=1, source_target_pairs={{0,2},{1,3},{2,0},{3,1},{4,6},{5,7},{6,4},{7,5},{8,10},{9,11},{10,... | collective-permute-start | bytes 2359304 | tf_op jit(solution)/shard_map/ppermute | solution.py:93
  131.9 76.1 %collective-permute-start.5 = (bf16[1536,256]{1,0:T(8,128)(2,1)}, bf16[1536,256]{1,0:T(8,128)(2,1)S(1)}, u32[]{:S(2)}, u32[]{:S(2)}) collective-permute-start(bf16[1536,256]{1,0:T(8,128)(2,1)} %get-tuple-element.84), channel_id=1, source_target_pairs={{0,2},{1,3},{2,0},{3,1},{4,6},{5,7},{6,4},{7,5},{8,10},{9,11},{10,... | collective-permute-start | bytes 2359304 | tf_op jit(solution)/shard_map/ppermute | solution.py:93
  133.4 54.5 %copy-start.1 = (f32[512]{0:T(512)S(1)}, f32[512]{0:T(512)}, u32[]{:S(2)}) copy-start(f32[512]{0:T(512)} %param.19) | copy-start | bytes 6148
  133.4 54.5 %copy-start.2 = (f32[512]{0:T(512)S(1)}, f32[512]{0:T(512)}, u32[]{:S(2)}) copy-start(f32[512]{0:T(512)} %param.20) | copy-start | bytes 6148

commit v8 on v7

--- a/solution.py
+++ b/solution.py
@@ -437,9 +437,9 @@
     )
 
 
-def batch_kernel(m, chunks, table_ref, *refs):
+def batch_kernel(m, widths, table_ref, *refs):
     matrix_hbm, scale_hbm, far_hbm, here_hbm, weight_hbm, for_mate_hbm, grad_hbm, bias_ref = refs[:8]
-    refs = refs[8:]
+    refs, chunks = refs[8:], len(widths)
     total_hbm, bias_sum_in = refs[:2] if m else (None, None)
     refs = refs[2:] if m else refs
     ended = m == MB - 1
@@ -579,13 +579,12 @@
     save(mate_pre_ref, mate_pre_hbm)
     if ended:
         save(mate_weight_ref, mate_weight_hbm)
-    step = width // chunks
     for i in range(wide):
         rows = slice(i * WIDE, (i + 1) * WIDE)
         away = product_back(pre_ref[rows, :], weight_ref[2]) + product_back(mate_pre_ref[rows, :], mate_weight_ref[1])
         away_ref[rows, :] = away.astype(BF16)
         for chunk in range(chunks):
-            columns = slice(chunk * step, (chunk + 1) * step)
+            columns = slice(sum(widths[:chunk]), sum(widths[: chunk + 1]))
             save(away_ref.at[rows, columns], away_hbm[chunk].at[rows])
     here_copy.wait_send()
     weight_copy.wait_send()
@@ -597,9 +596,9 @@
         item.wait()
 
 
-def batch(table, m, matrix, scale, far, here, weight, for_mate, out_grad, bias, total, bias_sum, chunks, after=()):
+def batch(table, m, matrix, scale, far, here, weight, for_mate, out_grad, bias, total, bias_sum, widths, after=()):
     nodes, width = far.array.shape
-    wide, narrow = nodes // WIDE, nodes // TILE
+    wide, narrow, chunks = nodes // WIDE, nodes // TILE, len(widths)
     flat = lambda i: (0, 0)
     ended = m == MB - 1
     parts = [((D, width // 2), F32), ((D, width // 2), BF16)] if ended else []
@@ -607,13 +606,13 @@
     if not ended:
         results = [((4, width, width), F32, None, None, pltpu.VMEM)]
     return launch(
-        f"batch{m}", functools.partial(batch_kernel, m, chunks), table,
+        f"batch{m}", functools.partial(batch_kernel, m, widths), table,
         [(array, None, None) for array in (matrix, scale, far, here, weight, for_mate, out_grad)]
         + [(bias, (1, width), flat)]
         + ([(total, None, None), (bias_sum, (1, width), flat)] if m else []),
         [((nodes, width), BF16, None, None, pltpu.VMEM)]
         + [((nodes, width), BF16, None, None)] * 2
-        + [((nodes, width // chunks), BF16, None, None)] * chunks
+        + [((nodes, columns), BF16, None, None) for columns in widths]
         + ([(for_mate.array.shape, BF16, None, None)] if ended else [])
         + results
         + [((1, width), F32, (1, width), flat)],
@@ -683,10 +682,10 @@
     ]
 
 
-def scatter_kernel(m, chunk, own_hbm, got_hbm, scale_hbm, matrix_hbm, grads_hbm, *refs):
+def scatter_kernel(m, first, own_hbm, got_hbm, scale_hbm, matrix_hbm, grads_hbm, *refs):
     width = got_hbm.shape[1]
     loads, work, stores = scatter_job(
-        m, own_hbm.shape[0], pl.ds(chunk * width, width), own_hbm, got_hbm, scale_hbm, matrix_hbm, grads_hbm, refs[:6], refs[6]
+        m, own_hbm.shape[0], pl.ds(first, width), own_hbm, got_hbm, scale_hbm, matrix_hbm, grads_hbm, refs[:6], refs[6]
     )
     for item in loads:
         item.start()
@@ -695,10 +694,10 @@
         item.wait()
 
 
-def scatter(m, chunk, own, got, scale, matrix, grads, after=()):
+def scatter(m, first, own, got, scale, matrix, grads, after=()):
     nodes, width = own.array.shape
     return launch(
-        f"scatter{m}_{chunk}", functools.partial(scatter_kernel, m, chunk), None,
+        f"scatter{m}_{first}", functools.partial(scatter_kernel, m, first), None,
         [(array, None, None) for array in (own, got, scale, matrix)],
         [((MB, nodes, width), BF16, None, None)],
         after=after, alias=(grads, 0), scratch=scatter_scratch(nodes, got.array.shape[1]),
@@ -1060,9 +1059,10 @@
     total, bias_sum = None, None
     outputs, pres, mates, away = [], [], [], []
     for m in range(MB):
-        chunks = 2 if m == MB - 1 else 1
+        widths = (width - width // 4, width // 4) if m == MB - 1 else (width,)
+        chunks = len(widths)
         out_m, pre_m, mate_m, *rest = batch(
-            table, m, matrix, scale, far[m], here, weight, for_mate, out_grad, bias_row, total, bias_sum, chunks,
+            table, m, matrix, scale, far[m], here, weight, for_mate, out_grad, bias_row, total, bias_sum, widths,
             [last],
         )
         outputs.append(Kept(out_m))
@@ -1082,7 +1082,7 @@
         scale, matrix, [bias_total],
     )
     for chunk, got in enumerate(away[-1]):
-        input_grads = scatter(MB - 1, chunk, Kept(last_back), got, scale, Kept(last_matrix), input_grads)
+        input_grads = scatter(MB - 1, sum(widths[:chunk]), Kept(last_back), got, scale, Kept(last_matrix), input_grads)
     return (outputs, input_grads, *updated[:3], *(row.reshape(width) for row in updated[3:]))
 
 

time: 212 us -> 212 us (level)
  transfers between devices with their start and end apart: 7 -> 7, of which waited for: 1 -> 1; matrix products, arithmetic and copies ran while one was open for 0% -> 0% of each run, Pallas kernels for 91% -> 92%
where the time goes in v8:
time: 212 us; the launch traced here: 211 us
  Pallas kernels  199 us (94%)
  starting transfers between devices  9.37 us (4%)
    pallas_call x11, Pallas kernels, launch(): pl.pallas_call(kernel, grid_spec=pltpu.PrefetchScalarGridSpec(num_scalar_...  199 us
    ppermute x7, starting transfers between devices, flip(): return lax.ppermute(values, axis, [(i, i ^ bit) for i in range(size)])  9.37 us
  transfers between devices with their start and end apart: 7, of which 1 were waited for; matrix products, arithmetic and copies ran while one was open for 0% of the time, Pallas kernels for 92%

profile of v8, /device:TPU:0, one launch (start us, length us, event | category | flops | bytes accessed | tf_op | source)
XLA Modules:
  0.0 211.2 jit_solution(1605665037974263538)
XLA Ops:
  0.6 1.4 first.1.refs_1_
  2.1 0.0 copy-start.4
  2.1 0.0 copy-start.3
  2.1 3.0 %collective-permute-start.2 = (bf16[1536,512]{1,0:T(8,128)(2,1)S(1)}, bf16[1536,512]{1,0:T(8,128)(2,1)}, u32[]{:S(2)}, u32[]{:S(2)}) collective-permute-start(bf16[1536,512]{1,0:T(8,128)(2,1)S(1)} %first.1.refs_1_), channel_id=1, source_target_pairs={{0,2},{1,3},{2,0},{3,1},{4,6},{5,7},{6,4},{7,5},{8,10},{9,11},{10,... | collective-permute-start | bytes 4718600 | tf_op jit(solution)/shard_map/ppermute | solution.py:93
  5.1 2.8 %pick1.1 = (bf16[1536,512]{1,0:T(8,128)(2,1)}, bf16[1536,512]{1,0:T(8,128)(2,1)}) custom-call(bf16[3,1536,512]{2,1,0:T(8,128)(2,1)} %refs_3_.1, bf16[1536,512]{1,0:T(8,128)(2,1)S(1)} %first.1.refs_1_), custom_call_target="tpu_custom_call" | custom-call | flops 1 | bytes 1 | tf_op jit(solution)/shard_map/pick1/pallas_call | solution.py:68
  7.9 0.1 collective-permute-start.1
  8.0 2.0 collective-permute-start
  10.0 0.0 copy-done.4
  10.0 0.1 select_reduce_fusion
  10.1 0.0 copy-done.3
  10.1 0.1 concatenate.3.refs_0_
  10.2 51.5 %front.1 = (bf16[3,1536,1536]{2,1,0:T(8,128)(2,1)}, f32[3,1536,128]{2,1,0:T(8,128)S(1)}, bf16[3,1536,512]{2,1,0:T(8,128)(2,1)}, bf16[8,512,512]{2,1,0:T(8,128)(2,1)}) custom-call(s32[21]{0:T(128)S(1)} %concatenate.3.refs_0_, f32[512,512]{1,0:T(8,128)} %refs_7_.7, s32[3,16,1536]{2,1,0:T(8,128)} %bitcast.16, bf16[3,1536,512]{2,1,0:T(8,128)(2,1)} %refs_3_.1, ...), custom_call_target="tpu_custom_call" | custom-call | flops 1 | bytes 1 | tf_op jit(solution)/shard_map/front/pallas_call | solution.py:68
  61.7 0.0 copy-start
  61.7 7.2 %place.1 = (bf16[4,512,512]{2,1,0:T(8,128)(2,1)S(1)}, bf16[2,512,512]{2,1,0:T(8,128)(2,1)S(1)}) custom-call(s32[21]{0:T(128)S(1)} %concatenate.3.refs_0_, bf16[8,512,512]{2,1,0:T(8,128)(2,1)} %get-tuple-element.55.refs_1_), custom_call_target="tpu_custom_call" | custom-call | flops 1 | bytes 1 | tf_op jit(solution)/shard_map/place/pallas_call | solution.py:68
  69.0 0.0 collective-permute-done.2.refs_3_
  69.0 0.0 copy-done
  69.0 19.4 %batch0.1 = (bf16[1536,512]{1,0:T(8,128)(2,1)S(1)}, bf16[1536,512]{1,0:T(8,128)(2,1)}, bf16[1536,512]{1,0:T(8,128)(2,1)}, bf16[1536,512]{1,0:T(8,128)(2,1)}, f32...) custom-call(s32[21]{0:T(128)S(1)} %concatenate.3.refs_0_, bf16[3,1536,1536]{2,1,0:T(8,128)(2,1)} %get-tuple-element.52.refs_1_.refs_17_, ...), custom_call_target="tpu_custom_call" | custom-call | flops 1 | bytes 1 | tf_op jit(solution)/shard_map/batch0/pallas_call | solution.py:68
  88.4 0.6 collective-permute-start.3
  89.0 0.0 collective-permute-done.1.refs_3_
  89.0 20.5 %batch1.1 = (bf16[1536,512]{1,0:T(8,128)(2,1)S(1)}, bf16[1536,512]{1,0:T(8,128)(2,1)}, bf16[1536,512]{1,0:T(8,128)(2,1)}, bf16[1536,512]{1,0:T(8,128)(2,1)}, f32...) custom-call(s32[21]{0:T(128)S(1)} %concatenate.3.refs_0_, bf16[3,1536,1536]{2,1,0:T(8,128)(2,1)} %get-tuple-element.52.refs_1_.refs_17_, ...), custom_call_target="tpu_custom_call" | custom-call | flops 1 | bytes 1 | tf_op jit(solution)/shard_map/batch1/pallas_call | solution.py:68
  109.5 1.6 collective-permute-start.4
  111.1 0.0 collective-permute-done.refs_3_
  111.1 20.2 %batch2.1 = (bf16[1536,512]{1,0:T(8,128)(2,1)S(1)}, bf16[1536,512]{1,0:T(8,128)(2,1)}, bf16[1536,512]{1,0:T(8,128)(2,1)}, bf16[1536,384]{1,0:T(8,128)(2,1)}, bf1...) custom-call(s32[21]{0:T(128)S(1)} %concatenate.3.refs_0_, ...), custom_call_target="tpu_custom_call" | custom-call | flops 1 | bytes 1 | tf_op jit(solution)/shard_map/batch2/pallas_call | solution.py:68
  131.3 0.6 collective-permute-start.6
  131.9 1.5 collective-permute-start.5
  133.4 0.0 copy-start.1
  133.4 0.0 copy-start.2
  133.4 54.5 %sum.1 = (f32[512,256]{1,0:T(8,128)S(1)}, bf16[512,256]{1,0:T(8,128)(2,1)S(1)}, f32[1,512]{1,0:T(1,128)S(1)}, bf16[3,1536,512]{2,1,0:T(8,128)(2,1)}) custom-call(s32[21]{0:T(128)S(1)} %concatenate.3.refs_0_, f32[2048,256]{1,0:T(8,128)} %get-tuple-element.63.refs_1_, bf16[2048,256]{1,0:T(8,128)(2,1)} %get-tuple-element.64.refs_2_, ...), custom_call_target="tpu_custom_call" | custom-call | flops 1 | bytes 1 | tf_op jit(solution)/shard_map/sum/pallas_call | solution.py:68
  187.9 0.0 collective-permute-done.3.refs_14_
  187.9 0.0 collective-permute-done.4.refs_15_
  187.9 0.0 copy-done.1
  187.9 0.0 copy-done.2
  187.9 13.9 %finish.1 = (f32[512,512]{1,0:T(8,128)}, f32[512,512]{1,0:T(8,128)}, f32[512,512]{1,0:T(8,128)}, f32[1,512]{1,0:T(1,128)}, f32[1,512]{1,0:T(1,128)}, /*index=5*/...) custom-call(s32[21]{0:T(128)S(1)} %concatenate.3.refs_0_, ...), custom_call_target="tpu_custom_call" | custom-call | flops 1 | bytes 1 | tf_op jit(solution)/shard_map/finish/pallas_call | solution.py:68
  201.8 0.0 collective-permute-done.6.refs_1_
  201.8 4.9 %scatter2_0.1.refs_4_ = bf16[3,1536,512]{2,1,0:T(8,128)(2,1)} custom-call(bf16[1536,512]{1,0:T(8,128)(2,1)S(1)} %get-tuple-element.83.refs_0_, bf16[1536,384]{1,0:T(8,128)(2,1)S(1)} %collective-permute-done.6.refs_1_, f32[3,1536,128]{2,1,0:T(8,128)S(1)} %get-tuple-element.53.refs_2_.refs_16_, ...), custom_call_target="tpu_custom_call", output_to_operand_aliasing={{}: (4, {})} | custom-call | flops 1 | bytes 1 | tf_op jit(solution)/shard_map/scatter2_0/pallas_call | solution.py:68
  206.7 1.3 collective-permute-done.5.refs_1_
  208.0 3.0 %scatter2_384.1 = bf16[3,1536,512]{2,1,0:T(8,128)(2,1)} custom-call(bf16[1536,512]{1,0:T(8,128)(2,1)S(1)} %get-tuple-element.83.refs_0_, bf16[1536,128]{1,0:T(8,128)(2,1)S(1)} %collective-permute-done.5.refs_1_, f32[3,1536,128]{2,1,0:T(8,128)S(1)} %get-tuple-element.53.refs_2_.refs_16_, ...), custom_call_target="tpu_custom_call", output_to_operand_aliasing={{}: (4, {})} | custom-call | flops 1 | bytes 1 | tf_op jit(solution)/shard_map/scatter2_384/pallas_call | solution.py:68
Async XLA Ops:
  2.1 7.9 %copy-start.4 = (s32[8]{0:T(128)S(1)}, s32[8]{0:T(128)}, u32[]{:S(2)}) copy-start(s32[8]{0:T(128)} %param.14) | copy-start | bytes 100
  2.1 8.0 %copy-start.3 = (s32[3,1]{0,1:T(1,128)S(1)}, s32[3,1]{0,1:T(1,128)}, u32[]{:S(2)}) copy-start(s32[3,1]{0,1:T(1,128)} %param.13) | copy-start | bytes 40
  2.1 66.9 %collective-permute-start.2 = (bf16[1536,512]{1,0:T(8,128)(2,1)S(1)}, bf16[1536,512]{1,0:T(8,128)(2,1)}, u32[]{:S(2)}, u32[]{:S(2)}) collective-permute-start(bf16[1536,512]{1,0:T(8,128)(2,1)S(1)} %first.1.refs_1_), channel_id=1, source_target_pairs={{0,2},{1,3},{2,0},{3,1},{4,6},{5,7},{6,4},{7,5},{8,10},{9,11},{10,... | collective-permute-start | bytes 4718600 | tf_op jit(solution)/shard_map/ppermute | solution.py:93
  7.9 81.1 %collective-permute-start.1 = (bf16[1536,512]{1,0:T(8,128)(2,1)}, bf16[1536,512]{1,0:T(8,128)(2,1)}, u32[]{:S(2)}, u32[]{:S(2)}) collective-permute-start(bf16[1536,512]{1,0:T(8,128)(2,1)} %get-tuple-element.58), channel_id=1, source_target_pairs={{0,2},{1,3},{2,0},{3,1},{4,6},{5,7},{6,4},{7,5},{8,10},{9,11},{10,... | collective-permute-start | bytes 4718600 | tf_op jit(solution)/shard_map/ppermute | solution.py:93
  8.0 103.1 %collective-permute-start = (bf16[1536,512]{1,0:T(8,128)(2,1)}, bf16[1536,512]{1,0:T(8,128)(2,1)S(1)}, u32[]{:S(2)}, u32[]{:S(2)}) collective-permute-start(bf16[1536,512]{1,0:T(8,128)(2,1)} %get-tuple-element.51.refs_4_), channel_id=1, source_target_pairs={{0,2},{1,3},{2,0},{3,1},{4,6},{5,7},{6,4},{7,5},{8,10},{9,11},{10,... | collective-permute-start | bytes 4718600 | tf_op jit(solution)/shard_map/ppermute | solution.py:93
  61.7 7.3 %copy-start = (f32[512]{0:T(512)S(1)}, f32[512]{0:T(512)}, u32[]{:S(2)}) copy-start(f32[512]{0:T(512)} %param.18) | copy-start | bytes 6148
  88.4 99.5 %collective-permute-start.3 = (bf16[1536,512]{1,0:T(8,128)(2,1)}, bf16[1536,512]{1,0:T(8,128)(2,1)S(1)}, u32[]{:S(2)}, u32[]{:S(2)}) collective-permute-start(bf16[1536,512]{1,0:T(8,128)(2,1)} %get-tuple-element.80), channel_id=1, source_target_pairs={{0,2},{1,3},{2,0},{3,1},{4,6},{5,7},{6,4},{7,5},{8,10},{9,11},{10,... | collective-permute-start | bytes 4718600 | tf_op jit(solution)/shard_map/ppermute | solution.py:93
  109.5 78.4 %collective-permute-start.4 = (bf16[1536,512]{1,0:T(8,128)(2,1)}, bf16[1536,512]{1,0:T(8,128)(2,1)S(1)}, u32[]{:S(2)}, u32[]{:S(2)}) collective-permute-start(bf16[1536,512]{1,0:T(8,128)(2,1)} %get-tuple-element.81), channel_id=1, source_target_pairs={{0,2},{1,3},{2,0},{3,1},{4,6},{5,7},{6,4},{7,5},{8,10},{9,11},{10,... | collective-permute-start | bytes 4718600 | tf_op jit(solution)/shard_map/ppermute | solution.py:93
  131.3 70.5 %collective-permute-start.6 = (bf16[1536,384]{1,0:T(8,128)(2,1)}, bf16[1536,384]{1,0:T(8,128)(2,1)S(1)}, u32[]{:S(2)}, u32[]{:S(2)}) collective-permute-start(bf16[1536,384]{1,0:T(8,128)(2,1)} %get-tuple-element.86), channel_id=1, source_target_pairs={{0,2},{1,3},{2,0},{3,1},{4,6},{5,7},{6,4},{7,5},{8,10},{9,11},{10,... | collective-permute-start | bytes 3538952 | tf_op jit(solution)/shard_map/ppermute | solution.py:93
  131.9 76.1 %collective-permute-start.5 = (bf16[1536,128]{1,0:T(8,128)(2,1)}, bf16[1536,128]{1,0:T(8,128)(2,1)S(1)}, u32[]{:S(2)}, u32[]{:S(2)}) collective-permute-start(bf16[1536,128]{1,0:T(8,128)(2,1)} %get-tuple-element.84), channel_id=1, source_target_pairs={{0,2},{1,3},{2,0},{3,1},{4,6},{5,7},{6,4},{7,5},{8,10},{9,11},{10,... | collective-permute-start | bytes 1179656 | tf_op jit(solution)/shard_map/ppermute | solution.py:93
  133.4 54.5 %copy-start.1 = (f32[512]{0:T(512)S(1)}, f32[512]{0:T(512)}, u32[]{:S(2)}) copy-start(f32[512]{0:T(512)} %param.19) | copy-start | bytes 6148
  133.4 54.5 %copy-start.2 = (f32[512]{0:T(512)S(1)}, f32[512]{0:T(512)}, u32[]{:S(2)}) copy-start(f32[512]{0:T(512)} %param.20) | copy-start | bytes 6148

commit v9 on v8

--- a/solution.py
+++ b/solution.py
@@ -156,20 +156,6 @@
             loads.append(pltpu.make_async_copy(piece(source, i), piece(buffer, i), load.at[place]))
             stores.append(pltpu.make_async_copy(piece(buffer, i), piece(target, i), store.at[place]))
     return loads, stores
-
-
-def first_kernel(source_hbm, target_ref, semaphore):
-    copy = pltpu.make_async_copy(source_hbm.at[0], target_ref, semaphore)
-    copy.start()
-    copy.wait()
-
-
-def pick_first(stacked):
-    return launch(
-        "first", first_kernel, None,
-        [(stacked, None, None)], [(stacked.shape[1:], stacked.dtype, None, None, pltpu.VMEM)],
-        scratch=[pltpu.SemaphoreType.DMA],
-    )
 
 
 def pick_kernel(batches, source_ref, *refs):
@@ -1046,8 +1032,8 @@
         array.reshape(1, width) for array in (master_bias, bias_first, bias_second)
     )
 
-    picked = pick_first(features)
-    picked = picked + pick(features, tuple(range(1, MB)), [Kept(picked[0])])
+    lead = features[0]
+    picked = [lead, *pick(features, tuple(range(1, MB)), [Kept(lead, None)])]
     far = [Kept(flip(array, "col", 2), None) for array in picked]
 
     matrix, scale, here, slots = front(

time: 212 us -> 212 us (level)
    pallas_call x11 -> x10, Pallas kernels: 199 us -> 198 us  [launch(): pl.pallas_call(kernel, grid_spec=pltpu.PrefetchScalarGridSpec(num_scalar_...]
where the time goes in v9:
time: 212 us; the launch traced here: 211 us
  Pallas kernels  198 us (93%)
  starting transfers between devices  9.37 us (4%)
    pallas_call x10, Pallas kernels, launch(): pl.pallas_call(kernel, grid_spec=pltpu.PrefetchScalarGridSpec(num_scalar_...  198 us
    ppermute x7, starting transfers between devices, flip(): return lax.ppermute(values, axis, [(i, i ^ bit) for i in range(size)])  9.37 us
  transfers between devices with their start and end apart: 7, of which 1 were waited for; matrix products, arithmetic and copies ran while one was open for 0% of the time, Pallas kernels for 92%

profile of v9, /device:TPU:0, one launch (start us, length us, event | category | flops | bytes accessed | tf_op | source)
XLA Modules:
  0.0 211.3 jit_solution(4183169979317815310)
XLA Ops:
  0.6 1.5 slice_bitcast_fusion.refs_1_
  2.1 0.0 copy-start.4
  2.2 0.0 copy-start.3
  2.2 3.0 %collective-permute-start.2 = (bf16[1536,512]{1,0:T(8,128)(2,1)S(1)}, bf16[1536,512]{1,0:T(8,128)(2,1)}, u32[]{:S(2)}, u32[]{:S(2)}) collective-permute-start(bf16[1536,512]{1,0:T(8,128)(2,1)S(1)} %slice_bitcast_fusion.refs_1_), channel_id=1, source_target_pairs={{0,2},{1,3},{2,0},{3,1},{4,6},{5,7},{6,4},{7,5},{8,10},{9,11},{10,... | collective-permute-start | bytes 4718600 | tf_op jit(solution)/shard_map/ppermute | solution.py:93
  5.2 2.8 %pick1.1 = (bf16[1536,512]{1,0:T(8,128)(2,1)}, bf16[1536,512]{1,0:T(8,128)(2,1)}) custom-call(bf16[3,1536,512]{2,1,0:T(8,128)(2,1)} %refs_3_.1, bf16[1536,512]{1,0:T(8,128)(2,1)S(1)} %slice_bitcast_fusion.refs_1_), custom_call_target="tpu_custom_call" | custom-call | flops 1 | bytes 1 | tf_op jit(solution)/shard_map/pick1/pallas_call | solution.py:68
  8.0 0.1 collective-permute-start.1
  8.1 2.0 collective-permute-start
  10.1 0.0 copy-done.4
  10.1 0.1 select_reduce_fusion
  10.2 0.0 copy-done.3
  10.2 0.1 concatenate.3.refs_0_
  10.3 51.5 %front.1 = (bf16[3,1536,1536]{2,1,0:T(8,128)(2,1)}, f32[3,1536,128]{2,1,0:T(8,128)S(1)}, bf16[3,1536,512]{2,1,0:T(8,128)(2,1)}, bf16[8,512,512]{2,1,0:T(8,128)(2,1)}) custom-call(s32[21]{0:T(128)S(1)} %concatenate.3.refs_0_, f32[512,512]{1,0:T(8,128)} %refs_7_.7, s32[3,16,1536]{2,1,0:T(8,128)} %bitcast.18, bf16[3,1536,512]{2,1,0:T(8,128)(2,1)} %refs_3_.1, ...), custom_call_target="tpu_custom_call" | custom-call | flops 1 | bytes 1 | tf_op jit(solution)/shard_map/front/pallas_call | solution.py:68
  61.8 0.0 copy-start
  61.8 7.2 %place.1 = (bf16[4,512,512]{2,1,0:T(8,128)(2,1)S(1)}, bf16[2,512,512]{2,1,0:T(8,128)(2,1)S(1)}) custom-call(s32[21]{0:T(128)S(1)} %concatenate.3.refs_0_, bf16[8,512,512]{2,1,0:T(8,128)(2,1)} %get-tuple-element.55.refs_1_), custom_call_target="tpu_custom_call" | custom-call | flops 1 | bytes 1 | tf_op jit(solution)/shard_map/place/pallas_call | solution.py:68
  69.1 0.0 collective-permute-done.2.refs_3_
  69.1 0.0 copy-done
  69.1 19.4 %batch0.1 = (bf16[1536,512]{1,0:T(8,128)(2,1)S(1)}, bf16[1536,512]{1,0:T(8,128)(2,1)}, bf16[1536,512]{1,0:T(8,128)(2,1)}, bf16[1536,512]{1,0:T(8,128)(2,1)}, f32...) custom-call(s32[21]{0:T(128)S(1)} %concatenate.3.refs_0_, bf16[3,1536,1536]{2,1,0:T(8,128)(2,1)} %get-tuple-element.52.refs_1_.refs_17_, ...), custom_call_target="tpu_custom_call" | custom-call | flops 1 | bytes 1 | tf_op jit(solution)/shard_map/batch0/pallas_call | solution.py:68
  88.5 0.6 collective-permute-start.3
  89.1 0.0 collective-permute-done.1.refs_3_
  89.1 20.5 %batch1.1 = (bf16[1536,512]{1,0:T(8,128)(2,1)S(1)}, bf16[1536,512]{1,0:T(8,128)(2,1)}, bf16[1536,512]{1,0:T(8,128)(2,1)}, bf16[1536,512]{1,0:T(8,128)(2,1)}, f32...) custom-call(s32[21]{0:T(128)S(1)} %concatenate.3.refs_0_, bf16[3,1536,1536]{2,1,0:T(8,128)(2,1)} %get-tuple-element.52.refs_1_.refs_17_, ...), custom_call_target="tpu_custom_call" | custom-call | flops 1 | bytes 1 | tf_op jit(solution)/shard_map/batch1/pallas_call | solution.py:68
  109.6 1.6 collective-permute-start.4
  111.2 0.0 collective-permute-done.refs_3_
  111.2 20.2 %batch2.1 = (bf16[1536,512]{1,0:T(8,128)(2,1)S(1)}, bf16[1536,512]{1,0:T(8,128)(2,1)}, bf16[1536,512]{1,0:T(8,128)(2,1)}, bf16[1536,384]{1,0:T(8,128)(2,1)}, bf1...) custom-call(s32[21]{0:T(128)S(1)} %concatenate.3.refs_0_, ...), custom_call_target="tpu_custom_call" | custom-call | flops 1 | bytes 1 | tf_op jit(solution)/shard_map/batch2/pallas_call | solution.py:68
  131.4 0.6 collective-permute-start.6
  132.0 1.5 collective-permute-start.5
  133.5 0.0 copy-start.1
  133.5 0.0 copy-start.2
  133.5 54.5 %sum.1 = (f32[512,256]{1,0:T(8,128)S(1)}, bf16[512,256]{1,0:T(8,128)(2,1)S(1)}, f32[1,512]{1,0:T(1,128)S(1)}, bf16[3,1536,512]{2,1,0:T(8,128)(2,1)}) custom-call(s32[21]{0:T(128)S(1)} %concatenate.3.refs_0_, f32[2048,256]{1,0:T(8,128)} %get-tuple-element.63.refs_1_, bf16[2048,256]{1,0:T(8,128)(2,1)} %get-tuple-element.64.refs_2_, ...), custom_call_target="tpu_custom_call" | custom-call | flops 1 | bytes 1 | tf_op jit(solution)/shard_map/sum/pallas_call | solution.py:68
  188.0 0.0 collective-permute-done.3.refs_14_
  188.0 0.0 collective-permute-done.4.refs_15_
  188.0 0.0 copy-done.1
  188.0 0.0 copy-done.2
  188.0 13.9 %finish.1 = (f32[512,512]{1,0:T(8,128)}, f32[512,512]{1,0:T(8,128)}, f32[512,512]{1,0:T(8,128)}, f32[1,512]{1,0:T(1,128)}, f32[1,512]{1,0:T(1,128)}, /*index=5*/...) custom-call(s32[21]{0:T(128)S(1)} %concatenate.3.refs_0_, ...), custom_call_target="tpu_custom_call" | custom-call | flops 1 | bytes 1 | tf_op jit(solution)/shard_map/finish/pallas_call | solution.py:68
  201.9 0.0 collective-permute-done.6.refs_1_
  201.9 4.9 %scatter2_0.1.refs_4_ = bf16[3,1536,512]{2,1,0:T(8,128)(2,1)} custom-call(bf16[1536,512]{1,0:T(8,128)(2,1)S(1)} %get-tuple-element.83.refs_0_, bf16[1536,384]{1,0:T(8,128)(2,1)S(1)} %collective-permute-done.6.refs_1_, f32[3,1536,128]{2,1,0:T(8,128)S(1)} %get-tuple-element.53.refs_2_.refs_16_, ...), custom_call_target="tpu_custom_call", output_to_operand_aliasing={{}: (4, {})} | custom-call | flops 1 | bytes 1 | tf_op jit(solution)/shard_map/scatter2_0/pallas_call | solution.py:68
  206.8 1.3 collective-permute-done.5.refs_1_
  208.1 3.0 %scatter2_384.1 = bf16[3,1536,512]{2,1,0:T(8,128)(2,1)} custom-call(bf16[1536,512]{1,0:T(8,128)(2,1)S(1)} %get-tuple-element.83.refs_0_, bf16[1536,128]{1,0:T(8,128)(2,1)S(1)} %collective-permute-done.5.refs_1_, f32[3,1536,128]{2,1,0:T(8,128)S(1)} %get-tuple-element.53.refs_2_.refs_16_, ...), custom_call_target="tpu_custom_call", output_to_operand_aliasing={{}: (4, {})} | custom-call | flops 1 | bytes 1 | tf_op jit(solution)/shard_map/scatter2_384/pallas_call | solution.py:68
Async XLA Ops:
  2.1 7.9 %copy-start.4 = (s32[8]{0:T(128)S(1)}, s32[8]{0:T(128)}, u32[]{:S(2)}) copy-start(s32[8]{0:T(128)} %param.14) | copy-start | bytes 100
  2.2 8.0 %copy-start.3 = (s32[3,1]{0,1:T(1,128)S(1)}, s32[3,1]{0,1:T(1,128)}, u32[]{:S(2)}) copy-start(s32[3,1]{0,1:T(1,128)} %param.13) | copy-start | bytes 40
  2.2 66.9 %collective-permute-start.2 = (bf16[1536,512]{1,0:T(8,128)(2,1)S(1)}, bf16[1536,512]{1,0:T(8,128)(2,1)}, u32[]{:S(2)}, u32[]{:S(2)}) collective-permute-start(bf16[1536,512]{1,0:T(8,128)(2,1)S(1)} %slice_bitcast_fusion.refs_1_), channel_id=1, source_target_pairs={{0,2},{1,3},{2,0},{3,1},{4,6},{5,7},{6,4},{7,5},{8,10},{9,11},{10,... | collective-permute-start | bytes 4718600 | tf_op jit(solution)/shard_map/ppermute | solution.py:93
  8.0 81.1 %collective-permute-start.1 = (bf16[1536,512]{1,0:T(8,128)(2,1)}, bf16[1536,512]{1,0:T(8,128)(2,1)}, u32[]{:S(2)}, u32[]{:S(2)}) collective-permute-start(bf16[1536,512]{1,0:T(8,128)(2,1)} %get-tuple-element.58), channel_id=1, source_target_pairs={{0,2},{1,3},{2,0},{3,1},{4,6},{5,7},{6,4},{7,5},{8,10},{9,11},{10,... | collective-permute-start | bytes 4718600 | tf_op jit(solution)/shard_map/ppermute | solution.py:93
  8.1 103.1 %collective-permute-start = (bf16[1536,512]{1,0:T(8,128)(2,1)}, bf16[1536,512]{1,0:T(8,128)(2,1)S(1)}, u32[]{:S(2)}, u32[]{:S(2)}) collective-permute-start(bf16[1536,512]{1,0:T(8,128)(2,1)} %get-tuple-element.51.refs_4_), channel_id=1, source_target_pairs={{0,2},{1,3},{2,0},{3,1},{4,6},{5,7},{6,4},{7,5},{8,10},{9,11},{10,... | collective-permute-start | bytes 4718600 | tf_op jit(solution)/shard_map/ppermute | solution.py:93
  61.8 7.3 %copy-start = (f32[512]{0:T(512)S(1)}, f32[512]{0:T(512)}, u32[]{:S(2)}) copy-start(f32[512]{0:T(512)} %param.18) | copy-start | bytes 6148
  88.5 99.5 %collective-permute-start.3 = (bf16[1536,512]{1,0:T(8,128)(2,1)}, bf16[1536,512]{1,0:T(8,128)(2,1)S(1)}, u32[]{:S(2)}, u32[]{:S(2)}) collective-permute-start(bf16[1536,512]{1,0:T(8,128)(2,1)} %get-tuple-element.80), channel_id=1, source_target_pairs={{0,2},{1,3},{2,0},{3,1},{4,6},{5,7},{6,4},{7,5},{8,10},{9,11},{10,... | collective-permute-start | bytes 4718600 | tf_op jit(solution)/shard_map/ppermute | solution.py:93
  109.6 78.4 %collective-permute-start.4 = (bf16[1536,512]{1,0:T(8,128)(2,1)}, bf16[1536,512]{1,0:T(8,128)(2,1)S(1)}, u32[]{:S(2)}, u32[]{:S(2)}) collective-permute-start(bf16[1536,512]{1,0:T(8,128)(2,1)} %get-tuple-element.81), channel_id=1, source_target_pairs={{0,2},{1,3},{2,0},{3,1},{4,6},{5,7},{6,4},{7,5},{8,10},{9,11},{10,... | collective-permute-start | bytes 4718600 | tf_op jit(solution)/shard_map/ppermute | solution.py:93
  131.4 70.5 %collective-permute-start.6 = (bf16[1536,384]{1,0:T(8,128)(2,1)}, bf16[1536,384]{1,0:T(8,128)(2,1)S(1)}, u32[]{:S(2)}, u32[]{:S(2)}) collective-permute-start(bf16[1536,384]{1,0:T(8,128)(2,1)} %get-tuple-element.86), channel_id=1, source_target_pairs={{0,2},{1,3},{2,0},{3,1},{4,6},{5,7},{6,4},{7,5},{8,10},{9,11},{10,... | collective-permute-start | bytes 3538952 | tf_op jit(solution)/shard_map/ppermute | solution.py:93
  132.0 76.1 %collective-permute-start.5 = (bf16[1536,128]{1,0:T(8,128)(2,1)}, bf16[1536,128]{1,0:T(8,128)(2,1)S(1)}, u32[]{:S(2)}, u32[]{:S(2)}) collective-permute-start(bf16[1536,128]{1,0:T(8,128)(2,1)} %get-tuple-element.84), channel_id=1, source_target_pairs={{0,2},{1,3},{2,0},{3,1},{4,6},{5,7},{6,4},{7,5},{8,10},{9,11},{10,... | collective-permute-start | bytes 1179656 | tf_op jit(solution)/shard_map/ppermute | solution.py:93
  133.5 54.5 %copy-start.1 = (f32[512]{0:T(512)S(1)}, f32[512]{0:T(512)}, u32[]{:S(2)}) copy-start(f32[512]{0:T(512)} %param.19) | copy-start | bytes 6148
  133.5 54.5 %copy-start.2 = (f32[512]{0:T(512)S(1)}, f32[512]{0:T(512)}, u32[]{:S(2)}) copy-start(f32[512]{0:T(512)} %param.20) | copy-start | bytes 6148
